TPU v7x, 256 devices: a whole 4x4x8 slice. The times are simulated.
256 devices in a mesh: seq: 64 (over x, y, z_hi), ch: 4 (over z_lo, core).
Axes of the slice: x: 4, y: 4, z: 8 (z_hi: 4, z_lo: 2; z = z_hi * 2 + z_lo), core: 2. Of those that a mesh axis runs over, the one named last changes fastest.
Arguments:
- value_rows: float32 [8192, 4096], P('seq', 'ch'), may hold values from -6 to 6
- key_rows: float32 [8192, 4096], P('seq', 'ch'), may hold values from -6 to 6
- query_rows: float32 [8192, 4096], P('seq', 'ch'), may hold values from -6 to 6
- pole_weights: float32 [16, 4096], P(None, 'ch'), may hold values from -0.225 to 0.225, as said below
- damping_speeds: float32 [16, 4096], P(None, 'ch'), may hold values from 6.1035156e-05 to 0.1, as said below
- out_weight: bfloat16 [4096, 4096], P('ch'), may hold values from -0.125 to 0.125
Outputs:
- mixed: bfloat16 [8192, 4096], P('seq', 'ch')
Inputs may be any that keep to these rules, and one draw needn't show every extreme that they name: `pole_weights`: amplitudes of the modes. `damping_speeds`: decay rates per position.
All inputs are finite; a program needn't handle non-finite values.
Results may differ from a plain program's by a relative error of at most 0.005.
Values sent between devices are 32-bit elements; how exact they have to be, the bound alone decides.
No kernel may reach another device: no remote copies, remote signals or barrier semaphores. Data moves between devices by JAX's collectives and lax.ppermute only.
A program may use at most 64 MiB of HBM per device.

v0:
```python
import jax
import jax.numpy as jnp
from jax import lax
from jax.experimental import pallas as pl
from jax.experimental.pallas import tpu as pltpu
from jax.sharding import PartitionSpec as P

MODES = 16
HALVES = MODES // 8
LANES = 128
SCOPE = 12 * 1024 * 1024
STEPS = (1, 3, 2)


def tiles(array):
    rows, columns = array.shape
    cut = array.reshape(rows // 8, 8, columns // LANES, LANES)
    return cut.transpose(0, 2, 1, 3).reshape(rows // 8, 8 * (columns // LANES), LANES)


def spread(values, index):
    return jnp.broadcast_to(values[index : index + 1, :], (8, LANES))


def f32(*shape):
    return jax.ShapeDtypeStruct(shape, jnp.float32)


def kernel_call(body, out_shape, inputs, flops, size, scratch=()):
    outs = jax.tree.map(lambda _: pl.BlockSpec(memory_space=pltpu.VMEM), out_shape)
    return pl.pallas_call(
        body,
        out_shape=out_shape,
        in_specs=[pl.BlockSpec(memory_space=pltpu.VMEM)] * len(inputs),
        out_specs=outs,
        scratch_shapes=scratch,
        cost_estimate=pl.CostEstimate(flops=flops, bytes_accessed=size, transcendentals=0),
        compiler_params=pltpu.CompilerParams(vmem_limit_bytes=SCOPE),
    )(*inputs)


def end_state_kernel(signal_ref, damping_ref, state_ref):
    outer, lanes = signal_ref.shape[0], signal_ref.shape[1] // 8
    place = lax.broadcasted_iota(jnp.int32, (8, LANES), 0)
    for g in range(lanes):
        block = pl.ds(8 * g, 8)
        signal = [signal_ref[i, block, :] for i in range(outer)]
        for half in range(HALVES):
            decay = jnp.exp(-damping_ref[half, block, :])
            result = None
            for m in range(8):
                once = spread(decay, m)
                twice = once * once
                four = twice * twice
                eight = four * four
                total = signal[0]
                for i in range(1, outer):
                    total = eight * total + signal[i]
                total = total + once * pltpu.roll(total, 1, 0)
                total = total + twice * pltpu.roll(total, 2, 0)
                total = total + four * pltpu.roll(total, 4, 0)
                if m != 7:
                    total = pltpu.roll(total, m + 1, 0)
                result = total if result is None else jnp.where(place == m, total, result)
            state_ref[half, block, :] = result


def local_kernel(signal_ref, damping_ref, gain_ref, out_ref):
    def row(ref, outer, inner):
        return ref[outer, pl.ds(inner, 8, stride=8), :]

    decay = [jnp.exp(-row(damping_ref, m // 8, m % 8)) for m in range(MODES)]
    gain = [row(gain_ref, m // 8, m % 8) for m in range(MODES)]

    def body(outer, state):
        for inner in range(8):
            signal = row(signal_ref, outer, inner)
            state = tuple(decay[m] * state[m] + signal for m in range(MODES))
            terms = [gain[m] * state[m] for m in range(MODES)]
            while len(terms) > 1:
                terms = [terms[n] + terms[n + 1] for n in range(0, len(terms), 2)]
            out_ref[outer, pl.ds(inner, 8, stride=8), :] = terms[0]
        return state

    zero = jnp.zeros((8, LANES), jnp.float32)
    lax.fori_loop(0, signal_ref.shape[0], body, (zero,) * MODES)


def places():
    at = lax.axis_index("seq")
    return [lax.rem(at, 4), lax.rem(lax.div(at, 4), 4), lax.div(at, 16)]


def run_kernel(axis, rows, damping_ref, out_ref):
    here = places()[axis]
    damping = damping_ref[...] * (-1.0 * rows * 4**axis)
    for n, step in enumerate((0, *STEPS)):
        there = here ^ step
        out_ref[n] = jnp.exp(damping * (3 - there).astype(jnp.float32))
        if step:
            ahead = jnp.maximum(here - there - 1, 0).astype(jnp.float32)
            before = (there < here).astype(jnp.float32)
            out_ref[3 + n] = jnp.exp(damping * ahead) * before


def last_kernel(rows, damping_ref, gain_ref, out_ref, near_ref, eight_ref, powers_ref):
    z, y, x = places()
    damping, gain = damping_ref[...], gain_ref[...]
    to_y = (z * rows).astype(jnp.float32)
    to_x = ((4 * y + z) * rows).astype(jnp.float32)
    near_ref[0] = gain
    near_ref[1] = gain * jnp.exp(-damping * to_y)
    for n, step in enumerate(STEPS):
        there = x ^ step
        ahead = jnp.maximum(x - there - 1, 0).astype(jnp.float32) * (16.0 * rows) + to_x
        before = (there < x).astype(jnp.float32)
        out_ref[n] = gain * jnp.exp(-damping * ahead) * before
    eight_ref[...] = jnp.exp(-8.0 * damping)
    since = 1.0 + lax.broadcasted_iota(jnp.int32, (8, LANES), 0).astype(jnp.float32)
    for g in range(damping.shape[1] // 8):
        for half in range(HALVES):
            part = damping_ref[half, 8 * g : 8 * g + 8, :]
            for m in range(8):
                powers_ref[8 * half + m, 8 * g : 8 * g + 8, :] = jnp.exp(
                    -spread(part, m) * since
                )


def project(gated_ref, weight_ref, pieces):
    own = lax.axis_index("ch")
    width = weight_ref.shape[1] // 4
    for out_ref, group, start in pieces:
        first = pl.multiple_of((own ^ group) * width + start, LANES)
        out_ref[...] = jnp.dot(
            gated_ref[...],
            weight_ref[:, pl.ds(first, out_ref.shape[1])],
            preferred_element_type=jnp.float32,
        )


def gate_kernel(pieces, *refs):
    query_ref, local_ref, powers_ref, eight_ref, base_ref, last_ref = refs[:6]
    arrived, weight_ref, gated_ref = refs[6:9], refs[9], refs[10]
    outs, state_ref = refs[11:-1], refs[-1]
    total = base_ref[...]
    for n in range(3):
        total = total + last_ref[n] * arrived[n][...]
    state_ref[...] = total
    outer, lanes = query_ref.shape[0], query_ref.shape[1] // 8

    def body(g, carry):
        block = pl.ds(pl.multiple_of(8 * g, 8), 8)
        rows = [local_ref[i, block, :] for i in range(outer)]
        for half in range(HALVES):
            entry, eight = state_ref[half, block, :], eight_ref[half, block, :]
            for m in range(8):
                term = spread(entry, m) * powers_ref[8 * half + m, block, :]
                factor = spread(eight, m)
                for i in range(outer):
                    rows[i] = rows[i] + term
                    if i + 1 < outer:
                        term = term * factor
        rows = [query_ref[i, block, :] * rows[i] for i in range(outer)]
        columns = pl.ds(pl.multiple_of(LANES * g, LANES), LANES)
        gated_ref[:, columns] = jnp.concatenate(rows, axis=0).astype(jnp.bfloat16)
        return carry

    lax.fori_loop(0, lanes, body, 0)
    project(gated_ref, weight_ref, [(o, *p) for o, p in zip(outs, pieces)])


def project_kernel(pieces, gated_ref, weight_ref, *outs):
    project(gated_ref, weight_ref, [(o, *p) for o, p in zip(outs, pieces)])


def run_own(axis, rows, damping_ref, state_ref, out_ref, own_ref):
    run_kernel(axis, rows, damping_ref, out_ref)
    own_ref[...] = out_ref[0] * state_ref[...]


def finish_kernel(*refs):
    *pieces, out_ref = refs
    half = len(pieces) // 2
    width = pieces[0].shape[1]
    for n in range(half):
        total = pieces[n][...] + pieces[half + n][...]
        out_ref[:, n * width : (n + 1) * width] = total.astype(jnp.bfloat16)


def partner_pairs(size, step):
    return [(i, i ^ step) for i in range(size)]


def local(value_rows, key_rows, query_rows, pole_weights, damping_speeds, out_weight):
    rows, channels = value_rows.shape
    count = lax.axis_size("seq")
    queries = tiles(query_rows)
    damping = tiles(damping_speeds)
    gain = tiles(pole_weights * jnp.sqrt(-jnp.expm1(-2.0 * damping_speeds)))
    shape = damping.shape

    def swap(state, axis):
        pairs = [partner_pairs(count, step * 4**axis) for step in STEPS]
        return [lax.ppermute(state, "seq", pair) for pair in pairs]

    def weighed(decays, first, terms):
        return sum(decays[first + n] * term for n, term in enumerate(terms))

    signal = tiles(key_rows * value_rows)
    state = kernel_call(
        end_state_kernel, f32(*shape), (signal, damping), 2_000_000_000, 600_000
    )
    decays_z, own_z = kernel_call(
        lambda *refs: run_own(0, rows, *refs),
        (f32(7, *shape), f32(*shape)),
        (damping, state),
        1_000_000_000,
        600_000,
    )
    decays_y = kernel_call(
        lambda *refs: run_kernel(1, rows, *refs),
        f32(7, *shape),
        (damping,),
        1_000_000_000,
        600_000,
    )
    near = kernel_call(
        local_kernel, f32(*signal.shape), (signal, damping, gain), 3_000_000_000, 1_000_000
    )
    last, to_run, eight, powers = kernel_call(
        lambda *refs: last_kernel(rows, *refs),
        (f32(3, *shape), f32(2, *shape), f32(*shape), f32(MODES, *shape[1:])),
        (damping, gain),
        1_000_000_000,
        1_000_000,
    )
    from_z = swap(state, 0)
    total_z = own_z + weighed(decays_z, 1, from_z)
    from_y = swap(total_z, 1)
    total_y = weighed(decays_y, 0, [total_z] + from_y)
    from_x = swap(total_y, 2)
    base = to_run[0] * weighed(decays_z, 4, from_z)
    base = base + to_run[1] * weighed(decays_y, 4, from_y)

    parts = 2
    width = out_weight.shape[1] // lax.axis_size("ch")
    piece = f32(rows, width // parts)
    starts = [n * (width // parts) for n in range(parts)]

    gated, first = kernel_call(
        lambda *refs: gate_kernel([(3, 0)], *refs),
        (jax.ShapeDtypeStruct((rows, channels), jnp.bfloat16), piece),
        (queries, near, powers, eight, base, last, *from_x, out_weight),
        1_500_000_000,
        3_000_000,
        (pltpu.VMEM(shape, jnp.float32),),
    )

    def projected(gated, pieces):
        return kernel_call(
            lambda *refs: project_kernel(pieces, *refs),
            (piece,) * len(pieces),
            (gated, out_weight),
            300_000_000 * len(pieces),
            1_000_000 * len(pieces),
        )

    def core_swap(pieces):
        return [lax.ppermute(one, "ch", partner_pairs(4, 1)) for one in pieces]

    def chip_swap(pieces):
        return [lax.ppermute(one, "ch", partner_pairs(4, 2)) for one in pieces]

    (kept,) = projected(gated, [(2, 0)])
    (arrived,) = core_swap([first])
    gated, away = lax.optimization_barrier((gated, kept + arrived))
    second, kept, *sent = projected(
        gated, [(3, starts[1]), (2, starts[1])] + [(g, n) for g in (1, 0) for n in starts]
    )
    arrived, *home = core_swap([second, *sent[:parts]])
    away = chip_swap([away, kept + arrived])
    home = [a + b for a, b in zip(sent[parts:], home)]
    return kernel_call(
        finish_kernel,
        jax.ShapeDtypeStruct((rows, width), jnp.bfloat16),
        (*home, *away),
        1_000_000,
        2_000_000,
    )


def solution(mesh):
    in_specs = (
        P("seq", "ch"),
        P("seq", "ch"),
        P("seq", "ch"),
        P(None, "ch"),
        P(None, "ch"),
        P("ch", None),
    )
    return jax.shard_map(
        local, mesh=mesh, in_specs=in_specs, out_specs=P("seq", "ch"), check_vma=False
    )
```

profile of v0, /device:TPU:1, one launch (start us, length us, event | category | flops | bytes accessed | tf_op | source)
XLA Modules:
  0.0 54.2 jit_solution(17228303314686897859)
XLA Ops:
  0.0 1.3 %multiply_bitcast_fusion.signal_ref = f32[16,64,128]{2,1,0:T(8,128)S(1)} fusion(f32[128,1024]{1,0:T(8,128)} %param.7, f32[128,1024]{1,0:T(8,128)} %param.6), kind=kLoop, calls=%fused_computation | loop fusion | flops 131072 | bytes 1572864 | tf_op jit(solution)/shard_map/reshape | solution.py:18
  1.3 0.0 copy-start.1
  1.3 0.8 %copy-done.1 = f32[16,1024]{1,0:T(8,128)S(1)} copy-done((f32[16,1024]{1,0:T(8,128)S(1)}, f32[16,1024]{1,0:T(8,128)}, u32[]{:S(2)}) %copy-start.1) | copy-done | bytes 65560
  2.1 0.8 %shard_map.66.refs_1_ = f32[2,64,128]{2,1,0:T(8,128)S(1)} custom-call(f32[16,64,128]{2,1,0:T(8,128)S(1)} %multiply_bitcast_fusion.signal_ref, f32[2,64,128]{2,1,0:T(8,128)S(1)} %bitcast.115), custom_call_target="tpu_custom_call" | custom-call | flops 2000000000 | bytes 600000 | tf_op jit(solution)/shard_map/pallas_call | solution.py:31
  2.9 0.0 copy-start.2
  3.0 7.8 %collective-permute-start.2 = (f32[2,64,128]{2,1,0:T(8,128)S(1)}, f32[2,64,128]{2,1,0:T(8,128)S(1)}, u32[]{:S(2)}, u32[]{:S(2)}) collective-permute-start(f32[2,64,128]{2,1,0:T(8,128)S(1)} %shard_map.66.refs_1_), channel_id=1, source_target_pairs={{0,8},{4,12},{8,0},{12,4},{16,24},{20,28},{24,16},{28,20},{32,40},... | collective-permute-start | bytes 196616 | tf_op jit(solution)/shard_map/ppermute | solution.py:204
  10.8 0.0 collective-permute-start.1
  10.8 1.2 %collective-permute-start = (f32[2,64,128]{2,1,0:T(8,128)S(1)}, f32[2,64,128]{2,1,0:T(8,128)S(1)}, u32[]{:S(2)}, u32[]{:S(2)}) collective-permute-start(f32[2,64,128]{2,1,0:T(8,128)S(1)} %shard_map.66.refs_1_), channel_id=1, source_target_pairs={{0,4},{4,0},{8,12},{12,8},{16,20},{20,16},{24,28},{28,24},{32,36},... | collective-permute-start | bytes 196616 | tf_op jit(solution)/shard_map/ppermute | solution.py:204
  12.0 0.1 shard_map.68
  12.1 0.0 copy-done.3
  12.1 0.1 shard_map.67
  12.2 0.0 slice-start
  12.2 0.0 copy-start
  12.2 0.3 collective-permute-done.2
  12.5 3.6 %collective-permute-done.1 = f32[2,64,128]{2,1,0:T(8,128)S(1)} collective-permute-done((f32[2,64,128]{2,1,0:T(8,128)S(1)}, f32[2,64,128]{2,1,0:T(8,128)S(1)}, u32[]{:S(2)}, u32[]{:S(2)}) %collective-permute-start.1) | collective-permute-done | bytes 65568 | tf_op jit(solution)/shard_map/ppermute | solution.py:204
  16.1 2.0 %collective-permute-done = f32[2,64,128]{2,1,0:T(8,128)S(1)} collective-permute-done((f32[2,64,128]{2,1,0:T(8,128)S(1)}, f32[2,64,128]{2,1,0:T(8,128)S(1)}, u32[]{:S(2)}, u32[]{:S(2)}) %collective-permute-start) | collective-permute-done | bytes 65568 | tf_op jit(solution)/shard_map/ppermute | solution.py:204
  18.2 3.0 %collective-permute-start.5 = (f32[2,64,128]{2,1,0:T(8,128)S(1)}, f32[2,64,128]{2,1,0:T(8,128)S(1)}, u32[]{:S(2)}, u32[]{:S(2)}) collective-permute-start(f32[2,64,128]{2,1,0:T(8,128)S(1)} %fusion.15), channel_id=1, source_target_pairs={{0,32},{4,36},{8,40},{12,44},{16,48},{20,52},{24,56},{28,60},{32,0... | collective-permute-start | bytes 196616 | tf_op jit(solution)/shard_map/ppermute | solution.py:204
  21.2 0.8 %collective-permute-start.4 = (f32[2,64,128]{2,1,0:T(8,128)S(1)}, f32[2,64,128]{2,1,0:T(8,128)S(1)}, u32[]{:S(2)}, u32[]{:S(2)}) collective-permute-start(f32[2,64,128]{2,1,0:T(8,128)S(1)} %fusion.15), channel_id=1, source_target_pairs={{0,48},{4,52},{8,56},{12,60},{16,32},{20,36},{24,40},{28,44},{32,1... | collective-permute-start | bytes 196616 | tf_op jit(solution)/shard_map/ppermute | solution.py:204
  22.0 0.0 collective-permute-start.3
  22.0 0.1 shard_map.65
  22.1 0.8 %collective-permute-done.5 = f32[2,64,128]{2,1,0:T(8,128)S(1)} collective-permute-done((f32[2,64,128]{2,1,0:T(8,128)S(1)}, f32[2,64,128]{2,1,0:T(8,128)S(1)}, u32[]{:S(2)}, u32[]{:S(2)}) %collective-permute-start.5) | collective-permute-done | bytes 65568 | tf_op jit(solution)/shard_map/ppermute | solution.py:204
  22.9 2.6 %collective-permute-done.4 = f32[2,64,128]{2,1,0:T(8,128)S(1)} collective-permute-done((f32[2,64,128]{2,1,0:T(8,128)S(1)}, f32[2,64,128]{2,1,0:T(8,128)S(1)}, u32[]{:S(2)}, u32[]{:S(2)}) %collective-permute-start.4) | collective-permute-done | bytes 65568 | tf_op jit(solution)/shard_map/ppermute | solution.py:204
  25.5 0.0 collective-permute-done.3
  25.5 0.1 fusion.1
  25.6 0.0 slice-start.1
  25.6 2.8 %collective-permute-start.8 = (f32[2,64,128]{2,1,0:T(8,128)S(1)}, f32[2,64,128]{2,1,0:T(8,128)S(1)}, u32[]{:S(2)}, u32[]{:S(2)}) collective-permute-start(f32[2,64,128]{2,1,0:T(8,128)S(1)} %get-tuple-element.37), channel_id=1, source_target_pairs={{0,128},{4,132},{8,136},{12,140},{16,144},{20,148},{24,152},{28,15... | collective-permute-start | bytes 196616 | tf_op jit(solution)/shard_map/ppermute | solution.py:204
  28.5 0.9 %collective-permute-start.7 = (f32[2,64,128]{2,1,0:T(8,128)S(1)}, f32[2,64,128]{2,1,0:T(8,128)S(1)}, u32[]{:S(2)}, u32[]{:S(2)}) collective-permute-start(f32[2,64,128]{2,1,0:T(8,128)S(1)} %get-tuple-element.37), channel_id=1, source_target_pairs={{0,192},{4,196},{8,200},{12,204},{16,208},{20,212},{24,216},{28,22... | collective-permute-start | bytes 196616 | tf_op jit(solution)/shard_map/ppermute | solution.py:204
  29.3 0.0 collective-permute-start.6
  29.3 1.2 %shard_map.64.refs_1_ = f32[16,64,128]{2,1,0:T(8,128)S(1)} custom-call(f32[16,64,128]{2,1,0:T(8,128)S(1)} %multiply_bitcast_fusion.signal_ref, f32[2,64,128]{2,1,0:T(8,128)S(1)} %bitcast.119, f32[2,64,128]{2,1,0:T(8,128)S(1)} %multiply_bitcast_fusion.1.gain_ref.refs_1_), custom_call_target="tpu_custom_call" | custom-call | flops 3000000000 | bytes 1000000 | tf_op jit(solution)/shard_map/pallas_call | solution.py:31
  30.5 0.0 collective-permute-done.8.refs_8_
  30.6 2.9 %collective-permute-done.7.refs_7_ = f32[2,64,128]{2,1,0:T(8,128)S(1)} collective-permute-done((f32[2,64,128]{2,1,0:T(8,128)S(1)}, f32[2,64,128]{2,1,0:T(8,128)S(1)}, u32[]{:S(2)}, u32[]{:S(2)}) %collective-permute-start.7) | collective-permute-done | bytes 65568 | tf_op jit(solution)/shard_map/ppermute | solution.py:204
  33.5 0.0 collective-permute-done.6.refs_6_
  33.5 1.0 %shard_map.69 = (bf16[128,1024]{1,0:T(8,128)(2,1)S(1)}, f32[128,512]{1,0:T(8,128)S(1)}) custom-call(f32[16,64,128]{2,1,0:T(8,128)S(1)} %bitcast.114, f32[16,64,128]{2,1,0:T(8,128)S(1)} %shard_map.64.refs_1_, f32[16,64,128]{2,1,0:T(8,128)S(1)} %get-tuple-element.21.refs_2_, f32[2,64,128]{2,1,0:T(8,128)S(1)} %get-tuple-element.22.refs_3_, ...), custom_call_target="tpu_custom_call" | custom-call | flops 1500000000 | bytes 3000000 | tf_op jit(solution)/shard_map/pallas_call | solution.py:31
  34.6 2.9 %collective-permute-start.9 = (f32[128,512]{1,0:T(8,128)S(1)}, f32[128,512]{1,0:T(8,128)S(1)}, u32[]{:S(2)}, u32[]{:S(2)}) collective-permute-start(f32[128,512]{1,0:T(8,128)S(1)} %get-tuple-element.28), channel_id=1, source_target_pairs={{0,1},{1,0},{2,3},{3,2},{4,5},{5,4},{6,7},{7,6},{8,9},{9,8},{10,11... | collective-permute-start | bytes 786440 | tf_op jit(solution)/shard_map/ppermute | solution.py:269
  37.5 0.3 shard_map.70
  37.8 0.8 %collective-permute-done.9 = f32[128,512]{1,0:T(8,128)S(1)} collective-permute-done((f32[128,512]{1,0:T(8,128)S(1)}, f32[128,512]{1,0:T(8,128)S(1)}, u32[]{:S(2)}, u32[]{:S(2)}) %collective-permute-start.9) | collective-permute-done | bytes 262176 | tf_op jit(solution)/shard_map/ppermute | solution.py:269
  38.7 1.0 %shard_map.71 = (f32[128,512]{1,0:T(8,128)S(1)}, f32[128,512]{1,0:T(8,128)S(1)}, f32[128,512]{1,0:T(8,128)S(1)}, f32[128,512]{1,0:T(8,128)S(1)}, f32[128,512]{1,0:T(8,128)S(1)}, /*index=5*/f32[128,512]{1,0:T(8,128)S(1)}) custom-call(bf16[128,1024]{1,0:T(8,128)(2,1)S(1)} %get-tuple-element.29.refs_0_, bf16[1024,4096]{1,0:T(8,128)(2,1)S(1)} %bitcast.113), custom_call_target="tpu_custom_call" | custom-call | flops 1800000000 | bytes 6000000 | tf_op jit(solution)/shard_map/pallas_call | solution.py:31
  39.7 0.5 collective-permute-start.13
  40.2 0.1 collective-permute-start.10
  40.3 0.4 collective-permute-start.12
  40.7 0.7 %collective-permute-start.11 = (f32[128,512]{1,0:T(8,128)S(1)}, f32[128,512]{1,0:T(8,128)S(1)}, u32[]{:S(2)}, u32[]{:S(2)}) collective-permute-start(f32[128,512]{1,0:T(8,128)S(1)} %get-tuple-element.33), channel_id=1, source_target_pairs={{0,1},{1,0},{2,3},{3,2},{4,5},{5,4},{6,7},{7,6},{8,9},{9,8},{10,11... | collective-permute-start | bytes 786440 | tf_op jit(solution)/shard_map/ppermute | solution.py:269
  41.3 0.0 collective-permute-done.13
  41.4 1.2 %collective-permute-start.14 = (f32[128,512]{1,0:T(8,128)S(1)}, f32[128,512]{1,0:T(8,128)S(1)}, u32[]{:S(2)}, u32[]{:S(2)}) collective-permute-start(f32[128,512]{1,0:T(8,128)S(1)} %add.59), channel_id=1, source_target_pairs={{0,2},{1,3},{2,0},{3,1},{4,6},{5,7},{6,4},{7,5},{8,10},{9,11},{10,... | collective-permute-start | bytes 786440 | tf_op jit(solution)/shard_map/ppermute | solution.py:272
  42.6 0.0 collective-permute-done.10
  42.6 0.0 collective-permute-done.11
  42.7 5.2 %collective-permute-done.12.refs_2_ = f32[128,512]{1,0:T(8,128)S(1)} collective-permute-done((f32[128,512]{1,0:T(8,128)S(1)}, f32[128,512]{1,0:T(8,128)S(1)}, u32[]{:S(2)}, u32[]{:S(2)}) %collective-permute-start.12) | collective-permute-done | bytes 262176 | tf_op jit(solution)/shard_map/ppermute | solution.py:272
  47.8 5.6 %collective-permute-done.14.refs_3_ = f32[128,512]{1,0:T(8,128)S(1)} collective-permute-done((f32[128,512]{1,0:T(8,128)S(1)}, f32[128,512]{1,0:T(8,128)S(1)}, u32[]{:S(2)}, u32[]{:S(2)}) %collective-permute-start.14) | collective-permute-done | bytes 262176 | tf_op jit(solution)/shard_map/ppermute | solution.py:272
  53.4 0.8 %shard_map.72 = bf16[128,1024]{1,0:T(8,128)(2,1)} custom-call(f32[128,512]{1,0:T(8,128)S(1)} %add.57.refs_0_, f32[128,512]{1,0:T(8,128)S(1)} %add.58.refs_1_, f32[128,512]{1,0:T(8,128)S(1)} %collective-permute-done.12.refs_2_, f32[128,512]{1,0:T(8,128)S(1)} %collective-permute-done.14.refs_3_), custom_call_target="tpu_custom_call" | custom-call | flops 1000000 | bytes 2000000 | tf_op jit(solution)/shard_map/pallas_call | solution.py:31
  (12 shorter events, 0.2 us)
Async XLA Ops:
  0.0 12.1 %copy-start.3 = (f32[16,1024]{1,0:T(8,128)S(1)}, f32[16,1024]{1,0:T(8,128)}, u32[]{:S(2)}) copy-start(f32[16,1024]{1,0:T(8,128)} %param.9) | copy-start | bytes 196612
  1.3 0.8 %copy-start.1 = (f32[16,1024]{1,0:T(8,128)S(1)}, f32[16,1024]{1,0:T(8,128)}, u32[]{:S(2)}) copy-start(f32[16,1024]{1,0:T(8,128)} %param.10) | copy-start | bytes 196612
  2.9 26.4 %copy-start.2 = (f32[16,1024]{1,0:T(8,128)S(1)}, f32[16,1024]{1,0:T(8,128)}, u32[]{:S(2)}) copy-start(f32[16,1024]{1,0:T(8,128)} %param.10) | copy-start | bytes 196612
  3.0 9.6 %collective-permute-start.2 = (f32[2,64,128]{2,1,0:T(8,128)S(1)}, f32[2,64,128]{2,1,0:T(8,128)S(1)}, u32[]{:S(2)}, u32[]{:S(2)}) collective-permute-start(f32[2,64,128]{2,1,0:T(8,128)S(1)} %shard_map.66.refs_1_), channel_id=1, source_target_pairs={{0,8},{4,12},{8,0},{12,4},{16,24},{20,28},{24,16},{28,20},{32,40},... | collective-permute-start | bytes 196616 | tf_op jit(solution)/shard_map/ppermute | solution.py:204
  10.8 5.3 %collective-permute-start.1 = (f32[2,64,128]{2,1,0:T(8,128)S(1)}, f32[2,64,128]{2,1,0:T(8,128)S(1)}, u32[]{:S(2)}, u32[]{:S(2)}) collective-permute-start(f32[2,64,128]{2,1,0:T(8,128)S(1)} %shard_map.66.refs_1_), channel_id=1, source_target_pairs={{0,12},{4,8},{8,4},{12,0},{16,28},{20,24},{24,20},{28,16},{32,44},... | collective-permute-start | bytes 196616 | tf_op jit(solution)/shard_map/ppermute | solution.py:204
  10.8 7.4 %collective-permute-start = (f32[2,64,128]{2,1,0:T(8,128)S(1)}, f32[2,64,128]{2,1,0:T(8,128)S(1)}, u32[]{:S(2)}, u32[]{:S(2)}) collective-permute-start(f32[2,64,128]{2,1,0:T(8,128)S(1)} %shard_map.66.refs_1_), channel_id=1, source_target_pairs={{0,4},{4,0},{8,12},{12,8},{16,20},{20,16},{24,28},{28,24},{32,36},... | collective-permute-start | bytes 196616 | tf_op jit(solution)/shard_map/ppermute | solution.py:204
  12.2 21.3 %slice-start = ((s8[8388608]{0:T(1024)(128)(4,1)}), s8[4194304]{0:T(1024)(128)(4,1)S(1)}, s32[]{:S(2)}) async-start(s8[8388608]{0:T(1024)(128)(4,1)} %bitcast.112), calls=%async_computation | async-start | bytes 8388608
  12.2 21.3 %copy-start = (f32[128,1024]{1,0:T(8,128)S(1)}, f32[128,1024]{1,0:T(8,128)}, u32[]{:S(2)}) copy-start(f32[128,1024]{1,0:T(8,128)} %param.8) | copy-start | bytes 1572868
  18.2 4.7 %collective-permute-start.5 = (f32[2,64,128]{2,1,0:T(8,128)S(1)}, f32[2,64,128]{2,1,0:T(8,128)S(1)}, u32[]{:S(2)}, u32[]{:S(2)}) collective-permute-start(f32[2,64,128]{2,1,0:T(8,128)S(1)} %fusion.15), channel_id=1, source_target_pairs={{0,32},{4,36},{8,40},{12,44},{16,48},{20,52},{24,56},{28,60},{32,0... | collective-permute-start | bytes 196616 | tf_op jit(solution)/shard_map/ppermute | solution.py:204
  21.2 4.3 %collective-permute-start.4 = (f32[2,64,128]{2,1,0:T(8,128)S(1)}, f32[2,64,128]{2,1,0:T(8,128)S(1)}, u32[]{:S(2)}, u32[]{:S(2)}) collective-permute-start(f32[2,64,128]{2,1,0:T(8,128)S(1)} %fusion.15), channel_id=1, source_target_pairs={{0,48},{4,52},{8,56},{12,60},{16,32},{20,36},{24,40},{28,44},{32,1... | collective-permute-start | bytes 196616 | tf_op jit(solution)/shard_map/ppermute | solution.py:204
  22.0 3.6 %collective-permute-start.3 = (f32[2,64,128]{2,1,0:T(8,128)S(1)}, f32[2,64,128]{2,1,0:T(8,128)S(1)}, u32[]{:S(2)}, u32[]{:S(2)}) collective-permute-start(f32[2,64,128]{2,1,0:T(8,128)S(1)} %fusion.15), channel_id=1, source_target_pairs={{0,16},{4,20},{8,24},{12,28},{16,0},{20,4},{24,8},{28,12},{32,48},... | collective-permute-start | bytes 196616 | tf_op jit(solution)/shard_map/ppermute | solution.py:204
  25.6 7.9 %slice-start.1 = ((s8[8388608]{0:T(1024)(128)(4,1)}), s8[4194304]{0:T(1024)(128)(4,1)S(1)}, s32[]{:S(2)}) async-start(s8[8388608]{0:T(1024)(128)(4,1)} %bitcast.112), calls=%async_computation.1 | async-start | bytes 8388608
  25.6 4.9 %collective-permute-start.8 = (f32[2,64,128]{2,1,0:T(8,128)S(1)}, f32[2,64,128]{2,1,0:T(8,128)S(1)}, u32[]{:S(2)}, u32[]{:S(2)}) collective-permute-start(f32[2,64,128]{2,1,0:T(8,128)S(1)} %get-tuple-element.37), channel_id=1, source_target_pairs={{0,128},{4,132},{8,136},{12,140},{16,144},{20,148},{24,152},{28,15... | collective-permute-start | bytes 196616 | tf_op jit(solution)/shard_map/ppermute | solution.py:204
  28.5 5.0 %collective-permute-start.7 = (f32[2,64,128]{2,1,0:T(8,128)S(1)}, f32[2,64,128]{2,1,0:T(8,128)S(1)}, u32[]{:S(2)}, u32[]{:S(2)}) collective-permute-start(f32[2,64,128]{2,1,0:T(8,128)S(1)} %get-tuple-element.37), channel_id=1, source_target_pairs={{0,192},{4,196},{8,200},{12,204},{16,208},{20,212},{24,216},{28,22... | collective-permute-start | bytes 196616 | tf_op jit(solution)/shard_map/ppermute | solution.py:204
  29.3 4.2 %collective-permute-start.6 = (f32[2,64,128]{2,1,0:T(8,128)S(1)}, f32[2,64,128]{2,1,0:T(8,128)S(1)}, u32[]{:S(2)}, u32[]{:S(2)}) collective-permute-start(f32[2,64,128]{2,1,0:T(8,128)S(1)} %get-tuple-element.37), channel_id=1, source_target_pairs={{0,64},{4,68},{8,72},{12,76},{16,80},{20,84},{24,88},{28,92},{32,9... | collective-permute-start | bytes 196616 | tf_op jit(solution)/shard_map/ppermute | solution.py:204
  34.6 4.1 %collective-permute-start.9 = (f32[128,512]{1,0:T(8,128)S(1)}, f32[128,512]{1,0:T(8,128)S(1)}, u32[]{:S(2)}, u32[]{:S(2)}) collective-permute-start(f32[128,512]{1,0:T(8,128)S(1)} %get-tuple-element.28), channel_id=1, source_target_pairs={{0,1},{1,0},{2,3},{3,2},{4,5},{5,4},{6,7},{7,6},{8,9},{9,8},{10,11... | collective-permute-start | bytes 786440 | tf_op jit(solution)/shard_map/ppermute | solution.py:269
  39.7 1.6 %collective-permute-start.13 = (f32[128,512]{1,0:T(8,128)S(1)}, f32[128,512]{1,0:T(8,128)S(1)}, u32[]{:S(2)}, u32[]{:S(2)}) collective-permute-start(f32[128,512]{1,0:T(8,128)S(1)} %get-tuple-element.36), channel_id=1, source_target_pairs={{0,1},{1,0},{2,3},{3,2},{4,5},{5,4},{6,7},{7,6},{8,9},{9,8},{10,11... | collective-permute-start | bytes 786440 | tf_op jit(solution)/shard_map/ppermute | solution.py:269
  40.2 2.4 %collective-permute-start.10 = (f32[128,512]{1,0:T(8,128)S(1)}, f32[128,512]{1,0:T(8,128)S(1)}, u32[]{:S(2)}, u32[]{:S(2)}) collective-permute-start(f32[128,512]{1,0:T(8,128)S(1)} %get-tuple-element.31), channel_id=1, source_target_pairs={{0,1},{1,0},{2,3},{3,2},{4,5},{5,4},{6,7},{7,6},{8,9},{9,8},{10,11... | collective-permute-start | bytes 786440 | tf_op jit(solution)/shard_map/ppermute | solution.py:269
  40.3 7.5 %collective-permute-start.12 = (f32[128,512]{1,0:T(8,128)S(1)}, f32[128,512]{1,0:T(8,128)S(1)}, u32[]{:S(2)}, u32[]{:S(2)}) collective-permute-start(f32[128,512]{1,0:T(8,128)S(1)} %add.56), channel_id=1, source_target_pairs={{0,2},{1,3},{2,0},{3,1},{4,6},{5,7},{6,4},{7,5},{8,10},{9,11},{10,... | collective-permute-start | bytes 786440 | tf_op jit(solution)/shard_map/ppermute | solution.py:272
  40.7 1.9 %collective-permute-start.11 = (f32[128,512]{1,0:T(8,128)S(1)}, f32[128,512]{1,0:T(8,128)S(1)}, u32[]{:S(2)}, u32[]{:S(2)}) collective-permute-start(f32[128,512]{1,0:T(8,128)S(1)} %get-tuple-element.33), channel_id=1, source_target_pairs={{0,1},{1,0},{2,3},{3,2},{4,5},{5,4},{6,7},{7,6},{8,9},{9,8},{10,11... | collective-permute-start | bytes 786440 | tf_op jit(solution)/shard_map/ppermute | solution.py:269
  41.4 12.1 %collective-permute-start.14 = (f32[128,512]{1,0:T(8,128)S(1)}, f32[128,512]{1,0:T(8,128)S(1)}, u32[]{:S(2)}, u32[]{:S(2)}) collective-permute-start(f32[128,512]{1,0:T(8,128)S(1)} %add.59), channel_id=1, source_target_pairs={{0,2},{1,3},{2,0},{3,1},{4,6},{5,7},{6,4},{7,5},{8,10},{9,11},{10,... | collective-permute-start | bytes 786440 | tf_op jit(solution)/shard_map/ppermute | solution.py:272
where the time goes:
time: 54.3 us; the launch traced here: 54.2 us
  waiting for transfers between devices  23.9 us (44%)
  starting transfers between devices  22.2 us (41%)
  Pallas kernels  5.43 us (10%)
  other arithmetic  1.61 us (3%)
  local copies, waits for them, and re-layouts  0.87 us (2%)
    ppermute x9, starting transfers between devices, swap(): return [lax.ppermute(state, 'seq', pair) for pair in pairs]  16.5 us
    ppermute x9, waiting for transfers between devices, swap(): return [lax.ppermute(state, 'seq', pair) for pair in pairs]  12.3 us
    ppermute x2, waiting for transfers between devices, chip_swap(): return [lax.ppermute(one, 'ch', partner_pairs(4, 2)) for one in pieces]  10.8 us
    pallas_call x9, Pallas kernels, kernel_call(): pl.pallas_call(body, out_shape=out_shape, in_specs=[pl.BlockSpec(memory_s...  5.43 us
    ppermute x4, starting transfers between devices, core_swap(): return [lax.ppermute(one, 'ch', partner_pairs(4, 1)) for one in pieces]  4.16 us
    ppermute x2, starting transfers between devices, chip_swap(): return [lax.ppermute(one, 'ch', partner_pairs(4, 2)) for one in pieces]  1.54 us
    reshape x2, other arithmetic, tiles(): cut.transpose(0, 2, 1, 3).reshape(rows // 8, 8 * (columns // LANES), LANES)  1.34 us
  transfers between devices with their start and end apart: 15, of which 9 were waited for; matrix products, arithmetic and copies ran while one was open for 0% of the time, Pallas kernels for 3%

commit v1 on v0

v1 whole, which is shorter than its diff:
```python
import jax
import jax.numpy as jnp
from jax import lax
from jax.experimental import pallas as pl
from jax.experimental.pallas import tpu as pltpu
from jax.sharding import PartitionSpec as P

MODES = 16
HALVES = MODES // 8
LANES = 128
SCOPE = 12 * 1024 * 1024
STEPS = (1, 3, 2)
HANDED = 8


def tiles(array):
    rows, columns = array.shape
    cut = array.reshape(rows // 8, 8, columns // LANES, LANES)
    return cut.transpose(0, 2, 1, 3).reshape(rows // 8, 8 * (columns // LANES), LANES)


def spread(values, index):
    return jnp.broadcast_to(values[index : index + 1, :], (8, LANES))


def f32(*shape):
    return jax.ShapeDtypeStruct(shape, jnp.float32)


def kernel_call(body, out_shape, inputs, flops, size, scratch=()):
    outs = jax.tree.map(lambda _: pl.BlockSpec(memory_space=pltpu.VMEM), out_shape)
    return pl.pallas_call(
        body,
        out_shape=out_shape,
        in_specs=[pl.BlockSpec(memory_space=pltpu.VMEM)] * len(inputs),
        out_specs=outs,
        scratch_shapes=scratch,
        cost_estimate=pl.CostEstimate(flops=flops, bytes_accessed=size, transcendentals=0),
        compiler_params=pltpu.CompilerParams(vmem_limit_bytes=SCOPE),
    )(*inputs)


def end_state_kernel(signal_ref, damping_ref, state_ref):
    outer, lanes = signal_ref.shape[0], signal_ref.shape[1] // 8
    place = lax.broadcasted_iota(jnp.int32, (8, LANES), 0)
    for g in range(lanes):
        block = pl.ds(8 * g, 8)
        signal = [signal_ref[i, block, :] for i in range(outer)]
        for half in range(HALVES):
            decay = jnp.exp(-damping_ref[half, block, :])
            result = None
            for m in range(8):
                once = spread(decay, m)
                twice = once * once
                four = twice * twice
                eight = four * four
                total = signal[0]
                for i in range(1, outer):
                    total = eight * total + signal[i]
                total = total + once * pltpu.roll(total, 1, 0)
                total = total + twice * pltpu.roll(total, 2, 0)
                total = total + four * pltpu.roll(total, 4, 0)
                if m != 7:
                    total = pltpu.roll(total, m + 1, 0)
                result = total if result is None else jnp.where(place == m, total, result)
            state_ref[half, block, :] = result


def local_kernel(signal_ref, damping_ref, gain_ref, query_ref, out_ref, handed_ref):
    def row(ref, outer, inner):
        return ref[outer, pl.ds(inner, 8, stride=8), :]

    decay = [jnp.exp(-row(damping_ref, m // 8, m % 8)) for m in range(MODES)]
    gain = [row(gain_ref, m // 8, m % 8) for m in range(MODES)]

    def body(outer, state):
        for inner in range(8):
            signal = row(signal_ref, outer, inner)
            state = tuple(decay[m] * state[m] + signal for m in range(MODES))
            terms = [gain[m] * state[m] for m in range(MODES)]
            while len(terms) > 1:
                terms = [terms[n] + terms[n + 1] for n in range(0, len(terms), 2)]
            out_ref[outer, pl.ds(inner, 8, stride=8), :] = terms[0]
        return state

    zero = jnp.zeros((8, LANES), jnp.float32)
    lax.fori_loop(0, signal_ref.shape[0], body, (zero,) * MODES)
    count = handed_ref.shape[1]
    handed_ref[0] = query_ref[0:count]
    handed_ref[1] = out_ref[0:count]


def places():
    at = lax.axis_index("seq")
    return [lax.rem(at, 4), lax.rem(lax.div(at, 4), 4), lax.div(at, 16)]


def helped(z):
    return lax.rem(z + jnp.where(lax.axis_index("ch") < 2, 3, 1), 4)


def entry_decay(damping, target, there):
    ahead = jnp.maximum(target - there - 1, 0).astype(jnp.float32)
    before = (there < target).astype(jnp.float32)
    return jnp.exp(damping * ahead) * before


def run_kernel(axis, rows, damping_ref, out_ref):
    here = places()[axis]
    damping = damping_ref[...] * (-1.0 * rows * 4**axis)
    for n, step in enumerate((0, *STEPS)):
        there = here ^ step
        out_ref[n] = jnp.exp(damping * (3 - there).astype(jnp.float32))
        if step:
            out_ref[3 + n] = entry_decay(damping, here, there)
        if axis == 0:
            out_ref[7 + n] = entry_decay(damping, helped(here), there)


def run_own(axis, rows, damping_ref, state_ref, out_ref, own_ref):
    run_kernel(axis, rows, damping_ref, out_ref)
    own_ref[...] = out_ref[0] * state_ref[...]


def last_kernel(rows, damping_ref, gain_ref, out_ref, scale_ref, eight_ref, powers_ref):
    z, y, x = places()
    damping, gain = damping_ref[...], gain_ref[...]
    scale_ref[0] = gain
    for n, target in enumerate((z, helped(z))):
        scale_ref[1 + n] = gain * jnp.exp(-damping * (target * rows).astype(jnp.float32))
    to_run = jnp.exp(-damping * (4 * y * rows).astype(jnp.float32))
    for n, step in enumerate(STEPS):
        out_ref[n] = to_run * entry_decay(damping * (-16.0 * rows), x, x ^ step)
    eight_ref[...] = jnp.exp(-8.0 * damping)
    since = 1.0 + lax.broadcasted_iota(jnp.int32, (8, LANES), 0).astype(jnp.float32)
    for g in range(damping.shape[1] // 8):
        for half in range(HALVES):
            part = damping_ref[half, 8 * g : 8 * g + 8, :]
            for m in range(8):
                powers_ref[8 * half + m, 8 * g : 8 * g + 8, :] = jnp.exp(
                    -spread(part, m) * since
                )


def project(gated, weight_ref, group):
    width = weight_ref.shape[1] // 4
    first = pl.multiple_of((lax.axis_index("ch") ^ group) * width, LANES)
    return jnp.dot(
        gated, weight_ref[:, pl.ds(first, width)], preferred_element_type=jnp.float32
    )


def project_away(gated_ref, weight_ref, group, out_ref):
    skipped = gated_ref.shape[0] - out_ref.shape[0]
    out_ref[...] = project(gated_ref[skipped:, :], weight_ref, group)


def gate_kernel(*refs):
    query_ref, local_ref, handed_ref, powers_ref, eight_ref = refs[:5]
    bases, scale_ref, last_ref, arrived, weight_ref = refs[5:7], *refs[7:9], refs[9:12], refs[12]
    gated_ref, sent_ref, state_ref = refs[13:]
    far = sum(last_ref[n] * arrived[n][...] for n in range(3))
    for n in range(2):
        state_ref[n] = bases[n][...] + scale_ref[1 + n] * far
    blocks = ((query_ref, local_ref), (handed_ref.at[0], handed_ref.at[1]))

    def body(g, carry):
        block = pl.ds(pl.multiple_of(8 * g, 8), 8)
        columns = pl.ds(pl.multiple_of(LANES * g, LANES), LANES)
        first = 0
        for n, (queries, locals_) in enumerate(blocks):
            outer = queries.shape[0]
            rows = [locals_[i, block, :] for i in range(outer)]
            for half in range(HALVES):
                entry, eight = state_ref[n, half, block, :], eight_ref[half, block, :]
                for m in range(8):
                    term = spread(entry, m) * powers_ref[8 * half + m, block, :]
                    factor = spread(eight, m)
                    for i in range(outer):
                        rows[i] = rows[i] + term
                        if i + 1 < outer:
                            term = term * factor
            rows = [queries[i, block, :] * rows[i] for i in range(outer)]
            gated_ref[pl.ds(first, 8 * outer), columns] = jnp.concatenate(
                rows, axis=0
            ).astype(jnp.bfloat16)
            first += 8 * outer
        return carry

    lax.fori_loop(0, query_ref.shape[1] // 8, body, 0)
    project_away(gated_ref, weight_ref, 3, sent_ref)


def rest_kernel(gated_ref, weight_ref, kept_ref, sent_ref, home_ref):
    project_away(gated_ref, weight_ref, 2, kept_ref)
    rows = home_ref.shape[0]
    sent_ref[...] = project(gated_ref[:rows, :], weight_ref, 1)
    home_ref[...] = project(gated_ref[:rows, :], weight_ref, 0)


def finish_kernel(home_ref, helped_ref, own_ref, out_ref):
    count = helped_ref.shape[0]
    out_ref[:count, :] = (home_ref[:count, :] + helped_ref[...]).astype(jnp.bfloat16)
    out_ref[count:, :] = (home_ref[count:, :] + own_ref[...]).astype(jnp.bfloat16)


def partner_pairs(size, step):
    return [(i, i ^ step) for i in range(size)]


def along_z(count, turn):
    pairs = []
    for i in range(4 * count):
        z, low = turn((i // 4) % 4, (i // 2) % 2)
        pairs.append((i, i // 16 * 16 + (z % 4) * 4 + low * 2 + i % 2))
    return pairs


def local(value_rows, key_rows, query_rows, pole_weights, damping_speeds, out_weight):
    rows, channels = value_rows.shape
    count = lax.axis_size("seq")
    queries = tiles(query_rows)
    damping = tiles(damping_speeds)
    gain = tiles(pole_weights * jnp.sqrt(-jnp.expm1(-2.0 * damping_speeds)))
    shape = damping.shape

    def swap(state, axis):
        pairs = [partner_pairs(count, step * 4**axis) for step in STEPS]
        return [lax.ppermute(state, "seq", pair) for pair in pairs]

    def run_total(own, decays, arrived):
        near_by, farthest = arrived[:-1], arrived[-1]
        own = lax.optimization_barrier(own + decays[len(arrived)] * farthest)
        return own + weighed(decays, 1, near_by)

    def weighed(decays, first, terms):
        return sum(decays[first + n] * term for n, term in enumerate(terms))

    signal = tiles(key_rows * value_rows)
    state = kernel_call(
        end_state_kernel, f32(*shape), (signal, damping), 2_000_000_000, 600_000
    )
    decays_z, own_z = kernel_call(
        lambda *refs: run_own(0, rows, *refs),
        (f32(11, *shape), f32(*shape)),
        (damping, state),
        1_000_000_000,
        800_000,
    )
    decays_y = kernel_call(
        lambda *refs: run_kernel(1, rows, *refs),
        f32(7, *shape),
        (damping,),
        1_000_000_000,
        600_000,
    )
    near, handed = kernel_call(
        local_kernel,
        (f32(*signal.shape), f32(2, HANDED, *signal.shape[1:])),
        (signal, damping, gain, queries),
        3_000_000_000,
        1_500_000,
    )
    last, scale, eight, powers = kernel_call(
        lambda *refs: last_kernel(rows, *refs),
        (f32(3, *shape), f32(3, *shape), f32(*shape), f32(MODES, *shape[1:])),
        (damping, gain),
        1_000_000_000,
        1_000_000,
    )
    from_z = swap(state, 0)
    total_z = run_total(own_z, decays_z, from_z)
    total_z, _ = lax.optimization_barrier((total_z, handed))
    handed = lax.ppermute(
        handed, ("seq", "ch"), along_z(count, lambda z, low: (z + 1 - 2 * low, low))
    )
    from_y = swap(total_z, 1)
    total_y = run_total(decays_y[0] * total_z, decays_y, from_y)
    from_x = swap(total_y, 2)
    from_runs = weighed(decays_y, 4, from_y)
    bases = [
        scale[0] * weighed(decays_z, 4, from_z) + scale[1] * from_runs,
        scale[0] * weighed(decays_z, 7, [state] + from_z) + scale[2] * from_runs,
    ]

    width = out_weight.shape[1] // lax.axis_size("ch")
    whole = f32(rows, width)
    gated, sent = kernel_call(
        gate_kernel,
        (jax.ShapeDtypeStruct((rows + 8 * HANDED, channels), jnp.bfloat16), whole),
        (
            queries,
            near,
            handed,
            powers,
            eight,
            *bases,
            scale,
            last,
            *from_x,
            out_weight,
        ),
        2_000_000_000,
        3_000_000,
        (pltpu.VMEM((2, *shape), jnp.float32),),
    )
    kept, home_sent, home_kept = kernel_call(
        rest_kernel, (whole,) * 3, (gated, out_weight), 1_500_000_000, 2_000_000
    )

    def core_swap(one):
        return lax.ppermute(one, "ch", partner_pairs(4, 1))

    away = kept + core_swap(sent)
    away, home_sent = lax.optimization_barrier((away, home_sent))
    cut = rows - 8 * HANDED
    helped_away = lax.ppermute(
        away[cut:],
        ("seq", "ch"),
        along_z(count, lambda z, low: (z - 1 + 2 * low, 1 - low)),
    )
    own_away = lax.ppermute(away[:cut], "ch", partner_pairs(4, 2))
    home = home_kept + core_swap(home_sent)
    return kernel_call(
        finish_kernel,
        jax.ShapeDtypeStruct((rows, width), jnp.bfloat16),
        (home, helped_away, own_away),
        1_000_000,
        2_000_000,
    )


def solution(mesh):
    in_specs = (
        P("seq", "ch"),
        P("seq", "ch"),
        P("seq", "ch"),
        P(None, "ch"),
        P(None, "ch"),
        P("ch", None),
    )
    return jax.shard_map(
        local, mesh=mesh, in_specs=in_specs, out_specs=P("seq", "ch"), check_vma=False
    )
```

time: 54.3 us -> 50.9 us (0.937)
  waiting for transfers between devices: 23.9 us -> 17.8 us
  starting transfers between devices: 22.2 us -> 24.6 us
    ppermute x6 -> x5, waiting for transfers between devices: 11.6 us -> 6.66 us  [the longest x1 4.3 us: local(): own_away = lax.ppermute(away[:cut], 'ch', partner_pairs(4, 2))]
    ppermute x6 -> x5, starting transfers between devices: 5.7 us -> 7.99 us  [the longest x2 3.27 us: core_swap(): return lax.ppermute(one, 'ch', partner_pairs(4, 1))]
    ppermute x9, waiting for transfers between devices: 12.3 us -> 11.1 us  [swap(): return [lax.ppermute(state, 'seq', pair) for pair in pairs]]
    pallas_call x9 -> x8, Pallas kernels: 5.43 us -> 5.67 us  [kernel_call(): pl.pallas_call(body, out_shape=out_shape, in_specs=[pl.BlockSpec(memory_s...]
  transfers between devices with their start and end apart: 15 -> 14, of which waited for: 9 -> 9; matrix products, arithmetic and copies ran while one was open for 0% -> 1% of each run, Pallas kernels for 3% -> 5%
where the time goes in v1:
time: 50.9 us; the launch traced here: 50.8 us
  starting transfers between devices  24.6 us (48%)
  waiting for transfers between devices  17.8 us (35%)
  Pallas kernels  5.67 us (11%)
  other arithmetic  1.69 us (3%)
  local copies, waits for them, and re-layouts  0.9 us (2%)
    ppermute x9, starting transfers between devices, swap(): return [lax.ppermute(state, 'seq', pair) for pair in pairs]  16.6 us
    ppermute x9, waiting for transfers between devices, swap(): return [lax.ppermute(state, 'seq', pair) for pair in pairs]  11.1 us
    pallas_call x8, Pallas kernels, kernel_call(): pl.pallas_call(body, out_shape=out_shape, in_specs=[pl.BlockSpec(memory_s...  5.67 us
    ppermute x1, waiting for transfers between devices, local(): own_away = lax.ppermute(away[:cut], 'ch', partner_pairs(4, 2))  4.3 us
    ppermute x2, starting transfers between devices, core_swap(): return lax.ppermute(one, 'ch', partner_pairs(4, 1))  3.27 us
    ppermute x1, starting transfers between devices, local(): lax.ppermute(away[cut:], ('seq', 'ch'), along_z(count, lambda z, low: (z...  2.46 us
    ppermute x1, waiting for transfers between devices, local(): lax.ppermute(away[cut:], ('seq', 'ch'), along_z(count, lambda z, low: (z...  1.82 us
    reshape x2, other arithmetic, tiles(): cut.transpose(0, 2, 1, 3).reshape(rows // 8, 8 * (columns // LANES), LANES)  1.37 us
  transfers between devices with their start and end apart: 14, of which 9 were waited for; matrix products, arithmetic and copies ran while one was open for 1% of the time, Pallas kernels for 5%

profile of v1, /device:TPU:1, one launch (start us, length us, event | category | flops | bytes accessed | tf_op | source)
XLA Modules:
  0.0 50.8 jit_solution(2475933769930082140)
XLA Ops:
  0.0 1.3 %multiply_bitcast_fusion.signal_ref = f32[16,64,128]{2,1,0:T(8,128)S(1)} fusion(f32[128,1024]{1,0:T(8,128)} %param.7, f32[128,1024]{1,0:T(8,128)} %param.6), kind=kLoop, calls=%fused_computation | loop fusion | flops 131072 | bytes 1572864 | tf_op jit(solution)/shard_map/reshape | solution.py:19
  1.3 0.0 copy-start.1
  1.3 0.8 %copy-done.1 = f32[16,1024]{1,0:T(8,128)S(1)} copy-done((f32[16,1024]{1,0:T(8,128)S(1)}, f32[16,1024]{1,0:T(8,128)}, u32[]{:S(2)}) %copy-start.1) | copy-done | bytes 65560
  2.2 0.8 %shard_map.66.refs_1_ = f32[2,64,128]{2,1,0:T(8,128)S(1)} custom-call(f32[16,64,128]{2,1,0:T(8,128)S(1)} %multiply_bitcast_fusion.signal_ref, f32[2,64,128]{2,1,0:T(8,128)S(1)} %bitcast.142), custom_call_target="tpu_custom_call" | custom-call | flops 2000000000 | bytes 600000 | tf_op jit(solution)/shard_map/pallas_call | solution.py:32
  3.0 7.8 %collective-permute-start.3 = (f32[2,64,128]{2,1,0:T(8,128)S(1)}, f32[2,64,128]{2,1,0:T(8,128)S(1)}, u32[]{:S(2)}, u32[]{:S(2)}) collective-permute-start(f32[2,64,128]{2,1,0:T(8,128)S(1)} %shard_map.66.refs_1_), channel_id=1, source_target_pairs={{0,8},{4,12},{8,0},{12,4},{16,24},{20,28},{24,16},{28,20},{32,40},... | collective-permute-start | bytes 196616 | tf_op jit(solution)/shard_map/ppermute | solution.py:229
  10.8 0.0 collective-permute-start.2
  10.8 1.2 %collective-permute-start.1 = (f32[2,64,128]{2,1,0:T(8,128)S(1)}, f32[2,64,128]{2,1,0:T(8,128)S(1)}, u32[]{:S(2)}, u32[]{:S(2)}) collective-permute-start(f32[2,64,128]{2,1,0:T(8,128)S(1)} %shard_map.66.refs_1_), channel_id=1, source_target_pairs={{0,4},{4,0},{8,12},{12,8},{16,20},{20,16},{24,28},{28,24},{32,36},... | collective-permute-start | bytes 196616 | tf_op jit(solution)/shard_map/ppermute | solution.py:229
  12.0 0.0 copy-done.3
  12.1 0.0 copy-done
  12.1 0.0 slice-start
  12.1 1.2 %shard_map.64 = (f32[16,64,128]{2,1,0:T(8,128)S(1)}, f32[2,8,64,128]{3,2,1,0:T(8,128)S(1)}) custom-call(f32[16,64,128]{2,1,0:T(8,128)S(1)} %multiply_bitcast_fusion.signal_ref, f32[2,64,128]{2,1,0:T(8,128)S(1)} %bitcast.143, f32[2,64,128]{2,1,0:T(8,128)S(1)} %multiply_bitcast_fusion.1.gain_ref.refs_1_, f32[16,64,128]{2,1,0:T(8,128)S(1)} %bitcast.140), custom_call_target="tpu_custom_call" | custom-call | flops 3000000000 | bytes 1500000 | tf_op jit(solution)/shard_map/pallas_call | solution.py:32
  13.3 0.0 slice-start.1
  13.3 1.2 %collective-permute-start = (f32[2,8,64,128]{3,2,1,0:T(8,128)S(1)}, f32[2,8,64,128]{3,2,1,0:T(8,128)S(1)}, u32[]{:S(2)}, u32[]{:S(2)}) collective-permute-start(f32[2,8,64,128]{3,2,1,0:T(8,128)S(1)} %get-tuple-element.22), channel_id=1, source_target_pairs={{0,4},{1,5},{2,14},{3,15},{4,8},{5,9},{6,2},{7,3},{8,12},{9,13},{1... | collective-permute-start | bytes 1572872 | tf_op jit(solution)/shard_map/ppermute | solution.py:274
  14.6 0.0 copy-done.2
  14.6 0.1 shard_map.68
  14.7 0.1 shard_map.67
  14.8 0.0 collective-permute-done.3
  14.8 1.3 %collective-permute-done.2 = f32[2,64,128]{2,1,0:T(8,128)S(1)} collective-permute-done((f32[2,64,128]{2,1,0:T(8,128)S(1)}, f32[2,64,128]{2,1,0:T(8,128)S(1)}, u32[]{:S(2)}, u32[]{:S(2)}) %collective-permute-start.2) | collective-permute-done | bytes 65568 | tf_op jit(solution)/shard_map/ppermute | solution.py:229
  16.1 2.1 %collective-permute-done.1 = f32[2,64,128]{2,1,0:T(8,128)S(1)} collective-permute-done((f32[2,64,128]{2,1,0:T(8,128)S(1)}, f32[2,64,128]{2,1,0:T(8,128)S(1)}, u32[]{:S(2)}, u32[]{:S(2)}) %collective-permute-start.1) | collective-permute-done | bytes 65568 | tf_op jit(solution)/shard_map/ppermute | solution.py:229
  18.3 3.0 %collective-permute-start.6 = (f32[2,64,128]{2,1,0:T(8,128)S(1)}, f32[2,64,128]{2,1,0:T(8,128)S(1)}, u32[]{:S(2)}, u32[]{:S(2)}) collective-permute-start(f32[2,64,128]{2,1,0:T(8,128)S(1)} %fusion.18), channel_id=1, source_target_pairs={{0,32},{4,36},{8,40},{12,44},{16,48},{20,52},{24,56},{28,60},{32,0... | collective-permute-start | bytes 196616 | tf_op jit(solution)/shard_map/ppermute | solution.py:229
  21.3 0.2 shard_map.65
  21.5 0.9 %collective-permute-start.5 = (f32[2,64,128]{2,1,0:T(8,128)S(1)}, f32[2,64,128]{2,1,0:T(8,128)S(1)}, u32[]{:S(2)}, u32[]{:S(2)}) collective-permute-start(f32[2,64,128]{2,1,0:T(8,128)S(1)} %fusion.18), channel_id=1, source_target_pairs={{0,48},{4,52},{8,56},{12,60},{16,32},{20,36},{24,40},{28,44},{32,1... | collective-permute-start | bytes 196616 | tf_op jit(solution)/shard_map/ppermute | solution.py:229
  22.3 0.0 collective-permute-start.4
  22.3 1.0 %collective-permute-done.6 = f32[2,64,128]{2,1,0:T(8,128)S(1)} collective-permute-done((f32[2,64,128]{2,1,0:T(8,128)S(1)}, f32[2,64,128]{2,1,0:T(8,128)S(1)}, u32[]{:S(2)}, u32[]{:S(2)}) %collective-permute-start.6) | collective-permute-done | bytes 65568 | tf_op jit(solution)/shard_map/ppermute | solution.py:229
  23.3 2.9 %collective-permute-done.5 = f32[2,64,128]{2,1,0:T(8,128)S(1)} collective-permute-done((f32[2,64,128]{2,1,0:T(8,128)S(1)}, f32[2,64,128]{2,1,0:T(8,128)S(1)}, u32[]{:S(2)}, u32[]{:S(2)}) %collective-permute-start.5) | collective-permute-done | bytes 65568 | tf_op jit(solution)/shard_map/ppermute | solution.py:229
  26.2 0.0 collective-permute-done.4
  26.2 0.1 fusion.12
  26.3 2.8 %collective-permute-start.9 = (f32[2,64,128]{2,1,0:T(8,128)S(1)}, f32[2,64,128]{2,1,0:T(8,128)S(1)}, u32[]{:S(2)}, u32[]{:S(2)}) collective-permute-start(f32[2,64,128]{2,1,0:T(8,128)S(1)} %get-tuple-element.39), channel_id=1, source_target_pairs={{0,128},{4,132},{8,136},{12,140},{16,144},{20,148},{24,152},{28,15... | collective-permute-start | bytes 196616 | tf_op jit(solution)/shard_map/ppermute | solution.py:229
  29.1 0.9 %collective-permute-start.8 = (f32[2,64,128]{2,1,0:T(8,128)S(1)}, f32[2,64,128]{2,1,0:T(8,128)S(1)}, u32[]{:S(2)}, u32[]{:S(2)}) collective-permute-start(f32[2,64,128]{2,1,0:T(8,128)S(1)} %get-tuple-element.39), channel_id=1, source_target_pairs={{0,192},{4,196},{8,200},{12,204},{16,208},{20,212},{24,216},{28,22... | collective-permute-start | bytes 196616 | tf_op jit(solution)/shard_map/ppermute | solution.py:229
  30.0 0.0 collective-permute-start.7
  30.0 1.0 %collective-permute-done.9.refs_11_ = f32[2,64,128]{2,1,0:T(8,128)S(1)} collective-permute-done((f32[2,64,128]{2,1,0:T(8,128)S(1)}, f32[2,64,128]{2,1,0:T(8,128)S(1)}, u32[]{:S(2)}, u32[]{:S(2)}) %collective-permute-start.9) | collective-permute-done | bytes 65568 | tf_op jit(solution)/shard_map/ppermute | solution.py:229
  31.0 2.9 %collective-permute-done.8.refs_10_ = f32[2,64,128]{2,1,0:T(8,128)S(1)} collective-permute-done((f32[2,64,128]{2,1,0:T(8,128)S(1)}, f32[2,64,128]{2,1,0:T(8,128)S(1)}, u32[]{:S(2)}, u32[]{:S(2)}) %collective-permute-start.8) | collective-permute-done | bytes 65568 | tf_op jit(solution)/shard_map/ppermute | solution.py:229
  33.9 0.0 collective-permute-done.7.refs_9_
  33.9 0.0 collective-permute-done.refs_2_
  33.9 0.0 slice-done
  33.9 1.5 %shard_map.69 = (bf16[192,1024]{1,0:T(8,128)(2,1)S(1)}, f32[128,1024]{1,0:T(8,128)S(1)}) custom-call(f32[16,64,128]{2,1,0:T(8,128)S(1)} %bitcast.141, f32[16,64,128]{2,1,0:T(8,128)S(1)} %get-tuple-element.21.refs_1_, f32[2,8,64,128]{3,2,1,0:T(8,128)S(1)} %collective-permute-done.refs_2_, f32[16,64,128]{2,1,0:T(8,128)S(1)} %get-tuple-element.23.refs_3_, ...), custom_call_target="tpu_custom_call" | custom-call | flops 2000000000 | bytes 3000000 | tf_op jit(solution)/shard_map/pallas_call | solution.py:32
  35.4 2.8 %collective-permute-start.10 = (f32[128,1024]{1,0:T(8,128)S(1)}, f32[128,1024]{1,0:T(8,128)S(1)}, u32[]{:S(2)}, u32[]{:S(2)}) collective-permute-start(f32[128,1024]{1,0:T(8,128)S(1)} %get-tuple-element.33), channel_id=1, source_target_pairs={{0,1},{1,0},{2,3},{3,2},{4,5},{5,4},{6,7},{7,6},{8,9},{9,8},{10,11... | collective-permute-start | bytes 1572872 | tf_op jit(solution)/shard_map/ppermute | solution.py:312
  38.2 1.0 %shard_map.70 = (f32[128,1024]{1,0:T(8,128)S(1)}, f32[128,1024]{1,0:T(8,128)S(1)}, f32[128,1024]{1,0:T(8,128)S(1)}) custom-call(bf16[192,1024]{1,0:T(8,128)(2,1)S(1)} %get-tuple-element.30.gated_ref, bf16[1024,4096]{1,0:T(8,128)(2,1)S(1)} %bitcast.139), custom_call_target="tpu_custom_call" | custom-call | flops 1500000000 | bytes 2000000 | tf_op jit(solution)/shard_map/pallas_call | solution.py:32
  39.2 0.5 %collective-permute-done.10 = f32[128,1024]{1,0:T(8,128)S(1)} collective-permute-done((f32[128,1024]{1,0:T(8,128)S(1)}, f32[128,1024]{1,0:T(8,128)S(1)}, u32[]{:S(2)}, u32[]{:S(2)}) %collective-permute-start.10) | collective-permute-done | bytes 524320 | tf_op jit(solution)/shard_map/ppermute | solution.py:312
  39.8 0.1 add.66
  39.9 0.5 collective-permute-start.11
  40.4 1.0 %collective-permute-start.13 = (f32[64,1024]{1,0:T(8,128)S(1)}, f32[64,1024]{1,0:T(8,128)S(1)}, u32[]{:S(2)}, u32[]{:S(2)}) collective-permute-start(f32[64,1024]{1,0:T(8,128)S(1)} %get-tuple-element.40), channel_id=1, source_target_pairs={{0,2},{1,3},{2,0},{3,1},{4,6},{5,7},{6,4},{7,5},{8,10},{9,11},{10,... | collective-permute-start | bytes 786440 | tf_op jit(solution)/shard_map/ppermute | solution.py:322
  41.4 2.5 %collective-permute-start.12 = (f32[64,1024]{1,0:T(8,128)S(1)}, f32[64,1024]{1,0:T(8,128)S(1)}, u32[]{:S(2)}, u32[]{:S(2)}) collective-permute-start(f32[64,1024]{1,0:T(8,128)S(1)} %get-tuple-element.41), channel_id=1, source_target_pairs={{0,14},{1,15},{2,4},{3,5},{4,2},{5,3},{6,8},{7,9},{8,6},{9,7},{10,... | collective-permute-start | bytes 786440 | tf_op jit(solution)/shard_map/ppermute | solution.py:317
  43.8 0.0 collective-permute-done.11
  43.8 0.1 add.67.home_ref
  43.9 4.3 %collective-permute-done.13.own_ref = f32[64,1024]{1,0:T(8,128)S(1)} collective-permute-done((f32[64,1024]{1,0:T(8,128)S(1)}, f32[64,1024]{1,0:T(8,128)S(1)}, u32[]{:S(2)}, u32[]{:S(2)}) %collective-permute-start.13) | collective-permute-done | bytes 262176 | tf_op jit(solution)/shard_map/ppermute | solution.py:322
  48.2 1.8 %collective-permute-done.12.helped_ref = f32[64,1024]{1,0:T(8,128)S(1)} collective-permute-done((f32[64,1024]{1,0:T(8,128)S(1)}, f32[64,1024]{1,0:T(8,128)S(1)}, u32[]{:S(2)}, u32[]{:S(2)}) %collective-permute-start.12) | collective-permute-done | bytes 262176 | tf_op jit(solution)/shard_map/ppermute | solution.py:317
  50.0 0.8 %shard_map.71 = bf16[128,1024]{1,0:T(8,128)(2,1)} custom-call(f32[128,1024]{1,0:T(8,128)S(1)} %add.67.home_ref, f32[64,1024]{1,0:T(8,128)S(1)} %collective-permute-done.12.helped_ref, f32[64,1024]{1,0:T(8,128)S(1)} %collective-permute-done.13.own_ref), custom_call_target="tpu_custom_call" | custom-call | flops 1000000 | bytes 2000000 | tf_op jit(solution)/shard_map/pallas_call | solution.py:32
  (11 shorter events, 0.2 us)
Async XLA Ops:
  0.0 12.0 %copy-start.3 = (f32[16,1024]{1,0:T(8,128)S(1)}, f32[16,1024]{1,0:T(8,128)}, u32[]{:S(2)}) copy-start(f32[16,1024]{1,0:T(8,128)} %param.9) | copy-start | bytes 196612
  0.0 12.0 %copy-start = (f32[128,1024]{1,0:T(8,128)S(1)}, f32[128,1024]{1,0:T(8,128)}, u32[]{:S(2)}) copy-start(f32[128,1024]{1,0:T(8,128)} %param.8) | copy-start | bytes 1572868
  1.3 0.8 %copy-start.1 = (f32[16,1024]{1,0:T(8,128)S(1)}, f32[16,1024]{1,0:T(8,128)}, u32[]{:S(2)}) copy-start(f32[16,1024]{1,0:T(8,128)} %param.10) | copy-start | bytes 196612
  2.2 12.4 %copy-start.2 = (f32[16,1024]{1,0:T(8,128)S(1)}, f32[16,1024]{1,0:T(8,128)}, u32[]{:S(2)}) copy-start(f32[16,1024]{1,0:T(8,128)} %param.10) | copy-start | bytes 196612
  3.0 11.8 %collective-permute-start.3 = (f32[2,64,128]{2,1,0:T(8,128)S(1)}, f32[2,64,128]{2,1,0:T(8,128)S(1)}, u32[]{:S(2)}, u32[]{:S(2)}) collective-permute-start(f32[2,64,128]{2,1,0:T(8,128)S(1)} %shard_map.66.refs_1_), channel_id=1, source_target_pairs={{0,8},{4,12},{8,0},{12,4},{16,24},{20,28},{24,16},{28,20},{32,40},... | collective-permute-start | bytes 196616 | tf_op jit(solution)/shard_map/ppermute | solution.py:229
  10.8 5.3 %collective-permute-start.2 = (f32[2,64,128]{2,1,0:T(8,128)S(1)}, f32[2,64,128]{2,1,0:T(8,128)S(1)}, u32[]{:S(2)}, u32[]{:S(2)}) collective-permute-start(f32[2,64,128]{2,1,0:T(8,128)S(1)} %shard_map.66.refs_1_), channel_id=1, source_target_pairs={{0,12},{4,8},{8,4},{12,0},{16,28},{20,24},{24,20},{28,16},{32,44},... | collective-permute-start | bytes 196616 | tf_op jit(solution)/shard_map/ppermute | solution.py:229
  10.8 7.5 %collective-permute-start.1 = (f32[2,64,128]{2,1,0:T(8,128)S(1)}, f32[2,64,128]{2,1,0:T(8,128)S(1)}, u32[]{:S(2)}, u32[]{:S(2)}) collective-permute-start(f32[2,64,128]{2,1,0:T(8,128)S(1)} %shard_map.66.refs_1_), channel_id=1, source_target_pairs={{0,4},{4,0},{8,12},{12,8},{16,20},{20,16},{24,28},{28,24},{32,36},... | collective-permute-start | bytes 196616 | tf_op jit(solution)/shard_map/ppermute | solution.py:229
  12.1 21.8 %slice-start = ((s8[8388608]{0:T(1024)(128)(4,1)}), s8[4194304]{0:T(1024)(128)(4,1)S(1)}, s32[]{:S(2)}) async-start(s8[8388608]{0:T(1024)(128)(4,1)} %bitcast.138), calls=%async_computation | async-start | bytes 8388608
  13.3 20.6 %slice-start.1 = ((s8[8388608]{0:T(1024)(128)(4,1)}), s8[4194304]{0:T(1024)(128)(4,1)S(1)}, s32[]{:S(2)}) async-start(s8[8388608]{0:T(1024)(128)(4,1)} %bitcast.138), calls=%async_computation.1 | async-start | bytes 8388608
  13.3 20.5 %collective-permute-start = (f32[2,8,64,128]{3,2,1,0:T(8,128)S(1)}, f32[2,8,64,128]{3,2,1,0:T(8,128)S(1)}, u32[]{:S(2)}, u32[]{:S(2)}) collective-permute-start(f32[2,8,64,128]{3,2,1,0:T(8,128)S(1)} %get-tuple-element.22), channel_id=1, source_target_pairs={{0,4},{1,5},{2,14},{3,15},{4,8},{5,9},{6,2},{7,3},{8,12},{9,13},{1... | collective-permute-start | bytes 1572872 | tf_op jit(solution)/shard_map/ppermute | solution.py:274
  18.3 5.0 %collective-permute-start.6 = (f32[2,64,128]{2,1,0:T(8,128)S(1)}, f32[2,64,128]{2,1,0:T(8,128)S(1)}, u32[]{:S(2)}, u32[]{:S(2)}) collective-permute-start(f32[2,64,128]{2,1,0:T(8,128)S(1)} %fusion.18), channel_id=1, source_target_pairs={{0,32},{4,36},{8,40},{12,44},{16,48},{20,52},{24,56},{28,60},{32,0... | collective-permute-start | bytes 196616 | tf_op jit(solution)/shard_map/ppermute | solution.py:229
  21.5 4.7 %collective-permute-start.5 = (f32[2,64,128]{2,1,0:T(8,128)S(1)}, f32[2,64,128]{2,1,0:T(8,128)S(1)}, u32[]{:S(2)}, u32[]{:S(2)}) collective-permute-start(f32[2,64,128]{2,1,0:T(8,128)S(1)} %fusion.18), channel_id=1, source_target_pairs={{0,48},{4,52},{8,56},{12,60},{16,32},{20,36},{24,40},{28,44},{32,1... | collective-permute-start | bytes 196616 | tf_op jit(solution)/shard_map/ppermute | solution.py:229
  22.3 3.8 %collective-permute-start.4 = (f32[2,64,128]{2,1,0:T(8,128)S(1)}, f32[2,64,128]{2,1,0:T(8,128)S(1)}, u32[]{:S(2)}, u32[]{:S(2)}) collective-permute-start(f32[2,64,128]{2,1,0:T(8,128)S(1)} %fusion.18), channel_id=1, source_target_pairs={{0,16},{4,20},{8,24},{12,28},{16,0},{20,4},{24,8},{28,12},{32,48},... | collective-permute-start | bytes 196616 | tf_op jit(solution)/shard_map/ppermute | solution.py:229
  26.3 4.7 %collective-permute-start.9 = (f32[2,64,128]{2,1,0:T(8,128)S(1)}, f32[2,64,128]{2,1,0:T(8,128)S(1)}, u32[]{:S(2)}, u32[]{:S(2)}) collective-permute-start(f32[2,64,128]{2,1,0:T(8,128)S(1)} %get-tuple-element.39), channel_id=1, source_target_pairs={{0,128},{4,132},{8,136},{12,140},{16,144},{20,148},{24,152},{28,15... | collective-permute-start | bytes 196616 | tf_op jit(solution)/shard_map/ppermute | solution.py:229
  29.1 4.8 %collective-permute-start.8 = (f32[2,64,128]{2,1,0:T(8,128)S(1)}, f32[2,64,128]{2,1,0:T(8,128)S(1)}, u32[]{:S(2)}, u32[]{:S(2)}) collective-permute-start(f32[2,64,128]{2,1,0:T(8,128)S(1)} %get-tuple-element.39), channel_id=1, source_target_pairs={{0,192},{4,196},{8,200},{12,204},{16,208},{20,212},{24,216},{28,22... | collective-permute-start | bytes 196616 | tf_op jit(solution)/shard_map/ppermute | solution.py:229
  30.0 3.9 %collective-permute-start.7 = (f32[2,64,128]{2,1,0:T(8,128)S(1)}, f32[2,64,128]{2,1,0:T(8,128)S(1)}, u32[]{:S(2)}, u32[]{:S(2)}) collective-permute-start(f32[2,64,128]{2,1,0:T(8,128)S(1)} %get-tuple-element.39), channel_id=1, source_target_pairs={{0,64},{4,68},{8,72},{12,76},{16,80},{20,84},{24,88},{28,92},{32,9... | collective-permute-start | bytes 196616 | tf_op jit(solution)/shard_map/ppermute | solution.py:229
  35.4 4.3 %collective-permute-start.10 = (f32[128,1024]{1,0:T(8,128)S(1)}, f32[128,1024]{1,0:T(8,128)S(1)}, u32[]{:S(2)}, u32[]{:S(2)}) collective-permute-start(f32[128,1024]{1,0:T(8,128)S(1)} %get-tuple-element.33), channel_id=1, source_target_pairs={{0,1},{1,0},{2,3},{3,2},{4,5},{5,4},{6,7},{7,6},{8,9},{9,8},{10,11... | collective-permute-start | bytes 1572872 | tf_op jit(solution)/shard_map/ppermute | solution.py:312
  39.9 4.0 %collective-permute-start.11 = (f32[128,1024]{1,0:T(8,128)S(1)}, f32[128,1024]{1,0:T(8,128)S(1)}, u32[]{:S(2)}, u32[]{:S(2)}) collective-permute-start(f32[128,1024]{1,0:T(8,128)S(1)} %get-tuple-element.35), channel_id=1, source_target_pairs={{0,1},{1,0},{2,3},{3,2},{4,5},{5,4},{6,7},{7,6},{8,9},{9,8},{10,11... | collective-permute-start | bytes 1572872 | tf_op jit(solution)/shard_map/ppermute | solution.py:312
  40.4 7.9 %collective-permute-start.13 = (f32[64,1024]{1,0:T(8,128)S(1)}, f32[64,1024]{1,0:T(8,128)S(1)}, u32[]{:S(2)}, u32[]{:S(2)}) collective-permute-start(f32[64,1024]{1,0:T(8,128)S(1)} %get-tuple-element.40), channel_id=1, source_target_pairs={{0,2},{1,3},{2,0},{3,1},{4,6},{5,7},{6,4},{7,5},{8,10},{9,11},{10,... | collective-permute-start | bytes 786440 | tf_op jit(solution)/shard_map/ppermute | solution.py:322
  41.4 8.7 %collective-permute-start.12 = (f32[64,1024]{1,0:T(8,128)S(1)}, f32[64,1024]{1,0:T(8,128)S(1)}, u32[]{:S(2)}, u32[]{:S(2)}) collective-permute-start(f32[64,1024]{1,0:T(8,128)S(1)} %get-tuple-element.41), channel_id=1, source_target_pairs={{0,14},{1,15},{2,4},{3,5},{4,2},{5,3},{6,8},{7,9},{8,6},{9,7},{10,... | collective-permute-start | bytes 786440 | tf_op jit(solution)/shard_map/ppermute | solution.py:317

commit v2 on v1

--- a/solution.py
+++ b/solution.py
@@ -40,7 +40,13 @@
     )(*inputs)
 
 
-def end_state_kernel(signal_ref, damping_ref, state_ref):
+def split(stacked_ref):
+    outer = stacked_ref.shape[0] - HALVES
+    return stacked_ref.at[pl.ds(0, outer)], stacked_ref.at[pl.ds(outer, HALVES)]
+
+
+def end_state_kernel(stacked_ref, state_ref):
+    signal_ref, damping_ref = split(stacked_ref)
     outer, lanes = signal_ref.shape[0], signal_ref.shape[1] // 8
     place = lax.broadcasted_iota(jnp.int32, (8, LANES), 0)
     for g in range(lanes):
@@ -66,7 +72,9 @@
             state_ref[half, block, :] = result
 
 
-def local_kernel(signal_ref, damping_ref, gain_ref, query_ref, out_ref, handed_ref):
+def local_kernel(stacked_ref, gain_ref, query_ref, out_ref, handed_ref):
+    signal_ref, damping_ref = split(stacked_ref)
+
     def row(ref, outer, inner):
         return ref[outer, pl.ds(inner, 8, stride=8), :]
 
@@ -105,9 +113,9 @@
     return jnp.exp(damping * ahead) * before
 
 
-def run_kernel(axis, rows, damping_ref, out_ref):
+def run_kernel(axis, rows, stacked_ref, out_ref):
     here = places()[axis]
-    damping = damping_ref[...] * (-1.0 * rows * 4**axis)
+    damping = split(stacked_ref)[1][...] * (-1.0 * rows * 4**axis)
     for n, step in enumerate((0, *STEPS)):
         there = here ^ step
         out_ref[n] = jnp.exp(damping * (3 - there).astype(jnp.float32))
@@ -117,13 +125,14 @@
             out_ref[7 + n] = entry_decay(damping, helped(here), there)
 
 
-def run_own(axis, rows, damping_ref, state_ref, out_ref, own_ref):
-    run_kernel(axis, rows, damping_ref, out_ref)
+def run_own(axis, rows, stacked_ref, state_ref, out_ref, own_ref):
+    run_kernel(axis, rows, stacked_ref, out_ref)
     own_ref[...] = out_ref[0] * state_ref[...]
 
 
-def last_kernel(rows, damping_ref, gain_ref, out_ref, scale_ref, eight_ref, powers_ref):
+def last_kernel(rows, stacked_ref, gain_ref, out_ref, scale_ref, eight_ref, powers_ref):
     z, y, x = places()
+    damping_ref = split(stacked_ref)[1]
     damping, gain = damping_ref[...], gain_ref[...]
     scale_ref[0] = gain
     for n, target in enumerate((z, helped(z))):
@@ -150,15 +159,18 @@
     )
 
 
-def project_away(gated_ref, weight_ref, group, out_ref):
-    skipped = gated_ref.shape[0] - out_ref.shape[0]
-    out_ref[...] = project(gated_ref[skipped:, :], weight_ref, group)
+def project_away(gated_ref, weight_ref, group, own_ref, helped_ref):
+    rows = own_ref.shape[0] + helped_ref.shape[0]
+    skipped = gated_ref.shape[0] - rows
+    result = project(gated_ref[skipped:, :], weight_ref, group)
+    own_ref[...] = result[: own_ref.shape[0]]
+    helped_ref[...] = result[own_ref.shape[0] :]
 
 
 def gate_kernel(*refs):
     query_ref, local_ref, handed_ref, powers_ref, eight_ref = refs[:5]
     bases, scale_ref, last_ref, arrived, weight_ref = refs[5:7], *refs[7:9], refs[9:12], refs[12]
-    gated_ref, sent_ref, state_ref = refs[13:]
+    gated_ref, own_ref, helped_ref, state_ref = refs[13:]
     far = sum(last_ref[n] * arrived[n][...] for n in range(3))
     for n in range(2):
         state_ref[n] = bases[n][...] + scale_ref[1 + n] * far
@@ -188,20 +200,21 @@
         return carry
 
     lax.fori_loop(0, query_ref.shape[1] // 8, body, 0)
-    project_away(gated_ref, weight_ref, 3, sent_ref)
-
-
-def rest_kernel(gated_ref, weight_ref, kept_ref, sent_ref, home_ref):
-    project_away(gated_ref, weight_ref, 2, kept_ref)
+    project_away(gated_ref, weight_ref, 3, own_ref, helped_ref)
+
+
+def rest_kernel(gated_ref, weight_ref, own_ref, helped_ref, sent_ref, home_ref):
+    project_away(gated_ref, weight_ref, 2, own_ref, helped_ref)
     rows = home_ref.shape[0]
     sent_ref[...] = project(gated_ref[:rows, :], weight_ref, 1)
     home_ref[...] = project(gated_ref[:rows, :], weight_ref, 0)
 
 
-def finish_kernel(home_ref, helped_ref, own_ref, out_ref):
+def finish_kernel(home_ref, helped_ref, own_ref, core_ref, out_ref):
     count = helped_ref.shape[0]
-    out_ref[:count, :] = (home_ref[:count, :] + helped_ref[...]).astype(jnp.bfloat16)
-    out_ref[count:, :] = (home_ref[count:, :] + own_ref[...]).astype(jnp.bfloat16)
+    for part, away_ref in ((pl.ds(0, count), helped_ref), (pl.ds(count, own_ref.shape[0]), own_ref)):
+        total = core_ref[part, :] + home_ref[part, :] + away_ref[...]
+        out_ref[part, :] = total.astype(jnp.bfloat16)
 
 
 def partner_pairs(size, step):
@@ -220,9 +233,11 @@
     rows, channels = value_rows.shape
     count = lax.axis_size("seq")
     queries = tiles(query_rows)
-    damping = tiles(damping_speeds)
+    more, below = ((0, MODES, 0), (0, 0, 0)), ((rows, 0, 0), (0, 0, 0))
+    keys, values = (lax.pad(one, 0.0, more) for one in (key_rows, value_rows))
+    stacked = tiles(keys * values + lax.pad(damping_speeds, 0.0, below))
     gain = tiles(pole_weights * jnp.sqrt(-jnp.expm1(-2.0 * damping_speeds)))
-    shape = damping.shape
+    shape = gain.shape
 
     def swap(state, axis):
         pairs = [partner_pairs(count, step * 4**axis) for step in STEPS]
@@ -236,35 +251,34 @@
     def weighed(decays, first, terms):
         return sum(decays[first + n] * term for n, term in enumerate(terms))
 
-    signal = tiles(key_rows * value_rows)
     state = kernel_call(
-        end_state_kernel, f32(*shape), (signal, damping), 2_000_000_000, 600_000
+        end_state_kernel, f32(*shape), (stacked,), 2_000_000_000, 600_000
     )
     decays_z, own_z = kernel_call(
         lambda *refs: run_own(0, rows, *refs),
         (f32(11, *shape), f32(*shape)),
-        (damping, state),
+        (stacked, state),
         1_000_000_000,
         800_000,
     )
     decays_y = kernel_call(
         lambda *refs: run_kernel(1, rows, *refs),
         f32(7, *shape),
-        (damping,),
+        (stacked,),
         1_000_000_000,
         600_000,
     )
     near, handed = kernel_call(
         local_kernel,
-        (f32(*signal.shape), f32(2, HANDED, *signal.shape[1:])),
-        (signal, damping, gain, queries),
+        (f32(*queries.shape), f32(2, HANDED, *queries.shape[1:])),
+        (stacked, gain, queries),
         3_000_000_000,
         1_500_000,
     )
     last, scale, eight, powers = kernel_call(
         lambda *refs: last_kernel(rows, *refs),
         (f32(3, *shape), f32(3, *shape), f32(*shape), f32(MODES, *shape[1:])),
-        (damping, gain),
+        (stacked, gain),
         1_000_000_000,
         1_000_000,
     )
@@ -285,9 +299,10 @@
 
     width = out_weight.shape[1] // lax.axis_size("ch")
     whole = f32(rows, width)
-    gated, sent = kernel_call(
+    away = (f32(rows - 8 * HANDED, width), f32(8 * HANDED, width))
+    gated, own_sent, helped_sent = kernel_call(
         gate_kernel,
-        (jax.ShapeDtypeStruct((rows + 8 * HANDED, channels), jnp.bfloat16), whole),
+        (jax.ShapeDtypeStruct((rows + 8 * HANDED, channels), jnp.bfloat16), *away),
         (
             queries,
             near,
@@ -304,27 +319,26 @@
         3_000_000,
         (pltpu.VMEM((2, *shape), jnp.float32),),
     )
-    kept, home_sent, home_kept = kernel_call(
-        rest_kernel, (whole,) * 3, (gated, out_weight), 1_500_000_000, 2_000_000
+    own_kept, helped_kept, home_sent, home_kept = kernel_call(
+        rest_kernel, (*away, whole, whole), (gated, out_weight), 1_000_000, 10_000
     )
 
     def core_swap(one):
         return lax.ppermute(one, "ch", partner_pairs(4, 1))
 
-    away = kept + core_swap(sent)
-    away, home_sent = lax.optimization_barrier((away, home_sent))
-    cut = rows - 8 * HANDED
+    own_away = own_kept + core_swap(own_sent)
+    own_away, home_sent = lax.optimization_barrier((own_away, home_sent))
+    helped_away = helped_kept + core_swap(helped_sent)
     helped_away = lax.ppermute(
-        away[cut:],
+        helped_away,
         ("seq", "ch"),
         along_z(count, lambda z, low: (z - 1 + 2 * low, 1 - low)),
     )
-    own_away = lax.ppermute(away[:cut], "ch", partner_pairs(4, 2))
-    home = home_kept + core_swap(home_sent)
+    own_away = lax.ppermute(own_away, "ch", partner_pairs(4, 2))
     return kernel_call(
         finish_kernel,
         jax.ShapeDtypeStruct((rows, width), jnp.bfloat16),
-        (home, helped_away, own_away),
+        (home_kept, helped_away, own_away, core_swap(home_sent)),
         1_000_000,
         2_000_000,
     )

time: 50.9 us -> 49.7 us (0.976)
  local copies, waits for them, and re-layouts: 0.9 us -> 0.03 us
    unnamed x12 -> x10, local copies, waits for them, and re-layouts: 0.86 us -> 0.03 us
    ppermute x2 -> x3, starting transfers between devices: 3.27 us -> 3.36 us  [core_swap(): return lax.ppermute(one, 'ch', partner_pairs(4, 1))]
  transfers between devices with their start and end apart: 14 -> 15, of which waited for: 9 -> 9; matrix products, arithmetic and copies ran while one was open for 1% -> 1% of each run, Pallas kernels for 5% -> 5%
where the time goes in v2:
time: 49.7 us; the launch traced here: 49.6 us
  starting transfers between devices  24.7 us (50%)
  waiting for transfers between devices  17.4 us (35%)
  Pallas kernels  5.68 us (11%)
  other arithmetic  1.65 us (3%)
    ppermute x9, starting transfers between devices, swap(): return [lax.ppermute(state, 'seq', pair) for pair in pairs]  16.6 us
    ppermute x9, waiting for transfers between devices, swap(): return [lax.ppermute(state, 'seq', pair) for pair in pairs]  11.1 us
    pallas_call x8, Pallas kernels, kernel_call(): pl.pallas_call(body, out_shape=out_shape, in_specs=[pl.BlockSpec(memory_s...  5.68 us
    ppermute x1, waiting for transfers between devices, local(): own_away = lax.ppermute(own_away, 'ch', partner_pairs(4, 2))  4.25 us
    ppermute x3, starting transfers between devices, core_swap(): return lax.ppermute(one, 'ch', partner_pairs(4, 1))  3.36 us
    ppermute x1, starting transfers between devices, local(): lax.ppermute(helped_away, ('seq', 'ch'), along_z(count, lambda z, low: (z...  2.54 us
    ppermute x1, waiting for transfers between devices, local(): lax.ppermute(helped_away, ('seq', 'ch'), along_z(count, lambda z, low: (z...  1.95 us
    reshape x2, other arithmetic, tiles(): cut.transpose(0, 2, 1, 3).reshape(rows // 8, 8 * (columns // LANES), LANES)  1.41 us
  transfers between devices with their start and end apart: 15, of which 9 were waited for; matrix products, arithmetic and copies ran while one was open for 1% of the time, Pallas kernels for 5%

profile of v2, /device:TPU:1, one launch (start us, length us, event | category | flops | bytes accessed | tf_op | source)
XLA Modules:
  0.0 49.6 jit_solution(17818183751118918911)
XLA Ops:
  0.0 0.0 copy-start.1
  0.0 1.4 %add_bitcast_fusion.stacked_ref.refs_0_ = f32[18,64,128]{2,1,0:T(8,128)S(1)} fusion(f32[16,1024]{1,0:T(8,128)} %param.10, f32[128,1024]{1,0:T(8,128)} %param.6, f32[128,1024]{1,0:T(8,128)} %param.7), kind=kLoop, calls=%fused_computation | loop fusion | flops 294912 | bytes 1703936 | tf_op jit(solution)/shard_map/reshape | solution.py:19
  1.4 0.8 %shard_map.66.refs_1_ = f32[2,64,128]{2,1,0:T(8,128)S(1)} custom-call(f32[18,64,128]{2,1,0:T(8,128)S(1)} %add_bitcast_fusion.stacked_ref.refs_0_), custom_call_target="tpu_custom_call" | custom-call | flops 2000000000 | bytes 600000 | tf_op jit(solution)/shard_map/pallas_call | solution.py:32
  2.2 7.8 %collective-permute-start.3 = (f32[2,64,128]{2,1,0:T(8,128)S(1)}, f32[2,64,128]{2,1,0:T(8,128)S(1)}, u32[]{:S(2)}, u32[]{:S(2)}) collective-permute-start(f32[2,64,128]{2,1,0:T(8,128)S(1)} %shard_map.66.refs_1_), channel_id=1, source_target_pairs={{0,8},{4,12},{8,0},{12,4},{16,24},{20,28},{24,16},{28,20},{32,40},... | collective-permute-start | bytes 196616 | tf_op jit(solution)/shard_map/ppermute | solution.py:244
  10.0 0.0 collective-permute-start.2
  10.0 1.2 %collective-permute-start.1 = (f32[2,64,128]{2,1,0:T(8,128)S(1)}, f32[2,64,128]{2,1,0:T(8,128)S(1)}, u32[]{:S(2)}, u32[]{:S(2)}) collective-permute-start(f32[2,64,128]{2,1,0:T(8,128)S(1)} %shard_map.66.refs_1_), channel_id=1, source_target_pairs={{0,4},{4,0},{8,12},{12,8},{16,20},{20,16},{24,28},{28,24},{32,36},... | collective-permute-start | bytes 196616 | tf_op jit(solution)/shard_map/ppermute | solution.py:244
  11.2 0.0 copy-done.1
  11.2 0.0 copy-done.2
  11.3 0.0 copy-done
  11.3 0.0 slice-start
  11.3 1.2 %shard_map.64 = (f32[16,64,128]{2,1,0:T(8,128)S(1)}, f32[2,8,64,128]{3,2,1,0:T(8,128)S(1)}) custom-call(f32[18,64,128]{2,1,0:T(8,128)S(1)} %add_bitcast_fusion.stacked_ref.refs_0_, f32[2,64,128]{2,1,0:T(8,128)S(1)} %multiply_bitcast_fusion.gain_ref.refs_1_, f32[16,64,128]{2,1,0:T(8,128)S(1)} %bitcast.135), custom_call_target="tpu_custom_call" | custom-call | flops 3000000000 | bytes 1500000 | tf_op jit(solution)/shard_map/pallas_call | solution.py:32
  12.5 0.0 slice-start.1
  12.5 1.2 %collective-permute-start = (f32[2,8,64,128]{3,2,1,0:T(8,128)S(1)}, f32[2,8,64,128]{3,2,1,0:T(8,128)S(1)}, u32[]{:S(2)}, u32[]{:S(2)}) collective-permute-start(f32[2,8,64,128]{3,2,1,0:T(8,128)S(1)} %get-tuple-element.24), channel_id=1, source_target_pairs={{0,4},{1,5},{2,14},{3,15},{4,8},{5,9},{6,2},{7,3},{8,12},{9,13},{1... | collective-permute-start | bytes 1572872 | tf_op jit(solution)/shard_map/ppermute | solution.py:288
  13.8 0.1 shard_map.68
  13.9 0.1 shard_map.67
  14.0 0.0 collective-permute-done.3
  14.0 1.3 %collective-permute-done.2 = f32[2,64,128]{2,1,0:T(8,128)S(1)} collective-permute-done((f32[2,64,128]{2,1,0:T(8,128)S(1)}, f32[2,64,128]{2,1,0:T(8,128)S(1)}, u32[]{:S(2)}, u32[]{:S(2)}) %collective-permute-start.2) | collective-permute-done | bytes 65568 | tf_op jit(solution)/shard_map/ppermute | solution.py:244
  15.3 2.1 %collective-permute-done.1 = f32[2,64,128]{2,1,0:T(8,128)S(1)} collective-permute-done((f32[2,64,128]{2,1,0:T(8,128)S(1)}, f32[2,64,128]{2,1,0:T(8,128)S(1)}, u32[]{:S(2)}, u32[]{:S(2)}) %collective-permute-start.1) | collective-permute-done | bytes 65568 | tf_op jit(solution)/shard_map/ppermute | solution.py:244
  17.5 3.0 %collective-permute-start.6 = (f32[2,64,128]{2,1,0:T(8,128)S(1)}, f32[2,64,128]{2,1,0:T(8,128)S(1)}, u32[]{:S(2)}, u32[]{:S(2)}) collective-permute-start(f32[2,64,128]{2,1,0:T(8,128)S(1)} %fusion.18), channel_id=1, source_target_pairs={{0,32},{4,36},{8,40},{12,44},{16,48},{20,52},{24,56},{28,60},{32,0... | collective-permute-start | bytes 196616 | tf_op jit(solution)/shard_map/ppermute | solution.py:244
  20.5 0.2 shard_map.65
  20.7 0.9 %collective-permute-start.5 = (f32[2,64,128]{2,1,0:T(8,128)S(1)}, f32[2,64,128]{2,1,0:T(8,128)S(1)}, u32[]{:S(2)}, u32[]{:S(2)}) collective-permute-start(f32[2,64,128]{2,1,0:T(8,128)S(1)} %fusion.18), channel_id=1, source_target_pairs={{0,48},{4,52},{8,56},{12,60},{16,32},{20,36},{24,40},{28,44},{32,1... | collective-permute-start | bytes 196616 | tf_op jit(solution)/shard_map/ppermute | solution.py:244
  21.5 0.0 collective-permute-start.4
  21.5 1.0 %collective-permute-done.6 = f32[2,64,128]{2,1,0:T(8,128)S(1)} collective-permute-done((f32[2,64,128]{2,1,0:T(8,128)S(1)}, f32[2,64,128]{2,1,0:T(8,128)S(1)}, u32[]{:S(2)}, u32[]{:S(2)}) %collective-permute-start.6) | collective-permute-done | bytes 65568 | tf_op jit(solution)/shard_map/ppermute | solution.py:244
  22.5 2.9 %collective-permute-done.5 = f32[2,64,128]{2,1,0:T(8,128)S(1)} collective-permute-done((f32[2,64,128]{2,1,0:T(8,128)S(1)}, f32[2,64,128]{2,1,0:T(8,128)S(1)}, u32[]{:S(2)}, u32[]{:S(2)}) %collective-permute-start.5) | collective-permute-done | bytes 65568 | tf_op jit(solution)/shard_map/ppermute | solution.py:244
  25.4 0.0 collective-permute-done.4
  25.4 0.1 fusion.12
  25.5 2.8 %collective-permute-start.9 = (f32[2,64,128]{2,1,0:T(8,128)S(1)}, f32[2,64,128]{2,1,0:T(8,128)S(1)}, u32[]{:S(2)}, u32[]{:S(2)}) collective-permute-start(f32[2,64,128]{2,1,0:T(8,128)S(1)} %get-tuple-element.43), channel_id=1, source_target_pairs={{0,128},{4,132},{8,136},{12,140},{16,144},{20,148},{24,152},{28,15... | collective-permute-start | bytes 196616 | tf_op jit(solution)/shard_map/ppermute | solution.py:244
  28.3 0.9 %collective-permute-start.8 = (f32[2,64,128]{2,1,0:T(8,128)S(1)}, f32[2,64,128]{2,1,0:T(8,128)S(1)}, u32[]{:S(2)}, u32[]{:S(2)}) collective-permute-start(f32[2,64,128]{2,1,0:T(8,128)S(1)} %get-tuple-element.43), channel_id=1, source_target_pairs={{0,192},{4,196},{8,200},{12,204},{16,208},{20,212},{24,216},{28,22... | collective-permute-start | bytes 196616 | tf_op jit(solution)/shard_map/ppermute | solution.py:244
  29.2 0.0 collective-permute-start.7
  29.2 1.0 %collective-permute-done.9.refs_11_ = f32[2,64,128]{2,1,0:T(8,128)S(1)} collective-permute-done((f32[2,64,128]{2,1,0:T(8,128)S(1)}, f32[2,64,128]{2,1,0:T(8,128)S(1)}, u32[]{:S(2)}, u32[]{:S(2)}) %collective-permute-start.9) | collective-permute-done | bytes 65568 | tf_op jit(solution)/shard_map/ppermute | solution.py:244
  30.2 2.9 %collective-permute-done.8.refs_10_ = f32[2,64,128]{2,1,0:T(8,128)S(1)} collective-permute-done((f32[2,64,128]{2,1,0:T(8,128)S(1)}, f32[2,64,128]{2,1,0:T(8,128)S(1)}, u32[]{:S(2)}, u32[]{:S(2)}) %collective-permute-start.8) | collective-permute-done | bytes 65568 | tf_op jit(solution)/shard_map/ppermute | solution.py:244
  33.1 0.0 collective-permute-done.7.refs_9_
  33.1 0.0 collective-permute-done.refs_2_
  33.1 0.0 slice-done
  33.1 0.0 slice-done.1
  33.1 1.5 %shard_map.69 = (bf16[192,1024]{1,0:T(8,128)(2,1)S(1)}, f32[64,1024]{1,0:T(8,128)S(1)}, f32[64,1024]{1,0:T(8,128)S(1)}) custom-call(f32[16,64,128]{2,1,0:T(8,128)S(1)} %bitcast.136, f32[16,64,128]{2,1,0:T(8,128)S(1)} %get-tuple-element.23.refs_1_, f32[2,8,64,128]{3,2,1,0:T(8,128)S(1)} %collective-permute-done.refs_2_, ...), custom_call_target="tpu_custom_call" | custom-call | flops 2000000000 | bytes 3000000 | tf_op jit(solution)/shard_map/pallas_call | solution.py:32
  34.6 2.8 %collective-permute-start.12 = (f32[64,1024]{1,0:T(8,128)S(1)}, f32[64,1024]{1,0:T(8,128)S(1)}, u32[]{:S(2)}, u32[]{:S(2)}) collective-permute-start(f32[64,1024]{1,0:T(8,128)S(1)} %get-tuple-element.37), channel_id=1, source_target_pairs={{0,1},{1,0},{2,3},{3,2},{4,5},{5,4},{6,7},{7,6},{8,9},{9,8},{10,11... | collective-permute-start | bytes 786440 | tf_op jit(solution)/shard_map/ppermute | solution.py:327
  37.4 0.1 collective-permute-start.10
  37.5 1.0 %shard_map.70 = (f32[64,1024]{1,0:T(8,128)S(1)}, f32[64,1024]{1,0:T(8,128)S(1)}, f32[128,1024]{1,0:T(8,128)S(1)}, f32[128,1024]{1,0:T(8,128)S(1)}) custom-call(bf16[192,1024]{1,0:T(8,128)(2,1)S(1)} %get-tuple-element.32.gated_ref, bf16[1024,4096]{1,0:T(8,128)(2,1)S(1)} %bitcast.134), custom_call_target="tpu_custom_call" | custom-call | flops 1000000 | bytes 10000 | tf_op jit(solution)/shard_map/pallas_call | solution.py:32
  38.5 0.1 collective-permute-done.12
  38.6 0.5 collective-permute-start.14
  39.1 0.9 %collective-permute-start.13 = (f32[64,1024]{1,0:T(8,128)S(1)}, f32[64,1024]{1,0:T(8,128)S(1)}, u32[]{:S(2)}, u32[]{:S(2)}) collective-permute-start(f32[64,1024]{1,0:T(8,128)S(1)} %add.77), channel_id=1, source_target_pairs={{0,2},{1,3},{2,0},{3,1},{4,6},{5,7},{6,4},{7,5},{8,10},{9,11},{10,... | collective-permute-start | bytes 786440 | tf_op jit(solution)/shard_map/ppermute | solution.py:337
  40.0 0.0 collective-permute-done.10
  40.1 2.5 %collective-permute-start.11 = (f32[64,1024]{1,0:T(8,128)S(1)}, f32[64,1024]{1,0:T(8,128)S(1)}, u32[]{:S(2)}, u32[]{:S(2)}) collective-permute-start(f32[64,1024]{1,0:T(8,128)S(1)} %add.76), channel_id=1, source_target_pairs={{0,14},{1,15},{2,4},{3,5},{4,2},{5,3},{6,8},{7,9},{8,6},{9,7},{10,... | collective-permute-start | bytes 786440 | tf_op jit(solution)/shard_map/ppermute | solution.py:332
  42.6 4.3 %collective-permute-done.13.own_ref = f32[64,1024]{1,0:T(8,128)S(1)} collective-permute-done((f32[64,1024]{1,0:T(8,128)S(1)}, f32[64,1024]{1,0:T(8,128)S(1)}, u32[]{:S(2)}, u32[]{:S(2)}) %collective-permute-start.13) | collective-permute-done | bytes 262176 | tf_op jit(solution)/shard_map/ppermute | solution.py:337
  46.8 1.9 %collective-permute-done.11.helped_ref = f32[64,1024]{1,0:T(8,128)S(1)} collective-permute-done((f32[64,1024]{1,0:T(8,128)S(1)}, f32[64,1024]{1,0:T(8,128)S(1)}, u32[]{:S(2)}, u32[]{:S(2)}) %collective-permute-start.11) | collective-permute-done | bytes 262176 | tf_op jit(solution)/shard_map/ppermute | solution.py:332
  48.8 0.0 collective-permute-done.14.core_ref
  48.8 0.8 %shard_map.71 = bf16[128,1024]{1,0:T(8,128)(2,1)} custom-call(f32[128,1024]{1,0:T(8,128)S(1)} %get-tuple-element.33.home_ref, f32[64,1024]{1,0:T(8,128)S(1)} %collective-permute-done.11.helped_ref, f32[64,1024]{1,0:T(8,128)S(1)} %collective-permute-done.13.own_ref, f32[128,1024]{1,0:T(8,128)S(1)} %collective-permute-done.14.core_ref), custom_call_target="tpu_custom_call" | custom-call | flops 1000000 | bytes 2000000 | tf_op jit(solution)/shard_map/pallas_call | solution.py:32
  (10 shorter events, 0.2 us)
Async XLA Ops:
  0.0 11.2 %copy-start.1 = (f32[16,1024]{1,0:T(8,128)S(1)}, f32[16,1024]{1,0:T(8,128)}, u32[]{:S(2)}) copy-start(f32[16,1024]{1,0:T(8,128)} %param.10) | copy-start | bytes 196612
  0.0 11.2 %copy-start.2 = (f32[16,1024]{1,0:T(8,128)S(1)}, f32[16,1024]{1,0:T(8,128)}, u32[]{:S(2)}) copy-start(f32[16,1024]{1,0:T(8,128)} %param.9) | copy-start | bytes 196612
  0.0 11.2 %copy-start = (f32[128,1024]{1,0:T(8,128)S(1)}, f32[128,1024]{1,0:T(8,128)}, u32[]{:S(2)}) copy-start(f32[128,1024]{1,0:T(8,128)} %param.8) | copy-start | bytes 1572868
  2.2 11.8 %collective-permute-start.3 = (f32[2,64,128]{2,1,0:T(8,128)S(1)}, f32[2,64,128]{2,1,0:T(8,128)S(1)}, u32[]{:S(2)}, u32[]{:S(2)}) collective-permute-start(f32[2,64,128]{2,1,0:T(8,128)S(1)} %shard_map.66.refs_1_), channel_id=1, source_target_pairs={{0,8},{4,12},{8,0},{12,4},{16,24},{20,28},{24,16},{28,20},{32,40},... | collective-permute-start | bytes 196616 | tf_op jit(solution)/shard_map/ppermute | solution.py:244
  10.0 5.3 %collective-permute-start.2 = (f32[2,64,128]{2,1,0:T(8,128)S(1)}, f32[2,64,128]{2,1,0:T(8,128)S(1)}, u32[]{:S(2)}, u32[]{:S(2)}) collective-permute-start(f32[2,64,128]{2,1,0:T(8,128)S(1)} %shard_map.66.refs_1_), channel_id=1, source_target_pairs={{0,12},{4,8},{8,4},{12,0},{16,28},{20,24},{24,20},{28,16},{32,44},... | collective-permute-start | bytes 196616 | tf_op jit(solution)/shard_map/ppermute | solution.py:244
  10.0 7.5 %collective-permute-start.1 = (f32[2,64,128]{2,1,0:T(8,128)S(1)}, f32[2,64,128]{2,1,0:T(8,128)S(1)}, u32[]{:S(2)}, u32[]{:S(2)}) collective-permute-start(f32[2,64,128]{2,1,0:T(8,128)S(1)} %shard_map.66.refs_1_), channel_id=1, source_target_pairs={{0,4},{4,0},{8,12},{12,8},{16,20},{20,16},{24,28},{28,24},{32,36},... | collective-permute-start | bytes 196616 | tf_op jit(solution)/shard_map/ppermute | solution.py:244
  11.3 21.8 %slice-start = ((s8[8388608]{0:T(1024)(128)(4,1)}), s8[4194304]{0:T(1024)(128)(4,1)S(1)}, s32[]{:S(2)}) async-start(s8[8388608]{0:T(1024)(128)(4,1)} %bitcast.133), calls=%async_computation | async-start | bytes 8388608
  12.5 20.5 %slice-start.1 = ((s8[8388608]{0:T(1024)(128)(4,1)}), s8[4194304]{0:T(1024)(128)(4,1)S(1)}, s32[]{:S(2)}) async-start(s8[8388608]{0:T(1024)(128)(4,1)} %bitcast.133), calls=%async_computation.1 | async-start | bytes 8388608
  12.5 20.5 %collective-permute-start = (f32[2,8,64,128]{3,2,1,0:T(8,128)S(1)}, f32[2,8,64,128]{3,2,1,0:T(8,128)S(1)}, u32[]{:S(2)}, u32[]{:S(2)}) collective-permute-start(f32[2,8,64,128]{3,2,1,0:T(8,128)S(1)} %get-tuple-element.24), channel_id=1, source_target_pairs={{0,4},{1,5},{2,14},{3,15},{4,8},{5,9},{6,2},{7,3},{8,12},{9,13},{1... | collective-permute-start | bytes 1572872 | tf_op jit(solution)/shard_map/ppermute | solution.py:288
  17.5 5.0 %collective-permute-start.6 = (f32[2,64,128]{2,1,0:T(8,128)S(1)}, f32[2,64,128]{2,1,0:T(8,128)S(1)}, u32[]{:S(2)}, u32[]{:S(2)}) collective-permute-start(f32[2,64,128]{2,1,0:T(8,128)S(1)} %fusion.18), channel_id=1, source_target_pairs={{0,32},{4,36},{8,40},{12,44},{16,48},{20,52},{24,56},{28,60},{32,0... | collective-permute-start | bytes 196616 | tf_op jit(solution)/shard_map/ppermute | solution.py:244
  20.7 4.7 %collective-permute-start.5 = (f32[2,64,128]{2,1,0:T(8,128)S(1)}, f32[2,64,128]{2,1,0:T(8,128)S(1)}, u32[]{:S(2)}, u32[]{:S(2)}) collective-permute-start(f32[2,64,128]{2,1,0:T(8,128)S(1)} %fusion.18), channel_id=1, source_target_pairs={{0,48},{4,52},{8,56},{12,60},{16,32},{20,36},{24,40},{28,44},{32,1... | collective-permute-start | bytes 196616 | tf_op jit(solution)/shard_map/ppermute | solution.py:244
  21.5 3.8 %collective-permute-start.4 = (f32[2,64,128]{2,1,0:T(8,128)S(1)}, f32[2,64,128]{2,1,0:T(8,128)S(1)}, u32[]{:S(2)}, u32[]{:S(2)}) collective-permute-start(f32[2,64,128]{2,1,0:T(8,128)S(1)} %fusion.18), channel_id=1, source_target_pairs={{0,16},{4,20},{8,24},{12,28},{16,0},{20,4},{24,8},{28,12},{32,48},... | collective-permute-start | bytes 196616 | tf_op jit(solution)/shard_map/ppermute | solution.py:244
  25.5 4.7 %collective-permute-start.9 = (f32[2,64,128]{2,1,0:T(8,128)S(1)}, f32[2,64,128]{2,1,0:T(8,128)S(1)}, u32[]{:S(2)}, u32[]{:S(2)}) collective-permute-start(f32[2,64,128]{2,1,0:T(8,128)S(1)} %get-tuple-element.43), channel_id=1, source_target_pairs={{0,128},{4,132},{8,136},{12,140},{16,144},{20,148},{24,152},{28,15... | collective-permute-start | bytes 196616 | tf_op jit(solution)/shard_map/ppermute | solution.py:244
  28.3 4.7 %collective-permute-start.8 = (f32[2,64,128]{2,1,0:T(8,128)S(1)}, f32[2,64,128]{2,1,0:T(8,128)S(1)}, u32[]{:S(2)}, u32[]{:S(2)}) collective-permute-start(f32[2,64,128]{2,1,0:T(8,128)S(1)} %get-tuple-element.43), channel_id=1, source_target_pairs={{0,192},{4,196},{8,200},{12,204},{16,208},{20,212},{24,216},{28,22... | collective-permute-start | bytes 196616 | tf_op jit(solution)/shard_map/ppermute | solution.py:244
  29.2 3.9 %collective-permute-start.7 = (f32[2,64,128]{2,1,0:T(8,128)S(1)}, f32[2,64,128]{2,1,0:T(8,128)S(1)}, u32[]{:S(2)}, u32[]{:S(2)}) collective-permute-start(f32[2,64,128]{2,1,0:T(8,128)S(1)} %get-tuple-element.43), channel_id=1, source_target_pairs={{0,64},{4,68},{8,72},{12,76},{16,80},{20,84},{24,88},{28,92},{32,9... | collective-permute-start | bytes 196616 | tf_op jit(solution)/shard_map/ppermute | solution.py:244
  34.6 4.0 %collective-permute-start.12 = (f32[64,1024]{1,0:T(8,128)S(1)}, f32[64,1024]{1,0:T(8,128)S(1)}, u32[]{:S(2)}, u32[]{:S(2)}) collective-permute-start(f32[64,1024]{1,0:T(8,128)S(1)} %get-tuple-element.37), channel_id=1, source_target_pairs={{0,1},{1,0},{2,3},{3,2},{4,5},{5,4},{6,7},{7,6},{8,9},{9,8},{10,11... | collective-permute-start | bytes 786440 | tf_op jit(solution)/shard_map/ppermute | solution.py:327
  37.4 2.6 %collective-permute-start.10 = (f32[64,1024]{1,0:T(8,128)S(1)}, f32[64,1024]{1,0:T(8,128)S(1)}, u32[]{:S(2)}, u32[]{:S(2)}) collective-permute-start(f32[64,1024]{1,0:T(8,128)S(1)} %get-tuple-element.35), channel_id=1, source_target_pairs={{0,1},{1,0},{2,3},{3,2},{4,5},{5,4},{6,7},{7,6},{8,9},{9,8},{10,11... | collective-permute-start | bytes 786440 | tf_op jit(solution)/shard_map/ppermute | solution.py:327
  38.6 10.2 %collective-permute-start.14 = (f32[128,1024]{1,0:T(8,128)S(1)}, f32[128,1024]{1,0:T(8,128)S(1)}, u32[]{:S(2)}, u32[]{:S(2)}) collective-permute-start(f32[128,1024]{1,0:T(8,128)S(1)} %get-tuple-element.40), channel_id=1, source_target_pairs={{0,1},{1,0},{2,3},{3,2},{4,5},{5,4},{6,7},{7,6},{8,9},{9,8},{10,11... | collective-permute-start | bytes 1572872 | tf_op jit(solution)/shard_map/ppermute | solution.py:327
  39.1 7.8 %collective-permute-start.13 = (f32[64,1024]{1,0:T(8,128)S(1)}, f32[64,1024]{1,0:T(8,128)S(1)}, u32[]{:S(2)}, u32[]{:S(2)}) collective-permute-start(f32[64,1024]{1,0:T(8,128)S(1)} %add.77), channel_id=1, source_target_pairs={{0,2},{1,3},{2,0},{3,1},{4,6},{5,7},{6,4},{7,5},{8,10},{9,11},{10,... | collective-permute-start | bytes 786440 | tf_op jit(solution)/shard_map/ppermute | solution.py:337
  40.1 8.7 %collective-permute-start.11 = (f32[64,1024]{1,0:T(8,128)S(1)}, f32[64,1024]{1,0:T(8,128)S(1)}, u32[]{:S(2)}, u32[]{:S(2)}) collective-permute-start(f32[64,1024]{1,0:T(8,128)S(1)} %add.76), channel_id=1, source_target_pairs={{0,14},{1,15},{2,4},{3,5},{4,2},{5,3},{6,8},{7,9},{8,6},{9,7},{10,... | collective-permute-start | bytes 786440 | tf_op jit(solution)/shard_map/ppermute | solution.py:332

commit v3 on v2

--- a/solution.py
+++ b/solution.py
@@ -179,27 +179,29 @@
     def body(g, carry):
         block = pl.ds(pl.multiple_of(8 * g, 8), 8)
         columns = pl.ds(pl.multiple_of(LANES * g, LANES), LANES)
-        first = 0
-        for n, (queries, locals_) in enumerate(blocks):
-            outer = queries.shape[0]
-            rows = [locals_[i, block, :] for i in range(outer)]
-            for half in range(HALVES):
-                entry, eight = state_ref[n, half, block, :], eight_ref[half, block, :]
-                for m in range(8):
-                    term = spread(entry, m) * powers_ref[8 * half + m, block, :]
-                    factor = spread(eight, m)
-                    for i in range(outer):
+        sums = [
+            [locals_[i, block, :] for i in range(locals_.shape[0])] for _, locals_ in blocks
+        ]
+        for half in range(HALVES):
+            eight = eight_ref[half, block, :]
+            entries = [state_ref[n, half, block, :] for n in range(2)]
+            for m in range(8):
+                power, factor = powers_ref[8 * half + m, block, :], spread(eight, m)
+                for rows, entry in zip(sums, entries):
+                    term = spread(entry, m) * power
+                    for i in range(len(rows)):
                         rows[i] = rows[i] + term
-                        if i + 1 < outer:
+                        if i + 1 < len(rows):
                             term = term * factor
-            rows = [queries[i, block, :] * rows[i] for i in range(outer)]
-            gated_ref[pl.ds(first, 8 * outer), columns] = jnp.concatenate(
-                rows, axis=0
-            ).astype(jnp.bfloat16)
-            first += 8 * outer
+        gated = [
+            queries[i, block, :] * rows[i]
+            for (queries, _), rows in zip(blocks, sums)
+            for i in range(len(rows))
+        ]
+        gated_ref[:, columns] = jnp.concatenate(gated, axis=0).astype(jnp.bfloat16)
         return carry
 
-    lax.fori_loop(0, query_ref.shape[1] // 8, body, 0)
+    lax.fori_loop(0, query_ref.shape[1] // 8, body, 0, unroll=2)
     project_away(gated_ref, weight_ref, 3, own_ref, helped_ref)
 
 
@@ -284,7 +286,7 @@
     )
     from_z = swap(state, 0)
     total_z = run_total(own_z, decays_z, from_z)
-    total_z, _ = lax.optimization_barrier((total_z, handed))
+    total_z, *_ = lax.optimization_barrier((total_z, handed, powers))
     handed = lax.ppermute(
         handed, ("seq", "ch"), along_z(count, lambda z, low: (z + 1 - 2 * low, low))
     )

time: 49.7 us -> 49.6 us (level)
  no operation moved by 1% of the time
where the time goes in v3:
time: 49.6 us; the launch traced here: 49.5 us
  starting transfers between devices  24.7 us (50%)
  waiting for transfers between devices  17.4 us (35%)
  Pallas kernels  5.6 us (11%)
  other arithmetic  1.63 us (3%)
    ppermute x9, starting transfers between devices, swap(): return [lax.ppermute(state, 'seq', pair) for pair in pairs]  16.6 us
    ppermute x9, waiting for transfers between devices, swap(): return [lax.ppermute(state, 'seq', pair) for pair in pairs]  11.1 us
    pallas_call x8, Pallas kernels, kernel_call(): pl.pallas_call(body, out_shape=out_shape, in_specs=[pl.BlockSpec(memory_s...  5.6 us
    ppermute x1, waiting for transfers between devices, local(): own_away = lax.ppermute(own_away, 'ch', partner_pairs(4, 2))  4.25 us
    ppermute x3, starting transfers between devices, core_swap(): return lax.ppermute(one, 'ch', partner_pairs(4, 1))  3.36 us
    ppermute x1, starting transfers between devices, local(): lax.ppermute(helped_away, ('seq', 'ch'), along_z(count, lambda z, low: (z...  2.46 us
    ppermute x1, waiting for transfers between devices, local(): lax.ppermute(helped_away, ('seq', 'ch'), along_z(count, lambda z, low: (z...  2.03 us
    reshape x2, other arithmetic, tiles(): cut.transpose(0, 2, 1, 3).reshape(rows // 8, 8 * (columns // LANES), LANES)  1.41 us
  transfers between devices with their start and end apart: 15, of which 9 were waited for; matrix products, arithmetic and copies ran while one was open for 1% of the time, Pallas kernels for 5%

profile of v3, /device:TPU:1, one launch (start us, length us, event | category | flops | bytes accessed | tf_op | source)
XLA Modules:
  0.0 49.5 jit_solution(1448009698913777839)
XLA Ops:
  0.0 0.0 copy-start.1
  0.0 1.4 %add_bitcast_fusion.stacked_ref.refs_0_ = f32[18,64,128]{2,1,0:T(8,128)S(1)} fusion(f32[16,1024]{1,0:T(8,128)} %param.10, f32[128,1024]{1,0:T(8,128)} %param.6, f32[128,1024]{1,0:T(8,128)} %param.7), kind=kLoop, calls=%fused_computation | loop fusion | flops 294912 | bytes 1703936 | tf_op jit(solution)/shard_map/reshape | solution.py:19
  1.4 0.8 %shard_map.66.refs_1_ = f32[2,64,128]{2,1,0:T(8,128)S(1)} custom-call(f32[18,64,128]{2,1,0:T(8,128)S(1)} %add_bitcast_fusion.stacked_ref.refs_0_), custom_call_target="tpu_custom_call" | custom-call | flops 2000000000 | bytes 600000 | tf_op jit(solution)/shard_map/pallas_call | solution.py:32
  2.2 7.8 %collective-permute-start.3 = (f32[2,64,128]{2,1,0:T(8,128)S(1)}, f32[2,64,128]{2,1,0:T(8,128)S(1)}, u32[]{:S(2)}, u32[]{:S(2)}) collective-permute-start(f32[2,64,128]{2,1,0:T(8,128)S(1)} %shard_map.66.refs_1_), channel_id=1, source_target_pairs={{0,8},{4,12},{8,0},{12,4},{16,24},{20,28},{24,16},{28,20},{32,40},... | collective-permute-start | bytes 196616 | tf_op jit(solution)/shard_map/ppermute | solution.py:246
  10.0 0.0 collective-permute-start.2
  10.0 1.2 %collective-permute-start.1 = (f32[2,64,128]{2,1,0:T(8,128)S(1)}, f32[2,64,128]{2,1,0:T(8,128)S(1)}, u32[]{:S(2)}, u32[]{:S(2)}) collective-permute-start(f32[2,64,128]{2,1,0:T(8,128)S(1)} %shard_map.66.refs_1_), channel_id=1, source_target_pairs={{0,4},{4,0},{8,12},{12,8},{16,20},{20,16},{24,28},{28,24},{32,36},... | collective-permute-start | bytes 196616 | tf_op jit(solution)/shard_map/ppermute | solution.py:246
  11.2 0.0 copy-done.1
  11.2 0.0 copy-done.2
  11.3 0.0 copy-done
  11.3 0.0 slice-start
  11.3 1.2 %shard_map.64 = (f32[16,64,128]{2,1,0:T(8,128)S(1)}, f32[2,8,64,128]{3,2,1,0:T(8,128)S(1)}) custom-call(f32[18,64,128]{2,1,0:T(8,128)S(1)} %add_bitcast_fusion.stacked_ref.refs_0_, f32[2,64,128]{2,1,0:T(8,128)S(1)} %multiply_bitcast_fusion.gain_ref.refs_1_, f32[16,64,128]{2,1,0:T(8,128)S(1)} %bitcast.135), custom_call_target="tpu_custom_call" | custom-call | flops 3000000000 | bytes 1500000 | tf_op jit(solution)/shard_map/pallas_call | solution.py:32
  12.5 0.0 slice-start.1
  12.5 1.2 %collective-permute-start = (f32[2,8,64,128]{3,2,1,0:T(8,128)S(1)}, f32[2,8,64,128]{3,2,1,0:T(8,128)S(1)}, u32[]{:S(2)}, u32[]{:S(2)}) collective-permute-start(f32[2,8,64,128]{3,2,1,0:T(8,128)S(1)} %get-tuple-element.24), channel_id=1, source_target_pairs={{0,4},{1,5},{2,14},{3,15},{4,8},{5,9},{6,2},{7,3},{8,12},{9,13},{1... | collective-permute-start | bytes 1572872 | tf_op jit(solution)/shard_map/ppermute | solution.py:290
  13.8 0.1 shard_map.67
  13.9 0.2 shard_map.65
  14.1 0.0 collective-permute-done.3
  14.1 1.2 %collective-permute-done.2 = f32[2,64,128]{2,1,0:T(8,128)S(1)} collective-permute-done((f32[2,64,128]{2,1,0:T(8,128)S(1)}, f32[2,64,128]{2,1,0:T(8,128)S(1)}, u32[]{:S(2)}, u32[]{:S(2)}) %collective-permute-start.2) | collective-permute-done | bytes 65568 | tf_op jit(solution)/shard_map/ppermute | solution.py:246
  15.3 2.1 %collective-permute-done.1 = f32[2,64,128]{2,1,0:T(8,128)S(1)} collective-permute-done((f32[2,64,128]{2,1,0:T(8,128)S(1)}, f32[2,64,128]{2,1,0:T(8,128)S(1)}, u32[]{:S(2)}, u32[]{:S(2)}) %collective-permute-start.1) | collective-permute-done | bytes 65568 | tf_op jit(solution)/shard_map/ppermute | solution.py:246
  17.5 3.0 %collective-permute-start.6 = (f32[2,64,128]{2,1,0:T(8,128)S(1)}, f32[2,64,128]{2,1,0:T(8,128)S(1)}, u32[]{:S(2)}, u32[]{:S(2)}) collective-permute-start(f32[2,64,128]{2,1,0:T(8,128)S(1)} %fusion.18), channel_id=1, source_target_pairs={{0,32},{4,36},{8,40},{12,44},{16,48},{20,52},{24,56},{28,60},{32,0... | collective-permute-start | bytes 196616 | tf_op jit(solution)/shard_map/ppermute | solution.py:246
  20.5 0.1 shard_map.68
  20.6 0.9 %collective-permute-start.5 = (f32[2,64,128]{2,1,0:T(8,128)S(1)}, f32[2,64,128]{2,1,0:T(8,128)S(1)}, u32[]{:S(2)}, u32[]{:S(2)}) collective-permute-start(f32[2,64,128]{2,1,0:T(8,128)S(1)} %fusion.18), channel_id=1, source_target_pairs={{0,48},{4,52},{8,56},{12,60},{16,32},{20,36},{24,40},{28,44},{32,1... | collective-permute-start | bytes 196616 | tf_op jit(solution)/shard_map/ppermute | solution.py:246
  21.4 0.0 collective-permute-start.4
  21.4 1.1 %collective-permute-done.6 = f32[2,64,128]{2,1,0:T(8,128)S(1)} collective-permute-done((f32[2,64,128]{2,1,0:T(8,128)S(1)}, f32[2,64,128]{2,1,0:T(8,128)S(1)}, u32[]{:S(2)}, u32[]{:S(2)}) %collective-permute-start.6) | collective-permute-done | bytes 65568 | tf_op jit(solution)/shard_map/ppermute | solution.py:246
  22.5 2.8 %collective-permute-done.5 = f32[2,64,128]{2,1,0:T(8,128)S(1)} collective-permute-done((f32[2,64,128]{2,1,0:T(8,128)S(1)}, f32[2,64,128]{2,1,0:T(8,128)S(1)}, u32[]{:S(2)}, u32[]{:S(2)}) %collective-permute-start.5) | collective-permute-done | bytes 65568 | tf_op jit(solution)/shard_map/ppermute | solution.py:246
  25.3 0.0 collective-permute-done.4
  25.3 0.1 fusion.12
  25.4 2.8 %collective-permute-start.9 = (f32[2,64,128]{2,1,0:T(8,128)S(1)}, f32[2,64,128]{2,1,0:T(8,128)S(1)}, u32[]{:S(2)}, u32[]{:S(2)}) collective-permute-start(f32[2,64,128]{2,1,0:T(8,128)S(1)} %get-tuple-element.43), channel_id=1, source_target_pairs={{0,128},{4,132},{8,136},{12,140},{16,144},{20,148},{24,152},{28,15... | collective-permute-start | bytes 196616 | tf_op jit(solution)/shard_map/ppermute | solution.py:246
  28.2 0.9 %collective-permute-start.8 = (f32[2,64,128]{2,1,0:T(8,128)S(1)}, f32[2,64,128]{2,1,0:T(8,128)S(1)}, u32[]{:S(2)}, u32[]{:S(2)}) collective-permute-start(f32[2,64,128]{2,1,0:T(8,128)S(1)} %get-tuple-element.43), channel_id=1, source_target_pairs={{0,192},{4,196},{8,200},{12,204},{16,208},{20,212},{24,216},{28,22... | collective-permute-start | bytes 196616 | tf_op jit(solution)/shard_map/ppermute | solution.py:246
  29.1 0.0 collective-permute-start.7
  29.1 1.0 %collective-permute-done.9.refs_11_ = f32[2,64,128]{2,1,0:T(8,128)S(1)} collective-permute-done((f32[2,64,128]{2,1,0:T(8,128)S(1)}, f32[2,64,128]{2,1,0:T(8,128)S(1)}, u32[]{:S(2)}, u32[]{:S(2)}) %collective-permute-start.9) | collective-permute-done | bytes 65568 | tf_op jit(solution)/shard_map/ppermute | solution.py:246
  30.1 2.9 %collective-permute-done.8.refs_10_ = f32[2,64,128]{2,1,0:T(8,128)S(1)} collective-permute-done((f32[2,64,128]{2,1,0:T(8,128)S(1)}, f32[2,64,128]{2,1,0:T(8,128)S(1)}, u32[]{:S(2)}, u32[]{:S(2)}) %collective-permute-start.8) | collective-permute-done | bytes 65568 | tf_op jit(solution)/shard_map/ppermute | solution.py:246
  33.0 0.0 collective-permute-done.7.refs_9_
  33.0 0.0 collective-permute-done.refs_2_
  33.0 0.0 slice-done
  33.0 0.0 slice-done.1
  33.0 1.5 %shard_map.69 = (bf16[192,1024]{1,0:T(8,128)(2,1)S(1)}, f32[64,1024]{1,0:T(8,128)S(1)}, f32[64,1024]{1,0:T(8,128)S(1)}) custom-call(f32[16,64,128]{2,1,0:T(8,128)S(1)} %bitcast.136, f32[16,64,128]{2,1,0:T(8,128)S(1)} %get-tuple-element.23.refs_1_, f32[2,8,64,128]{3,2,1,0:T(8,128)S(1)} %collective-permute-done.refs_2_, ...), custom_call_target="tpu_custom_call" | custom-call | flops 2000000000 | bytes 3000000 | tf_op jit(solution)/shard_map/pallas_call | solution.py:32
  34.4 2.8 %collective-permute-start.12 = (f32[64,1024]{1,0:T(8,128)S(1)}, f32[64,1024]{1,0:T(8,128)S(1)}, u32[]{:S(2)}, u32[]{:S(2)}) collective-permute-start(f32[64,1024]{1,0:T(8,128)S(1)} %get-tuple-element.37), channel_id=1, source_target_pairs={{0,1},{1,0},{2,3},{3,2},{4,5},{5,4},{6,7},{7,6},{8,9},{9,8},{10,11... | collective-permute-start | bytes 786440 | tf_op jit(solution)/shard_map/ppermute | solution.py:329
  37.2 0.1 collective-permute-start.10
  37.3 1.0 %shard_map.70 = (f32[64,1024]{1,0:T(8,128)S(1)}, f32[64,1024]{1,0:T(8,128)S(1)}, f32[128,1024]{1,0:T(8,128)S(1)}, f32[128,1024]{1,0:T(8,128)S(1)}) custom-call(bf16[192,1024]{1,0:T(8,128)(2,1)S(1)} %get-tuple-element.32.gated_ref, bf16[1024,4096]{1,0:T(8,128)(2,1)S(1)} %bitcast.134), custom_call_target="tpu_custom_call" | custom-call | flops 1000000 | bytes 10000 | tf_op jit(solution)/shard_map/pallas_call | solution.py:32
  38.3 0.1 collective-permute-done.12
  38.4 0.5 collective-permute-start.14
  38.9 1.0 %collective-permute-start.13 = (f32[64,1024]{1,0:T(8,128)S(1)}, f32[64,1024]{1,0:T(8,128)S(1)}, u32[]{:S(2)}, u32[]{:S(2)}) collective-permute-start(f32[64,1024]{1,0:T(8,128)S(1)} %add.77), channel_id=1, source_target_pairs={{0,2},{1,3},{2,0},{3,1},{4,6},{5,7},{6,4},{7,5},{8,10},{9,11},{10,... | collective-permute-start | bytes 786440 | tf_op jit(solution)/shard_map/ppermute | solution.py:339
  39.9 0.0 collective-permute-done.10
  40.0 2.5 %collective-permute-start.11 = (f32[64,1024]{1,0:T(8,128)S(1)}, f32[64,1024]{1,0:T(8,128)S(1)}, u32[]{:S(2)}, u32[]{:S(2)}) collective-permute-start(f32[64,1024]{1,0:T(8,128)S(1)} %add.76), channel_id=1, source_target_pairs={{0,14},{1,15},{2,4},{3,5},{4,2},{5,3},{6,8},{7,9},{8,6},{9,7},{10,... | collective-permute-start | bytes 786440 | tf_op jit(solution)/shard_map/ppermute | solution.py:334
  42.4 4.3 %collective-permute-done.13.own_ref = f32[64,1024]{1,0:T(8,128)S(1)} collective-permute-done((f32[64,1024]{1,0:T(8,128)S(1)}, f32[64,1024]{1,0:T(8,128)S(1)}, u32[]{:S(2)}, u32[]{:S(2)}) %collective-permute-start.13) | collective-permute-done | bytes 262176 | tf_op jit(solution)/shard_map/ppermute | solution.py:339
  46.7 2.0 %collective-permute-done.11.helped_ref = f32[64,1024]{1,0:T(8,128)S(1)} collective-permute-done((f32[64,1024]{1,0:T(8,128)S(1)}, f32[64,1024]{1,0:T(8,128)S(1)}, u32[]{:S(2)}, u32[]{:S(2)}) %collective-permute-start.11) | collective-permute-done | bytes 262176 | tf_op jit(solution)/shard_map/ppermute | solution.py:334
  48.7 0.0 collective-permute-done.14.core_ref
  48.7 0.8 %shard_map.71 = bf16[128,1024]{1,0:T(8,128)(2,1)} custom-call(f32[128,1024]{1,0:T(8,128)S(1)} %get-tuple-element.33.home_ref, f32[64,1024]{1,0:T(8,128)S(1)} %collective-permute-done.11.helped_ref, f32[64,1024]{1,0:T(8,128)S(1)} %collective-permute-done.13.own_ref, f32[128,1024]{1,0:T(8,128)S(1)} %collective-permute-done.14.core_ref), custom_call_target="tpu_custom_call" | custom-call | flops 1000000 | bytes 2000000 | tf_op jit(solution)/shard_map/pallas_call | solution.py:32
  (10 shorter events, 0.2 us)
Async XLA Ops:
  0.0 11.2 %copy-start.1 = (f32[16,1024]{1,0:T(8,128)S(1)}, f32[16,1024]{1,0:T(8,128)}, u32[]{:S(2)}) copy-start(f32[16,1024]{1,0:T(8,128)} %param.10) | copy-start | bytes 196612
  0.0 11.2 %copy-start.2 = (f32[16,1024]{1,0:T(8,128)S(1)}, f32[16,1024]{1,0:T(8,128)}, u32[]{:S(2)}) copy-start(f32[16,1024]{1,0:T(8,128)} %param.9) | copy-start | bytes 196612
  0.0 11.2 %copy-start = (f32[128,1024]{1,0:T(8,128)S(1)}, f32[128,1024]{1,0:T(8,128)}, u32[]{:S(2)}) copy-start(f32[128,1024]{1,0:T(8,128)} %param.8) | copy-start | bytes 1572868
  2.2 11.9 %collective-permute-start.3 = (f32[2,64,128]{2,1,0:T(8,128)S(1)}, f32[2,64,128]{2,1,0:T(8,128)S(1)}, u32[]{:S(2)}, u32[]{:S(2)}) collective-permute-start(f32[2,64,128]{2,1,0:T(8,128)S(1)} %shard_map.66.refs_1_), channel_id=1, source_target_pairs={{0,8},{4,12},{8,0},{12,4},{16,24},{20,28},{24,16},{28,20},{32,40},... | collective-permute-start | bytes 196616 | tf_op jit(solution)/shard_map/ppermute | solution.py:246
  10.0 5.3 %collective-permute-start.2 = (f32[2,64,128]{2,1,0:T(8,128)S(1)}, f32[2,64,128]{2,1,0:T(8,128)S(1)}, u32[]{:S(2)}, u32[]{:S(2)}) collective-permute-start(f32[2,64,128]{2,1,0:T(8,128)S(1)} %shard_map.66.refs_1_), channel_id=1, source_target_pairs={{0,12},{4,8},{8,4},{12,0},{16,28},{20,24},{24,20},{28,16},{32,44},... | collective-permute-start | bytes 196616 | tf_op jit(solution)/shard_map/ppermute | solution.py:246
  10.0 7.5 %collective-permute-start.1 = (f32[2,64,128]{2,1,0:T(8,128)S(1)}, f32[2,64,128]{2,1,0:T(8,128)S(1)}, u32[]{:S(2)}, u32[]{:S(2)}) collective-permute-start(f32[2,64,128]{2,1,0:T(8,128)S(1)} %shard_map.66.refs_1_), channel_id=1, source_target_pairs={{0,4},{4,0},{8,12},{12,8},{16,20},{20,16},{24,28},{28,24},{32,36},... | collective-permute-start | bytes 196616 | tf_op jit(solution)/shard_map/ppermute | solution.py:246
  11.3 21.7 %slice-start = ((s8[8388608]{0:T(1024)(128)(4,1)}), s8[4194304]{0:T(1024)(128)(4,1)S(1)}, s32[]{:S(2)}) async-start(s8[8388608]{0:T(1024)(128)(4,1)} %bitcast.133), calls=%async_computation | async-start | bytes 8388608
  12.5 20.4 %slice-start.1 = ((s8[8388608]{0:T(1024)(128)(4,1)}), s8[4194304]{0:T(1024)(128)(4,1)S(1)}, s32[]{:S(2)}) async-start(s8[8388608]{0:T(1024)(128)(4,1)} %bitcast.133), calls=%async_computation.1 | async-start | bytes 8388608
  12.5 20.4 %collective-permute-start = (f32[2,8,64,128]{3,2,1,0:T(8,128)S(1)}, f32[2,8,64,128]{3,2,1,0:T(8,128)S(1)}, u32[]{:S(2)}, u32[]{:S(2)}) collective-permute-start(f32[2,8,64,128]{3,2,1,0:T(8,128)S(1)} %get-tuple-element.24), channel_id=1, source_target_pairs={{0,4},{1,5},{2,14},{3,15},{4,8},{5,9},{6,2},{7,3},{8,12},{9,13},{1... | collective-permute-start | bytes 1572872 | tf_op jit(solution)/shard_map/ppermute | solution.py:290
  17.5 5.0 %collective-permute-start.6 = (f32[2,64,128]{2,1,0:T(8,128)S(1)}, f32[2,64,128]{2,1,0:T(8,128)S(1)}, u32[]{:S(2)}, u32[]{:S(2)}) collective-permute-start(f32[2,64,128]{2,1,0:T(8,128)S(1)} %fusion.18), channel_id=1, source_target_pairs={{0,32},{4,36},{8,40},{12,44},{16,48},{20,52},{24,56},{28,60},{32,0... | collective-permute-start | bytes 196616 | tf_op jit(solution)/shard_map/ppermute | solution.py:246
  20.6 4.7 %collective-permute-start.5 = (f32[2,64,128]{2,1,0:T(8,128)S(1)}, f32[2,64,128]{2,1,0:T(8,128)S(1)}, u32[]{:S(2)}, u32[]{:S(2)}) collective-permute-start(f32[2,64,128]{2,1,0:T(8,128)S(1)} %fusion.18), channel_id=1, source_target_pairs={{0,48},{4,52},{8,56},{12,60},{16,32},{20,36},{24,40},{28,44},{32,1... | collective-permute-start | bytes 196616 | tf_op jit(solution)/shard_map/ppermute | solution.py:246
  21.4 3.8 %collective-permute-start.4 = (f32[2,64,128]{2,1,0:T(8,128)S(1)}, f32[2,64,128]{2,1,0:T(8,128)S(1)}, u32[]{:S(2)}, u32[]{:S(2)}) collective-permute-start(f32[2,64,128]{2,1,0:T(8,128)S(1)} %fusion.18), channel_id=1, source_target_pairs={{0,16},{4,20},{8,24},{12,28},{16,0},{20,4},{24,8},{28,12},{32,48},... | collective-permute-start | bytes 196616 | tf_op jit(solution)/shard_map/ppermute | solution.py:246
  25.4 4.7 %collective-permute-start.9 = (f32[2,64,128]{2,1,0:T(8,128)S(1)}, f32[2,64,128]{2,1,0:T(8,128)S(1)}, u32[]{:S(2)}, u32[]{:S(2)}) collective-permute-start(f32[2,64,128]{2,1,0:T(8,128)S(1)} %get-tuple-element.43), channel_id=1, source_target_pairs={{0,128},{4,132},{8,136},{12,140},{16,144},{20,148},{24,152},{28,15... | collective-permute-start | bytes 196616 | tf_op jit(solution)/shard_map/ppermute | solution.py:246
  28.2 4.7 %collective-permute-start.8 = (f32[2,64,128]{2,1,0:T(8,128)S(1)}, f32[2,64,128]{2,1,0:T(8,128)S(1)}, u32[]{:S(2)}, u32[]{:S(2)}) collective-permute-start(f32[2,64,128]{2,1,0:T(8,128)S(1)} %get-tuple-element.43), channel_id=1, source_target_pairs={{0,192},{4,196},{8,200},{12,204},{16,208},{20,212},{24,216},{28,22... | collective-permute-start | bytes 196616 | tf_op jit(solution)/shard_map/ppermute | solution.py:246
  29.1 3.9 %collective-permute-start.7 = (f32[2,64,128]{2,1,0:T(8,128)S(1)}, f32[2,64,128]{2,1,0:T(8,128)S(1)}, u32[]{:S(2)}, u32[]{:S(2)}) collective-permute-start(f32[2,64,128]{2,1,0:T(8,128)S(1)} %get-tuple-element.43), channel_id=1, source_target_pairs={{0,64},{4,68},{8,72},{12,76},{16,80},{20,84},{24,88},{28,92},{32,9... | collective-permute-start | bytes 196616 | tf_op jit(solution)/shard_map/ppermute | solution.py:246
  34.4 4.0 %collective-permute-start.12 = (f32[64,1024]{1,0:T(8,128)S(1)}, f32[64,1024]{1,0:T(8,128)S(1)}, u32[]{:S(2)}, u32[]{:S(2)}) collective-permute-start(f32[64,1024]{1,0:T(8,128)S(1)} %get-tuple-element.37), channel_id=1, source_target_pairs={{0,1},{1,0},{2,3},{3,2},{4,5},{5,4},{6,7},{7,6},{8,9},{9,8},{10,11... | collective-permute-start | bytes 786440 | tf_op jit(solution)/shard_map/ppermute | solution.py:329
  37.2 2.7 %collective-permute-start.10 = (f32[64,1024]{1,0:T(8,128)S(1)}, f32[64,1024]{1,0:T(8,128)S(1)}, u32[]{:S(2)}, u32[]{:S(2)}) collective-permute-start(f32[64,1024]{1,0:T(8,128)S(1)} %get-tuple-element.35), channel_id=1, source_target_pairs={{0,1},{1,0},{2,3},{3,2},{4,5},{5,4},{6,7},{7,6},{8,9},{9,8},{10,11... | collective-permute-start | bytes 786440 | tf_op jit(solution)/shard_map/ppermute | solution.py:329
  38.4 10.3 %collective-permute-start.14 = (f32[128,1024]{1,0:T(8,128)S(1)}, f32[128,1024]{1,0:T(8,128)S(1)}, u32[]{:S(2)}, u32[]{:S(2)}) collective-permute-start(f32[128,1024]{1,0:T(8,128)S(1)} %get-tuple-element.40), channel_id=1, source_target_pairs={{0,1},{1,0},{2,3},{3,2},{4,5},{5,4},{6,7},{7,6},{8,9},{9,8},{10,11... | collective-permute-start | bytes 1572872 | tf_op jit(solution)/shard_map/ppermute | solution.py:329
  38.9 7.8 %collective-permute-start.13 = (f32[64,1024]{1,0:T(8,128)S(1)}, f32[64,1024]{1,0:T(8,128)S(1)}, u32[]{:S(2)}, u32[]{:S(2)}) collective-permute-start(f32[64,1024]{1,0:T(8,128)S(1)} %add.77), channel_id=1, source_target_pairs={{0,2},{1,3},{2,0},{3,1},{4,6},{5,7},{6,4},{7,5},{8,10},{9,11},{10,... | collective-permute-start | bytes 786440 | tf_op jit(solution)/shard_map/ppermute | solution.py:339
  40.0 8.7 %collective-permute-start.11 = (f32[64,1024]{1,0:T(8,128)S(1)}, f32[64,1024]{1,0:T(8,128)S(1)}, u32[]{:S(2)}, u32[]{:S(2)}) collective-permute-start(f32[64,1024]{1,0:T(8,128)S(1)} %add.76), channel_id=1, source_target_pairs={{0,14},{1,15},{2,4},{3,5},{4,2},{5,3},{6,8},{7,9},{8,6},{9,7},{10,... | collective-permute-start | bytes 786440 | tf_op jit(solution)/shard_map/ppermute | solution.py:334

commit v4 on v3

--- a/solution.py
+++ b/solution.py
@@ -212,11 +212,24 @@
     home_ref[...] = project(gated_ref[:rows, :], weight_ref, 0)
 
 
-def finish_kernel(home_ref, helped_ref, own_ref, core_ref, out_ref):
-    count = helped_ref.shape[0]
-    for part, away_ref in ((pl.ds(0, count), helped_ref), (pl.ds(count, own_ref.shape[0]), own_ref)):
-        total = core_ref[part, :] + home_ref[part, :] + away_ref[...]
+def in_turn(one, other):
+    ahead = lax.rem(lax.axis_index("ch"), 2) == 0
+    return jnp.where(ahead, one, other), jnp.where(ahead, other, one)
+
+
+def sum_kernel(own_ref, helped_ref, own_core_ref, helped_core_ref, first_ref, second_ref):
+    own, helped = own_ref[...] + own_core_ref[...], helped_ref[...] + helped_core_ref[...]
+    first_ref[...], second_ref[...] = in_turn(own, helped)
+
+
+def finish_kernel(home_ref, second_ref, first_ref, core_ref, out_ref):
+    own, helped = in_turn(first_ref[...], second_ref[...])
+    start = 0
+    for away in (helped, own):
+        part = pl.ds(start, away.shape[0])
+        total = home_ref[part, :] + core_ref[part, :] + away
         out_ref[part, :] = total.astype(jnp.bfloat16)
+        start += away.shape[0]
 
 
 def partner_pairs(size, step):
@@ -328,19 +341,24 @@
     def core_swap(one):
         return lax.ppermute(one, "ch", partner_pairs(4, 1))
 
-    own_away = own_kept + core_swap(own_sent)
-    own_away, home_sent = lax.optimization_barrier((own_away, home_sent))
-    helped_away = helped_kept + core_swap(helped_sent)
-    helped_away = lax.ppermute(
-        helped_away,
-        ("seq", "ch"),
-        along_z(count, lambda z, low: (z - 1 + 2 * low, 1 - low)),
-    )
-    own_away = lax.ppermute(own_away, "ch", partner_pairs(4, 2))
+    first, second = kernel_call(
+        sum_kernel,
+        away,
+        (own_kept, helped_kept, core_swap(own_sent), core_swap(helped_sent)),
+        1_000_000,
+        10_000,
+    )
+    first, home_sent = lax.optimization_barrier((first, home_sent))
+    pair = along_z(count, lambda z, low: (z, 1 - low))
+    other = along_z(count, lambda z, low: (z - 1 + 2 * low, 1 - low))
+    mixed = [(pair, other)[i % 2][i] for i in range(len(pair))]
+    turned = [(other, pair)[i % 2][i] for i in range(len(pair))]
+    second = lax.ppermute(second, ("seq", "ch"), turned)
+    first = lax.ppermute(first, ("seq", "ch"), mixed)
     return kernel_call(
         finish_kernel,
         jax.ShapeDtypeStruct((rows, width), jnp.bfloat16),
-        (home_kept, helped_away, own_away, core_swap(home_sent)),
+        (home_kept, second, first, core_swap(home_sent)),
         1_000_000,
         2_000_000,
     )

time: 49.6 us -> 49.1 us (0.990)
  starting transfers between devices: 24.7 us -> 23.6 us
  waiting for transfers between devices: 17.4 us -> 18 us
    ppermute x2, starting transfers between devices: 3.48 us -> 2.39 us  [the longest x1 2.39 us: local(): first = lax.ppermute(first, ('seq', 'ch'), mixed)]
    pallas_call x8 -> x9, Pallas kernels: 5.6 us -> 5.68 us  [kernel_call(): pl.pallas_call(body, out_shape=out_shape, in_specs=[pl.BlockSpec(memory_s...]
  transfers between devices with their start and end apart: 15 -> 15, of which waited for: 9 -> 10; matrix products, arithmetic and copies ran while one was open for 1% -> 0% of each run, Pallas kernels for 5% -> 5%
where the time goes in v4:
time: 49.1 us; the launch traced here: 49 us
  starting transfers between devices  23.6 us (48%)
  waiting for transfers between devices  18 us (37%)
  Pallas kernels  5.68 us (12%)
  other arithmetic  1.59 us (3%)
    ppermute x9, starting transfers between devices, swap(): return [lax.ppermute(state, 'seq', pair) for pair in pairs]  16.6 us
    ppermute x9, waiting for transfers between devices, swap(): return [lax.ppermute(state, 'seq', pair) for pair in pairs]  11 us
    pallas_call x9, Pallas kernels, kernel_call(): pl.pallas_call(body, out_shape=out_shape, in_specs=[pl.BlockSpec(memory_s...  5.68 us
    ppermute x1, waiting for transfers between devices, local(): first = lax.ppermute(first, ('seq', 'ch'), mixed)  5.19 us
    ppermute x3, starting transfers between devices, core_swap(): return lax.ppermute(one, 'ch', partner_pairs(4, 1))  3.37 us
    ppermute x1, starting transfers between devices, local(): first = lax.ppermute(first, ('seq', 'ch'), mixed)  2.39 us
    reshape x2, other arithmetic, tiles(): cut.transpose(0, 2, 1, 3).reshape(rows // 8, 8 * (columns // LANES), LANES)  1.41 us
    ppermute x1, waiting for transfers between devices, local(): second = lax.ppermute(second, ('seq', 'ch'), turned)  1.34 us
  transfers between devices with their start and end apart: 15, of which 10 were waited for; matrix products, arithmetic and copies ran while one was open for 0% of the time, Pallas kernels for 5%

profile of v4, /device:TPU:1, one launch (start us, length us, event | category | flops | bytes accessed | tf_op | source)
XLA Modules:
  0.0 49.0 jit_solution(2038133040230333662)
XLA Ops:
  0.0 1.4 %add_bitcast_fusion.stacked_ref.refs_0_ = f32[18,64,128]{2,1,0:T(8,128)S(1)} fusion(f32[16,1024]{1,0:T(8,128)} %param.10, f32[128,1024]{1,0:T(8,128)} %param.6, f32[128,1024]{1,0:T(8,128)} %param.7), kind=kLoop, calls=%fused_computation | loop fusion | flops 294912 | bytes 1703936 | tf_op jit(solution)/shard_map/reshape | solution.py:19
  1.4 0.8 %shard_map.66.refs_1_ = f32[2,64,128]{2,1,0:T(8,128)S(1)} custom-call(f32[18,64,128]{2,1,0:T(8,128)S(1)} %add_bitcast_fusion.stacked_ref.refs_0_), custom_call_target="tpu_custom_call" | custom-call | flops 2000000000 | bytes 600000 | tf_op jit(solution)/shard_map/pallas_call | solution.py:32
  2.2 7.8 %collective-permute-start.3 = (f32[2,64,128]{2,1,0:T(8,128)S(1)}, f32[2,64,128]{2,1,0:T(8,128)S(1)}, u32[]{:S(2)}, u32[]{:S(2)}) collective-permute-start(f32[2,64,128]{2,1,0:T(8,128)S(1)} %shard_map.66.refs_1_), channel_id=1, source_target_pairs={{0,8},{4,12},{8,0},{12,4},{16,24},{20,28},{24,16},{28,20},{32,40},... | collective-permute-start | bytes 196616 | tf_op jit(solution)/shard_map/ppermute | solution.py:259
  10.0 0.0 collective-permute-start.2
  10.0 1.2 %collective-permute-start.1 = (f32[2,64,128]{2,1,0:T(8,128)S(1)}, f32[2,64,128]{2,1,0:T(8,128)S(1)}, u32[]{:S(2)}, u32[]{:S(2)}) collective-permute-start(f32[2,64,128]{2,1,0:T(8,128)S(1)} %shard_map.66.refs_1_), channel_id=1, source_target_pairs={{0,4},{4,0},{8,12},{12,8},{16,20},{20,16},{24,28},{28,24},{32,36},... | collective-permute-start | bytes 196616 | tf_op jit(solution)/shard_map/ppermute | solution.py:259
  11.2 0.0 copy-done.1
  11.2 0.0 copy-done.2
  11.3 0.0 copy-done
  11.3 0.0 slice-start
  11.3 1.2 %shard_map.64 = (f32[16,64,128]{2,1,0:T(8,128)S(1)}, f32[2,8,64,128]{3,2,1,0:T(8,128)S(1)}) custom-call(f32[18,64,128]{2,1,0:T(8,128)S(1)} %add_bitcast_fusion.stacked_ref.refs_0_, f32[2,64,128]{2,1,0:T(8,128)S(1)} %multiply_bitcast_fusion.gain_ref.refs_1_, f32[16,64,128]{2,1,0:T(8,128)S(1)} %bitcast.135), custom_call_target="tpu_custom_call" | custom-call | flops 3000000000 | bytes 1500000 | tf_op jit(solution)/shard_map/pallas_call | solution.py:32
  12.5 0.0 slice-start.1
  12.5 1.2 %collective-permute-start = (f32[2,8,64,128]{3,2,1,0:T(8,128)S(1)}, f32[2,8,64,128]{3,2,1,0:T(8,128)S(1)}, u32[]{:S(2)}, u32[]{:S(2)}) collective-permute-start(f32[2,8,64,128]{3,2,1,0:T(8,128)S(1)} %get-tuple-element.26), channel_id=1, source_target_pairs={{0,4},{1,5},{2,14},{3,15},{4,8},{5,9},{6,2},{7,3},{8,12},{9,13},{1... | collective-permute-start | bytes 1572872 | tf_op jit(solution)/shard_map/ppermute | solution.py:303
  13.8 0.1 shard_map.67
  13.9 0.2 shard_map.65
  14.1 0.0 collective-permute-done.3
  14.1 1.2 %collective-permute-done.2 = f32[2,64,128]{2,1,0:T(8,128)S(1)} collective-permute-done((f32[2,64,128]{2,1,0:T(8,128)S(1)}, f32[2,64,128]{2,1,0:T(8,128)S(1)}, u32[]{:S(2)}, u32[]{:S(2)}) %collective-permute-start.2) | collective-permute-done | bytes 65568 | tf_op jit(solution)/shard_map/ppermute | solution.py:259
  15.3 2.1 %collective-permute-done.1 = f32[2,64,128]{2,1,0:T(8,128)S(1)} collective-permute-done((f32[2,64,128]{2,1,0:T(8,128)S(1)}, f32[2,64,128]{2,1,0:T(8,128)S(1)}, u32[]{:S(2)}, u32[]{:S(2)}) %collective-permute-start.1) | collective-permute-done | bytes 65568 | tf_op jit(solution)/shard_map/ppermute | solution.py:259
  17.5 3.0 %collective-permute-start.6 = (f32[2,64,128]{2,1,0:T(8,128)S(1)}, f32[2,64,128]{2,1,0:T(8,128)S(1)}, u32[]{:S(2)}, u32[]{:S(2)}) collective-permute-start(f32[2,64,128]{2,1,0:T(8,128)S(1)} %fusion.18), channel_id=1, source_target_pairs={{0,32},{4,36},{8,40},{12,44},{16,48},{20,52},{24,56},{28,60},{32,0... | collective-permute-start | bytes 196616 | tf_op jit(solution)/shard_map/ppermute | solution.py:259
  20.5 0.1 shard_map.68
  20.6 0.9 %collective-permute-start.5 = (f32[2,64,128]{2,1,0:T(8,128)S(1)}, f32[2,64,128]{2,1,0:T(8,128)S(1)}, u32[]{:S(2)}, u32[]{:S(2)}) collective-permute-start(f32[2,64,128]{2,1,0:T(8,128)S(1)} %fusion.18), channel_id=1, source_target_pairs={{0,48},{4,52},{8,56},{12,60},{16,32},{20,36},{24,40},{28,44},{32,1... | collective-permute-start | bytes 196616 | tf_op jit(solution)/shard_map/ppermute | solution.py:259
  21.4 0.0 collective-permute-start.4
  21.4 1.1 %collective-permute-done.6 = f32[2,64,128]{2,1,0:T(8,128)S(1)} collective-permute-done((f32[2,64,128]{2,1,0:T(8,128)S(1)}, f32[2,64,128]{2,1,0:T(8,128)S(1)}, u32[]{:S(2)}, u32[]{:S(2)}) %collective-permute-start.6) | collective-permute-done | bytes 65568 | tf_op jit(solution)/shard_map/ppermute | solution.py:259
  22.5 2.8 %collective-permute-done.5 = f32[2,64,128]{2,1,0:T(8,128)S(1)} collective-permute-done((f32[2,64,128]{2,1,0:T(8,128)S(1)}, f32[2,64,128]{2,1,0:T(8,128)S(1)}, u32[]{:S(2)}, u32[]{:S(2)}) %collective-permute-start.5) | collective-permute-done | bytes 65568 | tf_op jit(solution)/shard_map/ppermute | solution.py:259
  25.3 0.0 collective-permute-done.4
  25.3 0.1 fusion.12
  25.4 2.8 %collective-permute-start.9 = (f32[2,64,128]{2,1,0:T(8,128)S(1)}, f32[2,64,128]{2,1,0:T(8,128)S(1)}, u32[]{:S(2)}, u32[]{:S(2)}) collective-permute-start(f32[2,64,128]{2,1,0:T(8,128)S(1)} %get-tuple-element.47), channel_id=1, source_target_pairs={{0,128},{4,132},{8,136},{12,140},{16,144},{20,148},{24,152},{28,15... | collective-permute-start | bytes 196616 | tf_op jit(solution)/shard_map/ppermute | solution.py:259
  28.2 0.9 %collective-permute-start.8 = (f32[2,64,128]{2,1,0:T(8,128)S(1)}, f32[2,64,128]{2,1,0:T(8,128)S(1)}, u32[]{:S(2)}, u32[]{:S(2)}) collective-permute-start(f32[2,64,128]{2,1,0:T(8,128)S(1)} %get-tuple-element.47), channel_id=1, source_target_pairs={{0,192},{4,196},{8,200},{12,204},{16,208},{20,212},{24,216},{28,22... | collective-permute-start | bytes 196616 | tf_op jit(solution)/shard_map/ppermute | solution.py:259
  29.1 0.0 collective-permute-start.7
  29.1 1.0 %collective-permute-done.9.refs_11_ = f32[2,64,128]{2,1,0:T(8,128)S(1)} collective-permute-done((f32[2,64,128]{2,1,0:T(8,128)S(1)}, f32[2,64,128]{2,1,0:T(8,128)S(1)}, u32[]{:S(2)}, u32[]{:S(2)}) %collective-permute-start.9) | collective-permute-done | bytes 65568 | tf_op jit(solution)/shard_map/ppermute | solution.py:259
  30.1 2.9 %collective-permute-done.8.refs_10_ = f32[2,64,128]{2,1,0:T(8,128)S(1)} collective-permute-done((f32[2,64,128]{2,1,0:T(8,128)S(1)}, f32[2,64,128]{2,1,0:T(8,128)S(1)}, u32[]{:S(2)}, u32[]{:S(2)}) %collective-permute-start.8) | collective-permute-done | bytes 65568 | tf_op jit(solution)/shard_map/ppermute | solution.py:259
  33.0 0.0 collective-permute-done.7.refs_9_
  33.0 0.0 collective-permute-done.refs_2_
  33.0 0.0 slice-done
  33.0 0.0 slice-done.1
  33.0 1.5 %shard_map.69 = (bf16[192,1024]{1,0:T(8,128)(2,1)S(1)}, f32[64,1024]{1,0:T(8,128)S(1)}, f32[64,1024]{1,0:T(8,128)S(1)}) custom-call(f32[16,64,128]{2,1,0:T(8,128)S(1)} %bitcast.136, f32[16,64,128]{2,1,0:T(8,128)S(1)} %get-tuple-element.25.refs_1_, f32[2,8,64,128]{3,2,1,0:T(8,128)S(1)} %collective-permute-done.refs_2_, ...), custom_call_target="tpu_custom_call" | custom-call | flops 2000000000 | bytes 3000000 | tf_op jit(solution)/shard_map/pallas_call | solution.py:32
  34.5 2.8 %collective-permute-start.10 = (f32[64,1024]{1,0:T(8,128)S(1)}, f32[64,1024]{1,0:T(8,128)S(1)}, u32[]{:S(2)}, u32[]{:S(2)}) collective-permute-start(f32[64,1024]{1,0:T(8,128)S(1)} %get-tuple-element.38), channel_id=1, source_target_pairs={{0,1},{1,0},{2,3},{3,2},{4,5},{5,4},{6,7},{7,6},{8,9},{9,8},{10,11... | collective-permute-start | bytes 786440 | tf_op jit(solution)/shard_map/ppermute | solution.py:342
  37.3 0.1 collective-permute-start.11
  37.4 1.0 %shard_map.70 = (f32[64,1024]{1,0:T(8,128)S(1)}, f32[64,1024]{1,0:T(8,128)S(1)}, f32[128,1024]{1,0:T(8,128)S(1)}, f32[128,1024]{1,0:T(8,128)S(1)}) custom-call(bf16[192,1024]{1,0:T(8,128)(2,1)S(1)} %get-tuple-element.34.gated_ref, bf16[1024,4096]{1,0:T(8,128)(2,1)S(1)} %bitcast.134), custom_call_target="tpu_custom_call" | custom-call | flops 1000000 | bytes 10000 | tf_op jit(solution)/shard_map/pallas_call | solution.py:32
  38.4 0.1 collective-permute-done.10.own_core_ref
  38.4 0.4 collective-permute-done.11.helped_core_ref
  38.8 0.1 shard_map.71
  38.9 0.5 collective-permute-start.14
  39.3 2.4 %collective-permute-start.13 = (f32[64,1024]{1,0:T(8,128)S(1)}, f32[64,1024]{1,0:T(8,128)S(1)}, u32[]{:S(2)}, u32[]{:S(2)}) collective-permute-start(f32[64,1024]{1,0:T(8,128)S(1)} %get-tuple-element.43), channel_id=1, source_target_pairs={{0,2},{1,15},{2,0},{3,5},{4,6},{5,3},{6,4},{7,9},{8,10},{9,7},{10,... | collective-permute-start | bytes 786440 | tf_op jit(solution)/shard_map/ppermute | solution.py:357
  41.7 0.0 collective-permute-start.12
  41.7 5.2 %collective-permute-done.13.first_ref = f32[64,1024]{1,0:T(8,128)S(1)} collective-permute-done((f32[64,1024]{1,0:T(8,128)S(1)}, f32[64,1024]{1,0:T(8,128)S(1)}, u32[]{:S(2)}, u32[]{:S(2)}) %collective-permute-start.13) | collective-permute-done | bytes 262176 | tf_op jit(solution)/shard_map/ppermute | solution.py:357
  46.9 1.3 %collective-permute-done.12.second_ref = f32[64,1024]{1,0:T(8,128)S(1)} collective-permute-done((f32[64,1024]{1,0:T(8,128)S(1)}, f32[64,1024]{1,0:T(8,128)S(1)}, u32[]{:S(2)}, u32[]{:S(2)}) %collective-permute-start.12) | collective-permute-done | bytes 262176 | tf_op jit(solution)/shard_map/ppermute | solution.py:356
  48.2 0.0 collective-permute-done.14.core_ref
  48.2 0.8 %shard_map.72 = bf16[128,1024]{1,0:T(8,128)(2,1)} custom-call(f32[128,1024]{1,0:T(8,128)S(1)} %get-tuple-element.35.home_ref, f32[64,1024]{1,0:T(8,128)S(1)} %collective-permute-done.12.second_ref, f32[64,1024]{1,0:T(8,128)S(1)} %collective-permute-done.13.first_ref, f32[128,1024]{1,0:T(8,128)S(1)} %collective-permute-done.14.core_ref), custom_call_target="tpu_custom_call" | custom-call | flops 1000000 | bytes 2000000 | tf_op jit(solution)/shard_map/pallas_call | solution.py:32
  (9 shorter events, 0.1 us)
Async XLA Ops:
  0.0 11.2 %copy-start.1 = (f32[16,1024]{1,0:T(8,128)S(1)}, f32[16,1024]{1,0:T(8,128)}, u32[]{:S(2)}) copy-start(f32[16,1024]{1,0:T(8,128)} %param.10) | copy-start | bytes 196612
  0.0 11.2 %copy-start.2 = (f32[16,1024]{1,0:T(8,128)S(1)}, f32[16,1024]{1,0:T(8,128)}, u32[]{:S(2)}) copy-start(f32[16,1024]{1,0:T(8,128)} %param.9) | copy-start | bytes 196612
  0.0 11.2 %copy-start = (f32[128,1024]{1,0:T(8,128)S(1)}, f32[128,1024]{1,0:T(8,128)}, u32[]{:S(2)}) copy-start(f32[128,1024]{1,0:T(8,128)} %param.8) | copy-start | bytes 1572868
  2.2 11.9 %collective-permute-start.3 = (f32[2,64,128]{2,1,0:T(8,128)S(1)}, f32[2,64,128]{2,1,0:T(8,128)S(1)}, u32[]{:S(2)}, u32[]{:S(2)}) collective-permute-start(f32[2,64,128]{2,1,0:T(8,128)S(1)} %shard_map.66.refs_1_), channel_id=1, source_target_pairs={{0,8},{4,12},{8,0},{12,4},{16,24},{20,28},{24,16},{28,20},{32,40},... | collective-permute-start | bytes 196616 | tf_op jit(solution)/shard_map/ppermute | solution.py:259
  10.0 5.3 %collective-permute-start.2 = (f32[2,64,128]{2,1,0:T(8,128)S(1)}, f32[2,64,128]{2,1,0:T(8,128)S(1)}, u32[]{:S(2)}, u32[]{:S(2)}) collective-permute-start(f32[2,64,128]{2,1,0:T(8,128)S(1)} %shard_map.66.refs_1_), channel_id=1, source_target_pairs={{0,12},{4,8},{8,4},{12,0},{16,28},{20,24},{24,20},{28,16},{32,44},... | collective-permute-start | bytes 196616 | tf_op jit(solution)/shard_map/ppermute | solution.py:259
  10.0 7.5 %collective-permute-start.1 = (f32[2,64,128]{2,1,0:T(8,128)S(1)}, f32[2,64,128]{2,1,0:T(8,128)S(1)}, u32[]{:S(2)}, u32[]{:S(2)}) collective-permute-start(f32[2,64,128]{2,1,0:T(8,128)S(1)} %shard_map.66.refs_1_), channel_id=1, source_target_pairs={{0,4},{4,0},{8,12},{12,8},{16,20},{20,16},{24,28},{28,24},{32,36},... | collective-permute-start | bytes 196616 | tf_op jit(solution)/shard_map/ppermute | solution.py:259
  11.3 21.7 %slice-start = ((s8[8388608]{0:T(1024)(128)(4,1)}), s8[4194304]{0:T(1024)(128)(4,1)S(1)}, s32[]{:S(2)}) async-start(s8[8388608]{0:T(1024)(128)(4,1)} %bitcast.133), calls=%async_computation | async-start | bytes 8388608
  12.5 20.5 %slice-start.1 = ((s8[8388608]{0:T(1024)(128)(4,1)}), s8[4194304]{0:T(1024)(128)(4,1)S(1)}, s32[]{:S(2)}) async-start(s8[8388608]{0:T(1024)(128)(4,1)} %bitcast.133), calls=%async_computation.1 | async-start | bytes 8388608
  12.5 20.4 %collective-permute-start = (f32[2,8,64,128]{3,2,1,0:T(8,128)S(1)}, f32[2,8,64,128]{3,2,1,0:T(8,128)S(1)}, u32[]{:S(2)}, u32[]{:S(2)}) collective-permute-start(f32[2,8,64,128]{3,2,1,0:T(8,128)S(1)} %get-tuple-element.26), channel_id=1, source_target_pairs={{0,4},{1,5},{2,14},{3,15},{4,8},{5,9},{6,2},{7,3},{8,12},{9,13},{1... | collective-permute-start | bytes 1572872 | tf_op jit(solution)/shard_map/ppermute | solution.py:303
  17.5 5.0 %collective-permute-start.6 = (f32[2,64,128]{2,1,0:T(8,128)S(1)}, f32[2,64,128]{2,1,0:T(8,128)S(1)}, u32[]{:S(2)}, u32[]{:S(2)}) collective-permute-start(f32[2,64,128]{2,1,0:T(8,128)S(1)} %fusion.18), channel_id=1, source_target_pairs={{0,32},{4,36},{8,40},{12,44},{16,48},{20,52},{24,56},{28,60},{32,0... | collective-permute-start | bytes 196616 | tf_op jit(solution)/shard_map/ppermute | solution.py:259
  20.6 4.7 %collective-permute-start.5 = (f32[2,64,128]{2,1,0:T(8,128)S(1)}, f32[2,64,128]{2,1,0:T(8,128)S(1)}, u32[]{:S(2)}, u32[]{:S(2)}) collective-permute-start(f32[2,64,128]{2,1,0:T(8,128)S(1)} %fusion.18), channel_id=1, source_target_pairs={{0,48},{4,52},{8,56},{12,60},{16,32},{20,36},{24,40},{28,44},{32,1... | collective-permute-start | bytes 196616 | tf_op jit(solution)/shard_map/ppermute | solution.py:259
  21.4 3.8 %collective-permute-start.4 = (f32[2,64,128]{2,1,0:T(8,128)S(1)}, f32[2,64,128]{2,1,0:T(8,128)S(1)}, u32[]{:S(2)}, u32[]{:S(2)}) collective-permute-start(f32[2,64,128]{2,1,0:T(8,128)S(1)} %fusion.18), channel_id=1, source_target_pairs={{0,16},{4,20},{8,24},{12,28},{16,0},{20,4},{24,8},{28,12},{32,48},... | collective-permute-start | bytes 196616 | tf_op jit(solution)/shard_map/ppermute | solution.py:259
  25.4 4.7 %collective-permute-start.9 = (f32[2,64,128]{2,1,0:T(8,128)S(1)}, f32[2,64,128]{2,1,0:T(8,128)S(1)}, u32[]{:S(2)}, u32[]{:S(2)}) collective-permute-start(f32[2,64,128]{2,1,0:T(8,128)S(1)} %get-tuple-element.47), channel_id=1, source_target_pairs={{0,128},{4,132},{8,136},{12,140},{16,144},{20,148},{24,152},{28,15... | collective-permute-start | bytes 196616 | tf_op jit(solution)/shard_map/ppermute | solution.py:259
  28.2 4.7 %collective-permute-start.8 = (f32[2,64,128]{2,1,0:T(8,128)S(1)}, f32[2,64,128]{2,1,0:T(8,128)S(1)}, u32[]{:S(2)}, u32[]{:S(2)}) collective-permute-start(f32[2,64,128]{2,1,0:T(8,128)S(1)} %get-tuple-element.47), channel_id=1, source_target_pairs={{0,192},{4,196},{8,200},{12,204},{16,208},{20,212},{24,216},{28,22... | collective-permute-start | bytes 196616 | tf_op jit(solution)/shard_map/ppermute | solution.py:259
  29.1 3.9 %collective-permute-start.7 = (f32[2,64,128]{2,1,0:T(8,128)S(1)}, f32[2,64,128]{2,1,0:T(8,128)S(1)}, u32[]{:S(2)}, u32[]{:S(2)}) collective-permute-start(f32[2,64,128]{2,1,0:T(8,128)S(1)} %get-tuple-element.47), channel_id=1, source_target_pairs={{0,64},{4,68},{8,72},{12,76},{16,80},{20,84},{24,88},{28,92},{32,9... | collective-permute-start | bytes 196616 | tf_op jit(solution)/shard_map/ppermute | solution.py:259
  34.5 4.0 %collective-permute-start.10 = (f32[64,1024]{1,0:T(8,128)S(1)}, f32[64,1024]{1,0:T(8,128)S(1)}, u32[]{:S(2)}, u32[]{:S(2)}) collective-permute-start(f32[64,1024]{1,0:T(8,128)S(1)} %get-tuple-element.38), channel_id=1, source_target_pairs={{0,1},{1,0},{2,3},{3,2},{4,5},{5,4},{6,7},{7,6},{8,9},{9,8},{10,11... | collective-permute-start | bytes 786440 | tf_op jit(solution)/shard_map/ppermute | solution.py:342
  37.3 1.5 %collective-permute-start.11 = (f32[64,1024]{1,0:T(8,128)S(1)}, f32[64,1024]{1,0:T(8,128)S(1)}, u32[]{:S(2)}, u32[]{:S(2)}) collective-permute-start(f32[64,1024]{1,0:T(8,128)S(1)} %get-tuple-element.39), channel_id=1, source_target_pairs={{0,1},{1,0},{2,3},{3,2},{4,5},{5,4},{6,7},{7,6},{8,9},{9,8},{10,11... | collective-permute-start | bytes 786440 | tf_op jit(solution)/shard_map/ppermute | solution.py:342
  38.9 9.4 %collective-permute-start.14 = (f32[128,1024]{1,0:T(8,128)S(1)}, f32[128,1024]{1,0:T(8,128)S(1)}, u32[]{:S(2)}, u32[]{:S(2)}) collective-permute-start(f32[128,1024]{1,0:T(8,128)S(1)} %get-tuple-element.44), channel_id=1, source_target_pairs={{0,1},{1,0},{2,3},{3,2},{4,5},{5,4},{6,7},{7,6},{8,9},{9,8},{10,11... | collective-permute-start | bytes 1572872 | tf_op jit(solution)/shard_map/ppermute | solution.py:342
  39.3 7.6 %collective-permute-start.13 = (f32[64,1024]{1,0:T(8,128)S(1)}, f32[64,1024]{1,0:T(8,128)S(1)}, u32[]{:S(2)}, u32[]{:S(2)}) collective-permute-start(f32[64,1024]{1,0:T(8,128)S(1)} %get-tuple-element.43), channel_id=1, source_target_pairs={{0,2},{1,15},{2,0},{3,5},{4,6},{5,3},{6,4},{7,9},{8,10},{9,7},{10,... | collective-permute-start | bytes 786440 | tf_op jit(solution)/shard_map/ppermute | solution.py:357
  41.7 6.5 %collective-permute-start.12 = (f32[64,1024]{1,0:T(8,128)S(1)}, f32[64,1024]{1,0:T(8,128)S(1)}, u32[]{:S(2)}, u32[]{:S(2)}) collective-permute-start(f32[64,1024]{1,0:T(8,128)S(1)} %get-tuple-element.40), channel_id=1, source_target_pairs={{0,14},{1,3},{2,4},{3,1},{4,2},{5,7},{6,8},{7,5},{8,6},{9,11},{10,... | collective-permute-start | bytes 786440 | tf_op jit(solution)/shard_map/ppermute | solution.py:356

commit v5 on v4

--- a/solution.py
+++ b/solution.py
@@ -213,7 +213,7 @@
 
 
 def in_turn(one, other):
-    ahead = lax.rem(lax.axis_index("ch"), 2) == 0
+    ahead = lax.rem(lax.axis_index("ch"), 2) == 1
     return jnp.where(ahead, one, other), jnp.where(ahead, other, one)
 
 
@@ -348,11 +348,10 @@
         1_000_000,
         10_000,
     )
-    first, home_sent = lax.optimization_barrier((first, home_sent))
     pair = along_z(count, lambda z, low: (z, 1 - low))
     other = along_z(count, lambda z, low: (z - 1 + 2 * low, 1 - low))
-    mixed = [(pair, other)[i % 2][i] for i in range(len(pair))]
-    turned = [(other, pair)[i % 2][i] for i in range(len(pair))]
+    mixed = [(other, pair)[i % 2][i] for i in range(len(pair))]
+    turned = [(pair, other)[i % 2][i] for i in range(len(pair))]
     second = lax.ppermute(second, ("seq", "ch"), turned)
     first = lax.ppermute(first, ("seq", "ch"), mixed)
     return kernel_call(

time: 49.1 us -> 49 us (level)
    ppermute x1, waiting for transfers between devices: 1.34 us -> 5.03 us  [local(): second = lax.ppermute(second, ('seq', 'ch'), turned)]
    ppermute x1, waiting for transfers between devices: 5.19 us -> 1.68 us  [local(): first = lax.ppermute(first, ('seq', 'ch'), mixed)]
    ppermute x1, starting transfers between devices: 0.01 us -> 2.47 us  [local(): second = lax.ppermute(second, ('seq', 'ch'), turned)]
    ppermute x1, starting transfers between devices: 2.39 us -> 0.01 us  [local(): first = lax.ppermute(first, ('seq', 'ch'), mixed)]
  transfers between devices with their start and end apart: 15 -> 15, of which waited for: 10 -> 8; matrix products, arithmetic and copies ran while one was open for 0% -> 0% of each run, Pallas kernels for 5% -> 5%
where the time goes in v5:
time: 49 us; the launch traced here: 48.9 us
  starting transfers between devices  23.7 us (48%)
  waiting for transfers between devices  17.8 us (36%)
  Pallas kernels  5.68 us (12%)
  other arithmetic  1.59 us (3%)
    ppermute x9, starting transfers between devices, swap(): return [lax.ppermute(state, 'seq', pair) for pair in pairs]  16.6 us
    ppermute x9, waiting for transfers between devices, swap(): return [lax.ppermute(state, 'seq', pair) for pair in pairs]  11 us
    pallas_call x9, Pallas kernels, kernel_call(): pl.pallas_call(body, out_shape=out_shape, in_specs=[pl.BlockSpec(memory_s...  5.68 us
    ppermute x1, waiting for transfers between devices, local(): second = lax.ppermute(second, ('seq', 'ch'), turned)  5.03 us
    ppermute x3, starting transfers between devices, core_swap(): return lax.ppermute(one, 'ch', partner_pairs(4, 1))  3.41 us
    ppermute x1, starting transfers between devices, local(): second = lax.ppermute(second, ('seq', 'ch'), turned)  2.47 us
    ppermute x1, waiting for transfers between devices, local(): first = lax.ppermute(first, ('seq', 'ch'), mixed)  1.68 us
    reshape x2, other arithmetic, tiles(): cut.transpose(0, 2, 1, 3).reshape(rows // 8, 8 * (columns // LANES), LANES)  1.41 us
  transfers between devices with their start and end apart: 15, of which 8 were waited for; matrix products, arithmetic and copies ran while one was open for 0% of the time, Pallas kernels for 5%

profile of v5, /device:TPU:1, one launch (start us, length us, event | category | flops | bytes accessed | tf_op | source)
XLA Modules:
  0.0 48.9 jit_solution(15446985464318685707)
XLA Ops:
  0.0 1.4 %add_bitcast_fusion.stacked_ref.refs_0_ = f32[18,64,128]{2,1,0:T(8,128)S(1)} fusion(f32[16,1024]{1,0:T(8,128)} %param.10, f32[128,1024]{1,0:T(8,128)} %param.6, f32[128,1024]{1,0:T(8,128)} %param.7), kind=kLoop, calls=%fused_computation | loop fusion | flops 294912 | bytes 1703936 | tf_op jit(solution)/shard_map/reshape | solution.py:19
  1.4 0.8 %shard_map.66.refs_1_ = f32[2,64,128]{2,1,0:T(8,128)S(1)} custom-call(f32[18,64,128]{2,1,0:T(8,128)S(1)} %add_bitcast_fusion.stacked_ref.refs_0_), custom_call_target="tpu_custom_call" | custom-call | flops 2000000000 | bytes 600000 | tf_op jit(solution)/shard_map/pallas_call | solution.py:32
  2.2 7.8 %collective-permute-start.3 = (f32[2,64,128]{2,1,0:T(8,128)S(1)}, f32[2,64,128]{2,1,0:T(8,128)S(1)}, u32[]{:S(2)}, u32[]{:S(2)}) collective-permute-start(f32[2,64,128]{2,1,0:T(8,128)S(1)} %shard_map.66.refs_1_), channel_id=1, source_target_pairs={{0,8},{4,12},{8,0},{12,4},{16,24},{20,28},{24,16},{28,20},{32,40},... | collective-permute-start | bytes 196616 | tf_op jit(solution)/shard_map/ppermute | solution.py:259
  10.0 0.0 collective-permute-start.2
  10.0 1.2 %collective-permute-start.1 = (f32[2,64,128]{2,1,0:T(8,128)S(1)}, f32[2,64,128]{2,1,0:T(8,128)S(1)}, u32[]{:S(2)}, u32[]{:S(2)}) collective-permute-start(f32[2,64,128]{2,1,0:T(8,128)S(1)} %shard_map.66.refs_1_), channel_id=1, source_target_pairs={{0,4},{4,0},{8,12},{12,8},{16,20},{20,16},{24,28},{28,24},{32,36},... | collective-permute-start | bytes 196616 | tf_op jit(solution)/shard_map/ppermute | solution.py:259
  11.2 0.0 copy-done.1
  11.2 0.0 copy-done.2
  11.3 0.0 copy-done
  11.3 0.0 slice-start
  11.3 1.2 %shard_map.64 = (f32[16,64,128]{2,1,0:T(8,128)S(1)}, f32[2,8,64,128]{3,2,1,0:T(8,128)S(1)}) custom-call(f32[18,64,128]{2,1,0:T(8,128)S(1)} %add_bitcast_fusion.stacked_ref.refs_0_, f32[2,64,128]{2,1,0:T(8,128)S(1)} %multiply_bitcast_fusion.gain_ref.refs_1_, f32[16,64,128]{2,1,0:T(8,128)S(1)} %bitcast.135), custom_call_target="tpu_custom_call" | custom-call | flops 3000000000 | bytes 1500000 | tf_op jit(solution)/shard_map/pallas_call | solution.py:32
  12.5 0.0 slice-start.1
  12.5 1.2 %collective-permute-start = (f32[2,8,64,128]{3,2,1,0:T(8,128)S(1)}, f32[2,8,64,128]{3,2,1,0:T(8,128)S(1)}, u32[]{:S(2)}, u32[]{:S(2)}) collective-permute-start(f32[2,8,64,128]{3,2,1,0:T(8,128)S(1)} %get-tuple-element.24), channel_id=1, source_target_pairs={{0,4},{1,5},{2,14},{3,15},{4,8},{5,9},{6,2},{7,3},{8,12},{9,13},{1... | collective-permute-start | bytes 1572872 | tf_op jit(solution)/shard_map/ppermute | solution.py:303
  13.8 0.1 shard_map.67
  13.9 0.2 shard_map.65
  14.1 0.0 collective-permute-done.3
  14.1 1.2 %collective-permute-done.2 = f32[2,64,128]{2,1,0:T(8,128)S(1)} collective-permute-done((f32[2,64,128]{2,1,0:T(8,128)S(1)}, f32[2,64,128]{2,1,0:T(8,128)S(1)}, u32[]{:S(2)}, u32[]{:S(2)}) %collective-permute-start.2) | collective-permute-done | bytes 65568 | tf_op jit(solution)/shard_map/ppermute | solution.py:259
  15.3 2.1 %collective-permute-done.1 = f32[2,64,128]{2,1,0:T(8,128)S(1)} collective-permute-done((f32[2,64,128]{2,1,0:T(8,128)S(1)}, f32[2,64,128]{2,1,0:T(8,128)S(1)}, u32[]{:S(2)}, u32[]{:S(2)}) %collective-permute-start.1) | collective-permute-done | bytes 65568 | tf_op jit(solution)/shard_map/ppermute | solution.py:259
  17.5 3.0 %collective-permute-start.6 = (f32[2,64,128]{2,1,0:T(8,128)S(1)}, f32[2,64,128]{2,1,0:T(8,128)S(1)}, u32[]{:S(2)}, u32[]{:S(2)}) collective-permute-start(f32[2,64,128]{2,1,0:T(8,128)S(1)} %fusion.18), channel_id=1, source_target_pairs={{0,32},{4,36},{8,40},{12,44},{16,48},{20,52},{24,56},{28,60},{32,0... | collective-permute-start | bytes 196616 | tf_op jit(solution)/shard_map/ppermute | solution.py:259
  20.5 0.1 shard_map.68
  20.6 0.9 %collective-permute-start.5 = (f32[2,64,128]{2,1,0:T(8,128)S(1)}, f32[2,64,128]{2,1,0:T(8,128)S(1)}, u32[]{:S(2)}, u32[]{:S(2)}) collective-permute-start(f32[2,64,128]{2,1,0:T(8,128)S(1)} %fusion.18), channel_id=1, source_target_pairs={{0,48},{4,52},{8,56},{12,60},{16,32},{20,36},{24,40},{28,44},{32,1... | collective-permute-start | bytes 196616 | tf_op jit(solution)/shard_map/ppermute | solution.py:259
  21.4 0.0 collective-permute-start.4
  21.4 1.1 %collective-permute-done.6 = f32[2,64,128]{2,1,0:T(8,128)S(1)} collective-permute-done((f32[2,64,128]{2,1,0:T(8,128)S(1)}, f32[2,64,128]{2,1,0:T(8,128)S(1)}, u32[]{:S(2)}, u32[]{:S(2)}) %collective-permute-start.6) | collective-permute-done | bytes 65568 | tf_op jit(solution)/shard_map/ppermute | solution.py:259
  22.5 2.8 %collective-permute-done.5 = f32[2,64,128]{2,1,0:T(8,128)S(1)} collective-permute-done((f32[2,64,128]{2,1,0:T(8,128)S(1)}, f32[2,64,128]{2,1,0:T(8,128)S(1)}, u32[]{:S(2)}, u32[]{:S(2)}) %collective-permute-start.5) | collective-permute-done | bytes 65568 | tf_op jit(solution)/shard_map/ppermute | solution.py:259
  25.3 0.0 collective-permute-done.4
  25.3 0.1 fusion.12
  25.4 2.8 %collective-permute-start.9 = (f32[2,64,128]{2,1,0:T(8,128)S(1)}, f32[2,64,128]{2,1,0:T(8,128)S(1)}, u32[]{:S(2)}, u32[]{:S(2)}) collective-permute-start(f32[2,64,128]{2,1,0:T(8,128)S(1)} %get-tuple-element.43), channel_id=1, source_target_pairs={{0,128},{4,132},{8,136},{12,140},{16,144},{20,148},{24,152},{28,15... | collective-permute-start | bytes 196616 | tf_op jit(solution)/shard_map/ppermute | solution.py:259
  28.2 0.9 %collective-permute-start.8 = (f32[2,64,128]{2,1,0:T(8,128)S(1)}, f32[2,64,128]{2,1,0:T(8,128)S(1)}, u32[]{:S(2)}, u32[]{:S(2)}) collective-permute-start(f32[2,64,128]{2,1,0:T(8,128)S(1)} %get-tuple-element.43), channel_id=1, source_target_pairs={{0,192},{4,196},{8,200},{12,204},{16,208},{20,212},{24,216},{28,22... | collective-permute-start | bytes 196616 | tf_op jit(solution)/shard_map/ppermute | solution.py:259
  29.1 0.0 collective-permute-start.7
  29.1 1.0 %collective-permute-done.9.refs_11_ = f32[2,64,128]{2,1,0:T(8,128)S(1)} collective-permute-done((f32[2,64,128]{2,1,0:T(8,128)S(1)}, f32[2,64,128]{2,1,0:T(8,128)S(1)}, u32[]{:S(2)}, u32[]{:S(2)}) %collective-permute-start.9) | collective-permute-done | bytes 65568 | tf_op jit(solution)/shard_map/ppermute | solution.py:259
  30.1 2.9 %collective-permute-done.8.refs_10_ = f32[2,64,128]{2,1,0:T(8,128)S(1)} collective-permute-done((f32[2,64,128]{2,1,0:T(8,128)S(1)}, f32[2,64,128]{2,1,0:T(8,128)S(1)}, u32[]{:S(2)}, u32[]{:S(2)}) %collective-permute-start.8) | collective-permute-done | bytes 65568 | tf_op jit(solution)/shard_map/ppermute | solution.py:259
  33.0 0.0 collective-permute-done.7.refs_9_
  33.0 0.0 collective-permute-done.refs_2_
  33.0 0.0 slice-done
  33.0 0.0 slice-done.1
  33.0 1.5 %shard_map.69 = (bf16[192,1024]{1,0:T(8,128)(2,1)S(1)}, f32[64,1024]{1,0:T(8,128)S(1)}, f32[64,1024]{1,0:T(8,128)S(1)}) custom-call(f32[16,64,128]{2,1,0:T(8,128)S(1)} %bitcast.136, f32[16,64,128]{2,1,0:T(8,128)S(1)} %get-tuple-element.23.refs_1_, f32[2,8,64,128]{3,2,1,0:T(8,128)S(1)} %collective-permute-done.refs_2_, ...), custom_call_target="tpu_custom_call" | custom-call | flops 2000000000 | bytes 3000000 | tf_op jit(solution)/shard_map/pallas_call | solution.py:32
  34.5 2.8 %collective-permute-start.10 = (f32[64,1024]{1,0:T(8,128)S(1)}, f32[64,1024]{1,0:T(8,128)S(1)}, u32[]{:S(2)}, u32[]{:S(2)}) collective-permute-start(f32[64,1024]{1,0:T(8,128)S(1)} %get-tuple-element.36), channel_id=1, source_target_pairs={{0,1},{1,0},{2,3},{3,2},{4,5},{5,4},{6,7},{7,6},{8,9},{9,8},{10,11... | collective-permute-start | bytes 786440 | tf_op jit(solution)/shard_map/ppermute | solution.py:342
  37.3 0.1 collective-permute-start.11
  37.4 1.0 %shard_map.70 = (f32[64,1024]{1,0:T(8,128)S(1)}, f32[64,1024]{1,0:T(8,128)S(1)}, f32[128,1024]{1,0:T(8,128)S(1)}, f32[128,1024]{1,0:T(8,128)S(1)}) custom-call(bf16[192,1024]{1,0:T(8,128)(2,1)S(1)} %get-tuple-element.32.gated_ref, bf16[1024,4096]{1,0:T(8,128)(2,1)S(1)} %bitcast.134), custom_call_target="tpu_custom_call" | custom-call | flops 1000000 | bytes 10000 | tf_op jit(solution)/shard_map/pallas_call | solution.py:32
  38.4 0.5 %collective-permute-start.14 = (f32[128,1024]{1,0:T(8,128)S(1)}, f32[128,1024]{1,0:T(8,128)S(1)}, u32[]{:S(2)}, u32[]{:S(2)}) collective-permute-start(f32[128,1024]{1,0:T(8,128)S(1)} %get-tuple-element.40), channel_id=1, source_target_pairs={{0,1},{1,0},{2,3},{3,2},{4,5},{5,4},{6,7},{7,6},{8,9},{9,8},{10,11... | collective-permute-start | bytes 1572872 | tf_op jit(solution)/shard_map/ppermute | solution.py:342
  38.9 0.0 collective-permute-done.10.own_core_ref
  38.9 0.0 collective-permute-done.11.helped_core_ref
  38.9 0.1 shard_map.71
  38.9 2.5 %collective-permute-start.12 = (f32[64,1024]{1,0:T(8,128)S(1)}, f32[64,1024]{1,0:T(8,128)S(1)}, u32[]{:S(2)}, u32[]{:S(2)}) collective-permute-start(f32[64,1024]{1,0:T(8,128)S(1)} %get-tuple-element.38), channel_id=1, source_target_pairs={{0,2},{1,15},{2,0},{3,5},{4,6},{5,3},{6,4},{7,9},{8,10},{9,7},{10,... | collective-permute-start | bytes 786440 | tf_op jit(solution)/shard_map/ppermute | solution.py:355
  41.4 0.0 collective-permute-start.13
  41.4 5.0 %collective-permute-done.12.second_ref = f32[64,1024]{1,0:T(8,128)S(1)} collective-permute-done((f32[64,1024]{1,0:T(8,128)S(1)}, f32[64,1024]{1,0:T(8,128)S(1)}, u32[]{:S(2)}, u32[]{:S(2)}) %collective-permute-start.12) | collective-permute-done | bytes 262176 | tf_op jit(solution)/shard_map/ppermute | solution.py:355
  46.4 1.7 %collective-permute-done.13.first_ref = f32[64,1024]{1,0:T(8,128)S(1)} collective-permute-done((f32[64,1024]{1,0:T(8,128)S(1)}, f32[64,1024]{1,0:T(8,128)S(1)}, u32[]{:S(2)}, u32[]{:S(2)}) %collective-permute-start.13) | collective-permute-done | bytes 262176 | tf_op jit(solution)/shard_map/ppermute | solution.py:356
  48.1 0.0 collective-permute-done.14.core_ref
  48.1 0.8 %shard_map.72 = bf16[128,1024]{1,0:T(8,128)(2,1)} custom-call(f32[128,1024]{1,0:T(8,128)S(1)} %get-tuple-element.33.home_ref, f32[64,1024]{1,0:T(8,128)S(1)} %collective-permute-done.12.second_ref, f32[64,1024]{1,0:T(8,128)S(1)} %collective-permute-done.13.first_ref, f32[128,1024]{1,0:T(8,128)S(1)} %collective-permute-done.14.core_ref), custom_call_target="tpu_custom_call" | custom-call | flops 1000000 | bytes 2000000 | tf_op jit(solution)/shard_map/pallas_call | solution.py:32
  (9 shorter events, 0.1 us)
Async XLA Ops:
  0.0 11.2 %copy-start.1 = (f32[16,1024]{1,0:T(8,128)S(1)}, f32[16,1024]{1,0:T(8,128)}, u32[]{:S(2)}) copy-start(f32[16,1024]{1,0:T(8,128)} %param.10) | copy-start | bytes 196612
  0.0 11.2 %copy-start.2 = (f32[16,1024]{1,0:T(8,128)S(1)}, f32[16,1024]{1,0:T(8,128)}, u32[]{:S(2)}) copy-start(f32[16,1024]{1,0:T(8,128)} %param.9) | copy-start | bytes 196612
  0.0 11.2 %copy-start = (f32[128,1024]{1,0:T(8,128)S(1)}, f32[128,1024]{1,0:T(8,128)}, u32[]{:S(2)}) copy-start(f32[128,1024]{1,0:T(8,128)} %param.8) | copy-start | bytes 1572868
  2.2 11.9 %collective-permute-start.3 = (f32[2,64,128]{2,1,0:T(8,128)S(1)}, f32[2,64,128]{2,1,0:T(8,128)S(1)}, u32[]{:S(2)}, u32[]{:S(2)}) collective-permute-start(f32[2,64,128]{2,1,0:T(8,128)S(1)} %shard_map.66.refs_1_), channel_id=1, source_target_pairs={{0,8},{4,12},{8,0},{12,4},{16,24},{20,28},{24,16},{28,20},{32,40},... | collective-permute-start | bytes 196616 | tf_op jit(solution)/shard_map/ppermute | solution.py:259
  10.0 5.3 %collective-permute-start.2 = (f32[2,64,128]{2,1,0:T(8,128)S(1)}, f32[2,64,128]{2,1,0:T(8,128)S(1)}, u32[]{:S(2)}, u32[]{:S(2)}) collective-permute-start(f32[2,64,128]{2,1,0:T(8,128)S(1)} %shard_map.66.refs_1_), channel_id=1, source_target_pairs={{0,12},{4,8},{8,4},{12,0},{16,28},{20,24},{24,20},{28,16},{32,44},... | collective-permute-start | bytes 196616 | tf_op jit(solution)/shard_map/ppermute | solution.py:259
  10.0 7.5 %collective-permute-start.1 = (f32[2,64,128]{2,1,0:T(8,128)S(1)}, f32[2,64,128]{2,1,0:T(8,128)S(1)}, u32[]{:S(2)}, u32[]{:S(2)}) collective-permute-start(f32[2,64,128]{2,1,0:T(8,128)S(1)} %shard_map.66.refs_1_), channel_id=1, source_target_pairs={{0,4},{4,0},{8,12},{12,8},{16,20},{20,16},{24,28},{28,24},{32,36},... | collective-permute-start | bytes 196616 | tf_op jit(solution)/shard_map/ppermute | solution.py:259
  11.3 21.7 %slice-start = ((s8[8388608]{0:T(1024)(128)(4,1)}), s8[4194304]{0:T(1024)(128)(4,1)S(1)}, s32[]{:S(2)}) async-start(s8[8388608]{0:T(1024)(128)(4,1)} %bitcast.133), calls=%async_computation | async-start | bytes 8388608
  12.5 20.5 %slice-start.1 = ((s8[8388608]{0:T(1024)(128)(4,1)}), s8[4194304]{0:T(1024)(128)(4,1)S(1)}, s32[]{:S(2)}) async-start(s8[8388608]{0:T(1024)(128)(4,1)} %bitcast.133), calls=%async_computation.1 | async-start | bytes 8388608
  12.5 20.4 %collective-permute-start = (f32[2,8,64,128]{3,2,1,0:T(8,128)S(1)}, f32[2,8,64,128]{3,2,1,0:T(8,128)S(1)}, u32[]{:S(2)}, u32[]{:S(2)}) collective-permute-start(f32[2,8,64,128]{3,2,1,0:T(8,128)S(1)} %get-tuple-element.24), channel_id=1, source_target_pairs={{0,4},{1,5},{2,14},{3,15},{4,8},{5,9},{6,2},{7,3},{8,12},{9,13},{1... | collective-permute-start | bytes 1572872 | tf_op jit(solution)/shard_map/ppermute | solution.py:303
  17.5 5.0 %collective-permute-start.6 = (f32[2,64,128]{2,1,0:T(8,128)S(1)}, f32[2,64,128]{2,1,0:T(8,128)S(1)}, u32[]{:S(2)}, u32[]{:S(2)}) collective-permute-start(f32[2,64,128]{2,1,0:T(8,128)S(1)} %fusion.18), channel_id=1, source_target_pairs={{0,32},{4,36},{8,40},{12,44},{16,48},{20,52},{24,56},{28,60},{32,0... | collective-permute-start | bytes 196616 | tf_op jit(solution)/shard_map/ppermute | solution.py:259
  20.6 4.7 %collective-permute-start.5 = (f32[2,64,128]{2,1,0:T(8,128)S(1)}, f32[2,64,128]{2,1,0:T(8,128)S(1)}, u32[]{:S(2)}, u32[]{:S(2)}) collective-permute-start(f32[2,64,128]{2,1,0:T(8,128)S(1)} %fusion.18), channel_id=1, source_target_pairs={{0,48},{4,52},{8,56},{12,60},{16,32},{20,36},{24,40},{28,44},{32,1... | collective-permute-start | bytes 196616 | tf_op jit(solution)/shard_map/ppermute | solution.py:259
  21.4 3.8 %collective-permute-start.4 = (f32[2,64,128]{2,1,0:T(8,128)S(1)}, f32[2,64,128]{2,1,0:T(8,128)S(1)}, u32[]{:S(2)}, u32[]{:S(2)}) collective-permute-start(f32[2,64,128]{2,1,0:T(8,128)S(1)} %fusion.18), channel_id=1, source_target_pairs={{0,16},{4,20},{8,24},{12,28},{16,0},{20,4},{24,8},{28,12},{32,48},... | collective-permute-start | bytes 196616 | tf_op jit(solution)/shard_map/ppermute | solution.py:259
  25.4 4.7 %collective-permute-start.9 = (f32[2,64,128]{2,1,0:T(8,128)S(1)}, f32[2,64,128]{2,1,0:T(8,128)S(1)}, u32[]{:S(2)}, u32[]{:S(2)}) collective-permute-start(f32[2,64,128]{2,1,0:T(8,128)S(1)} %get-tuple-element.43), channel_id=1, source_target_pairs={{0,128},{4,132},{8,136},{12,140},{16,144},{20,148},{24,152},{28,15... | collective-permute-start | bytes 196616 | tf_op jit(solution)/shard_map/ppermute | solution.py:259
  28.2 4.7 %collective-permute-start.8 = (f32[2,64,128]{2,1,0:T(8,128)S(1)}, f32[2,64,128]{2,1,0:T(8,128)S(1)}, u32[]{:S(2)}, u32[]{:S(2)}) collective-permute-start(f32[2,64,128]{2,1,0:T(8,128)S(1)} %get-tuple-element.43), channel_id=1, source_target_pairs={{0,192},{4,196},{8,200},{12,204},{16,208},{20,212},{24,216},{28,22... | collective-permute-start | bytes 196616 | tf_op jit(solution)/shard_map/ppermute | solution.py:259
  29.1 3.9 %collective-permute-start.7 = (f32[2,64,128]{2,1,0:T(8,128)S(1)}, f32[2,64,128]{2,1,0:T(8,128)S(1)}, u32[]{:S(2)}, u32[]{:S(2)}) collective-permute-start(f32[2,64,128]{2,1,0:T(8,128)S(1)} %get-tuple-element.43), channel_id=1, source_target_pairs={{0,64},{4,68},{8,72},{12,76},{16,80},{20,84},{24,88},{28,92},{32,9... | collective-permute-start | bytes 196616 | tf_op jit(solution)/shard_map/ppermute | solution.py:259
  34.5 4.4 %collective-permute-start.10 = (f32[64,1024]{1,0:T(8,128)S(1)}, f32[64,1024]{1,0:T(8,128)S(1)}, u32[]{:S(2)}, u32[]{:S(2)}) collective-permute-start(f32[64,1024]{1,0:T(8,128)S(1)} %get-tuple-element.36), channel_id=1, source_target_pairs={{0,1},{1,0},{2,3},{3,2},{4,5},{5,4},{6,7},{7,6},{8,9},{9,8},{10,11... | collective-permute-start | bytes 786440 | tf_op jit(solution)/shard_map/ppermute | solution.py:342
  37.3 1.6 %collective-permute-start.11 = (f32[64,1024]{1,0:T(8,128)S(1)}, f32[64,1024]{1,0:T(8,128)S(1)}, u32[]{:S(2)}, u32[]{:S(2)}) collective-permute-start(f32[64,1024]{1,0:T(8,128)S(1)} %get-tuple-element.37), channel_id=1, source_target_pairs={{0,1},{1,0},{2,3},{3,2},{4,5},{5,4},{6,7},{7,6},{8,9},{9,8},{10,11... | collective-permute-start | bytes 786440 | tf_op jit(solution)/shard_map/ppermute | solution.py:342
  38.4 9.8 %collective-permute-start.14 = (f32[128,1024]{1,0:T(8,128)S(1)}, f32[128,1024]{1,0:T(8,128)S(1)}, u32[]{:S(2)}, u32[]{:S(2)}) collective-permute-start(f32[128,1024]{1,0:T(8,128)S(1)} %get-tuple-element.40), channel_id=1, source_target_pairs={{0,1},{1,0},{2,3},{3,2},{4,5},{5,4},{6,7},{7,6},{8,9},{9,8},{10,11... | collective-permute-start | bytes 1572872 | tf_op jit(solution)/shard_map/ppermute | solution.py:342
  38.9 7.5 %collective-permute-start.12 = (f32[64,1024]{1,0:T(8,128)S(1)}, f32[64,1024]{1,0:T(8,128)S(1)}, u32[]{:S(2)}, u32[]{:S(2)}) collective-permute-start(f32[64,1024]{1,0:T(8,128)S(1)} %get-tuple-element.38), channel_id=1, source_target_pairs={{0,2},{1,15},{2,0},{3,5},{4,6},{5,3},{6,4},{7,9},{8,10},{9,7},{10,... | collective-permute-start | bytes 786440 | tf_op jit(solution)/shard_map/ppermute | solution.py:355
  41.4 6.7 %collective-permute-start.13 = (f32[64,1024]{1,0:T(8,128)S(1)}, f32[64,1024]{1,0:T(8,128)S(1)}, u32[]{:S(2)}, u32[]{:S(2)}) collective-permute-start(f32[64,1024]{1,0:T(8,128)S(1)} %get-tuple-element.39), channel_id=1, source_target_pairs={{0,14},{1,3},{2,4},{3,1},{4,2},{5,7},{6,8},{7,5},{8,6},{9,11},{10,... | collective-permute-start | bytes 786440 | tf_op jit(solution)/shard_map/ppermute | solution.py:356
